TPU v7x, 32 devices: a whole 2x2x4 slice. The times are simulated.
32 devices in a mesh: row: 8 (over z, y), col: 4 (over x, core).
Axes of the slice: x: 2, y: 2, z: 4, core: 2. Of those that a mesh axis runs over, the one named last changes fastest.
Arguments:
- start_vectors: float32 [64, 4096], P(None, ('row', 'col')), may hold values from -6 to 6
- cluster_order: int32 [32, 128], P(('row', 'col')), may hold values from 0 to 127, each once within a row
- weights: bfloat16 [4096, 4, 1024], P('row', 'col'), may hold values from 0 to 1, as said below
- block_mask: int32 [32, 4, 8], P('row', 'col'), may hold values 0 or 1
Outputs:
- embedding: float32 [64, 4096], P(None, ('row', 'col'))
Inputs may be any that keep to these rules, and one draw needn't show every extreme that they name: Each row of cluster_order holds every number of 0 to 127 once. `block_mask`: entries below the diagonal blocks are read only through their mirror. `weights`: every node except the last of its cluster block has a positive weight to the next node of its cluster block.
All inputs are finite; a program needn't handle non-finite values.
Results may differ from a plain program's by a relative error of at most 0.00087.
Values may be sent and summed in bfloat16 or wider, within the bound.
No kernel may reach another device: no remote copies, remote signals or barrier semaphores. Data moves between devices by JAX's collectives and lax.ppermute only.
A program may use at most 64 MiB of HBM per device.

v0:
```python
import math

import jax
import jax.numpy as jnp
from jax import lax
from jax.sharding import PartitionSpec as P

ITERS = 3


def orthonormalize(panel_in):
    partial_gram = lax.dot_general(
        panel_in,
        panel_in,
        (((1,), (1,)), ((), ())),
        precision=lax.Precision.HIGHEST,
        preferred_element_type=jnp.float32,
    )
    total_gram = lax.psum(partial_gram, ("row", "col"))
    factor = jnp.linalg.cholesky(total_gram)
    return jax.scipy.linalg.solve_triangular(factor, panel_in, lower=True)


def collect_direct(term):
    return lax.psum_scatter(term, "col", scatter_dimension=1, tiled=True)


def direct_part(matrix, vectors):
    return lax.dot_general(
        lax.all_gather(vectors, "row", axis=1, tiled=True),
        matrix,
        (((1,), (1,)), ((), ())),
        preferred_element_type=jnp.float32,
    )


def local(start_vectors, cluster_order, weights, block_mask):
    row_index = lax.axis_index("row")
    col_index = lax.axis_index("col")
    row_count = lax.axis_size("row")
    col_count = lax.axis_size("col")
    block_len = start_vectors.shape[1]
    stored = weights[:, 0, :]
    live_mask = block_mask[:, 0, :]
    local_rows = row_index * col_count * block_len + jnp.arange(
        col_count * block_len, dtype=jnp.int32
    )
    col_position = jnp.arange(row_count * block_len, dtype=jnp.int32)
    local_cols = (
        col_position // block_len * col_count + col_index
    ) * block_len + col_position % block_len
    row_spans = row_index * col_count + jnp.arange(col_count, dtype=jnp.int32)
    col_spans = jnp.arange(row_count, dtype=jnp.int32) * col_count + col_index
    same_block = row_spans[:, None] == col_spans[None, :]
    keep_upper = ((live_mask > 0) | same_block)[:, None, :, None] & (
        local_rows.reshape(col_count, block_len, 1, 1)
        < local_cols.reshape(1, 1, row_count, block_len)
    )
    zero_value = jnp.zeros((), jnp.bfloat16)
    upper_part = jnp.where(
        keep_upper, stored.reshape(col_count, block_len, row_count, block_len), zero_value
    )
    ones_cols = jnp.ones((row_count * block_len,), jnp.bfloat16)
    relayed, relayed_mask = (
        lax.all_to_all(
            lax.all_to_all(stored, "row", split_axis=1, concat_axis=1, tiled=True),
            "col",
            split_axis=0,
            concat_axis=0,
            tiled=True,
        ),
        lax.all_to_all(
            lax.all_to_all(live_mask, "row", split_axis=1, concat_axis=1, tiled=True),
            "col",
            split_axis=0,
            concat_axis=0,
            tiled=True,
        ),
    )
    mirror_keep = ((relayed_mask > 0) | same_block)[:, None, :, None] & (
        local_cols.reshape(row_count, block_len).T.reshape(1, block_len, row_count, 1)
        < local_rows.reshape(col_count, 1, 1, block_len)
    )
    mirrored = jnp.where(
        mirror_keep, relayed.reshape(col_count, block_len, row_count, block_len), zero_value
    )
    matrix = (upper_part + jnp.swapaxes(mirrored, 1, 3)).reshape(
        col_count * block_len, row_count * block_len
    )
    degree = collect_direct(jnp.dot(matrix, ones_cols, preferred_element_type=jnp.float32)[None, :])
    inverse_root = 1.0 / jnp.sqrt(degree)
    picked = jnp.take_along_axis(
        start_vectors, jnp.broadcast_to(cluster_order, start_vectors.shape), axis=1
    )
    panel_now = orthonormalize(picked)
    for round_index in range(ITERS):
        vectors = (inverse_root * panel_now).astype(jnp.bfloat16)
        panel_now = orthonormalize(
            panel_now + inverse_root * collect_direct(direct_part(matrix, vectors))
        )
    total_nodes = block_len * row_count * col_count
    return math.sqrt(total_nodes) * panel_now


def solution(mesh):
    placed = (
        P(None, ("row", "col")),
        P(("row", "col"), None),
        P("row", "col", None),
        P("row", "col", None),
    )
    return jax.shard_map(
        local, mesh=mesh, in_specs=placed, out_specs=P(None, ("row", "col")), check_vma=False
    )
```

profile of v0, /device:TPU:0, one launch (start us, length us, event | category | flops | bytes accessed | tf_op | source)
XLA Modules:
  0.0 481.7 jit_solution(14483653872120444080)
XLA Ops:
  6.5 1.4 copy.55
  7.9 7.3 %all-to-all-start = ((s32[4,8,1]{0,2,1:T(1,128)}), s32[4,8,1]{0,2,1:T(1,128)S(1)}, u32[]{:S(2)}, u32[]{:S(2)}) async-start(s32[4,8,1]{0,2,1:T(1,128)} %copy.55), calls=%async_computation | async-start | bytes 8192 | tf_op jit(solution)/shard_map/all_to_all | solution.py:73
  15.2 1.5 copy.58
  18.0 3.6 all-to-all-done
  21.6 3.6 all-to-all-start.2
  25.2 50.7 %gather_fusion = f32[8192]{0:T(1024)S(1)} fusion(f32[64,128]{1,0:T(8,128)S(1)} %copy-done, s32[8192]{0:T(1024)S(1)} %or_bitcast_fusion), kind=kCustom, calls=%fused_computation | custom fusion | bytes 131072 | tf_op jit(solution)/shard_map/jit(take_along_axis)/gather | solution.py:92
  76.1 40.9 %psum.28 = f32[64,64]{0,1:T(8,128)S(1)} all-reduce(f32[64,64]{0,1:T(8,128)S(1)} %fusion.28), channel_id=1, replica_groups=mesh['row'=8,'col'=4] {'row','col'}, use_global_device_ids=true, to_apply=%region_0.1 | all-reduce | flops 4096 | bytes 32768 | tf_op jit(solution)/shard_map/psum | solution.py:19
  117.1 5.8 %cholesky.74 = f32[64,64]{1,0:T(8,128)S(1)} custom-call(f32[64,64]{1,0:T(8,128)S(1)} %fusion.27), custom_call_target="Cholesky" | custom-call | tf_op jit(solution)/shard_map/jit(cholesky)/cholesky | solution.py:20
  124.3 3.5 all-to-all-start.1
  129.8 1.7 all-to-all-done.1
  131.5 4.2 all-to-all-start.3
  136.6 13.7 %all-to-all-done.3 = bf16[4,128,1024]{2,1,0:T(8,128)(2,1)} async-done(((bf16[4,128,1024]{2,1,0:T(8,128)(2,1)}), bf16[4,128,1024]{2,1,0:T(8,128)(2,1)}, u32[]{:S(2)}, u32[]{:S(2)}) %all-to-all-start.3) | async-done | bytes 1048608 | tf_op jit(solution)/shard_map/all_to_all | solution.py:65
  150.2 1.6 copy.61
  151.9 1.5 fusion
  155.2 4.9 %custom-call.10 = f32[1,64,64]{1,2,0:T(8,128)S(1)} custom-call(f32[1,64,64]{2,1,0:T(8,128)S(1)} %fusion.13), custom_call_target="InvertDiagBlocksLowerTriangular" | custom-call | tf_op jit(solution)/shard_map/jit(_solve_triangular)/triangular_solve | solution.py:21
  160.1 14.1 %reduce-scatter.13.cloned.1.call-done = f32[128,1]{1,0:T(8,128)} async-done(((f32[512,1]{1,0:T(8,128)}), f32[128,1]{1,0:T(8,128)}) %reduce-scatter.13.cloned.1.call-update) | async-done | bytes 528
  175.4 26.2 %all_gather.9 = bf16[64,1024]{1,0:T(8,128)(2,1)S(1)} all-gather(bf16[64,128]{1,0:T(8,128)(2,1)S(1)} %get-tuple-element.9), channel_id=1, replica_groups=mesh['row'=8,'col'=4] {'row'}, dimensions={1}, use_global_device_ids=true | all-gather | bytes 147456 | tf_op jit(solution)/shard_map/all_gather | solution.py:30
  202.7 18.1 %reduce-scatter.7.cloned.1.call-done = f32[64,128]{1,0:T(8,128)} async-done(((f32[64,512]{1,0:T(8,128)}), f32[64,128]{1,0:T(8,128)}) %reduce-scatter.7.cloned.1.call-update) | async-done | bytes 32784 | tf_op jit(solution)/shard_map/reduce_scatter | solution.py:25
  221.8 39.5 %psum.29 = f32[64,64]{0,1:T(8,128)S(1)} all-reduce(f32[64,64]{0,1:T(8,128)S(1)} %fusion.52), channel_id=1, replica_groups=mesh['row'=8,'col'=4] {'row','col'}, use_global_device_ids=true, to_apply=%region_5.8 | all-reduce | flops 4096 | bytes 32768 | tf_op jit(solution)/shard_map/psum | solution.py:19
  261.4 5.8 %cholesky.85 = f32[64,64]{1,0:T(8,128)S(1)} custom-call(f32[64,64]{1,0:T(8,128)S(1)} %fusion.24), custom_call_target="Cholesky" | custom-call | tf_op jit(solution)/shard_map/jit(cholesky)/cholesky | solution.py:20
  268.6 4.9 %custom-call.11 = f32[1,64,64]{1,2,0:T(8,128)S(1)} custom-call(f32[1,64,64]{2,1,0:T(8,128)S(1)} %fusion.14), custom_call_target="InvertDiagBlocksLowerTriangular" | custom-call | tf_op jit(solution)/shard_map/jit(_solve_triangular)/triangular_solve | solution.py:21
  274.5 26.1 %all_gather.10 = bf16[64,1024]{1,0:T(8,128)(2,1)S(1)} all-gather(bf16[64,128]{1,0:T(8,128)(2,1)S(1)} %get-tuple-element.11), channel_id=1, replica_groups=mesh['row'=8,'col'=4] {'row'}, dimensions={1}, use_global_device_ids=true | all-gather | bytes 147456 | tf_op jit(solution)/shard_map/all_gather | solution.py:30
  301.8 18.9 %reduce-scatter.9.cloned.1.call-done = f32[64,128]{1,0:T(8,128)} async-done(((f32[64,512]{1,0:T(8,128)}), f32[64,128]{1,0:T(8,128)}) %reduce-scatter.9.cloned.1.call-update) | async-done | bytes 32784 | tf_op jit(solution)/shard_map/reduce_scatter | solution.py:25
  321.7 39.7 %psum.30 = f32[64,64]{0,1:T(8,128)S(1)} all-reduce(f32[64,64]{0,1:T(8,128)S(1)} %fusion.53), channel_id=1, replica_groups=mesh['row'=8,'col'=4] {'row','col'}, use_global_device_ids=true, to_apply=%region_7.10 | all-reduce | flops 4096 | bytes 32768 | tf_op jit(solution)/shard_map/psum | solution.py:19
  361.5 5.8 %cholesky.96 = f32[64,64]{1,0:T(8,128)S(1)} custom-call(f32[64,64]{1,0:T(8,128)S(1)} %fusion.21), custom_call_target="Cholesky" | custom-call | tf_op jit(solution)/shard_map/jit(cholesky)/cholesky | solution.py:20
  368.7 4.9 %custom-call.12 = f32[1,64,64]{1,2,0:T(8,128)S(1)} custom-call(f32[1,64,64]{2,1,0:T(8,128)S(1)} %fusion.15), custom_call_target="InvertDiagBlocksLowerTriangular" | custom-call | tf_op jit(solution)/shard_map/jit(_solve_triangular)/triangular_solve | solution.py:21
  374.6 26.1 %all_gather.11 = bf16[64,1024]{1,0:T(8,128)(2,1)S(1)} all-gather(bf16[64,128]{1,0:T(8,128)(2,1)S(1)} %get-tuple-element.13), channel_id=1, replica_groups=mesh['row'=8,'col'=4] {'row'}, dimensions={1}, use_global_device_ids=true | all-gather | bytes 147456 | tf_op jit(solution)/shard_map/all_gather | solution.py:30
  401.9 18.9 %reduce-scatter.11.cloned.1.call-done = f32[64,128]{1,0:T(8,128)} async-done(((f32[64,512]{1,0:T(8,128)}), f32[64,128]{1,0:T(8,128)}) %reduce-scatter.11.cloned.1.call-update) | async-done | bytes 32784 | tf_op jit(solution)/shard_map/reduce_scatter | solution.py:25
  421.8 39.5 %psum.31 = f32[64,64]{0,1:T(8,128)S(1)} all-reduce(f32[64,64]{0,1:T(8,128)S(1)} %fusion.54), channel_id=1, replica_groups=mesh['row'=8,'col'=4] {'row','col'}, use_global_device_ids=true, to_apply=%region_9.12 | all-reduce | flops 4096 | bytes 32768 | tf_op jit(solution)/shard_map/psum | solution.py:19
  461.4 5.8 %cholesky.107 = f32[64,64]{1,0:T(8,128)S(1)} custom-call(f32[64,64]{1,0:T(8,128)S(1)} %fusion.18), custom_call_target="Cholesky" | custom-call | tf_op jit(solution)/shard_map/jit(cholesky)/cholesky | solution.py:20
  468.6 4.9 %custom-call.13 = f32[1,64,64]{1,2,0:T(8,128)S(1)} custom-call(f32[1,64,64]{2,1,0:T(8,128)S(1)} %fusion.16), custom_call_target="InvertDiagBlocksLowerTriangular" | custom-call | tf_op jit(solution)/shard_map/jit(_solve_triangular)/triangular_solve | solution.py:21
  473.5 1.6 convolution_multiply_fusion
  (66 shorter events, 21.4 us)
Async XLA Ops:
  6.5 18.7 %copy-start = (f32[64,128]{1,0:T(8,128)S(1)}, f32[64,128]{1,0:T(8,128)}, u32[]{:S(2)}) copy-start(f32[64,128]{1,0:T(8,128)} %param.7) | copy-start | bytes 98308
  7.9 13.7 %all-to-all-start = ((s32[4,8,1]{0,2,1:T(1,128)}), s32[4,8,1]{0,2,1:T(1,128)S(1)}, u32[]{:S(2)}, u32[]{:S(2)}) async-start(s32[4,8,1]{0,2,1:T(1,128)} %copy.55), calls=%async_computation | async-start | bytes 8192 | tf_op jit(solution)/shard_map/all_to_all | solution.py:73
  18.0 7.1 %copy-start.3 = (s32[1,128]{1,0:T(1,128)S(1)}, s32[1,128]{1,0:T(1,128)}, u32[]{:S(2)}) copy-start(s32[1,128]{1,0:T(1,128)} %param.8) | copy-start | bytes 1540
  21.6 102.7 %all-to-all-start.2 = ((bf16[512,8,128]{2,0,1:T(8,128)(2,1)}), bf16[512,8,128]{2,0,1:T(8,128)(2,1)S(1)}, u32[]{:S(2)}, u32[]{:S(2)}) async-start(bf16[512,8,128]{2,0,1:T(8,128)(2,1)} %copy.59), calls=%async_computation.2 | async-start | bytes 2097152 | tf_op jit(solution)/shard_map/all_to_all | solution.py:66
  124.3 7.2 %all-to-all-start.1 = ((s32[4,1,8]{2,1,0:T(1,128)}), s32[4,1,8]{2,1,0:T(1,128)S(1)}, u32[]{:S(2)}, u32[]{:S(2)}) async-start(s32[4,1,8]{2,1,0:T(1,128)} %copy.57), calls=%async_computation.1 | async-start | bytes 4096 | tf_op jit(solution)/shard_map/all_to_all | solution.py:72
  129.8 6.0 %copy-start.1 = (bf16[512,1,1024]{2,0,1:T(8,128)(2,1)S(1)}, bf16[512,1,1024]{2,0,1:T(8,128)(2,1)}, u32[]{:S(2)}) copy-start(bf16[512,1,1024]{2,0,1:T(8,128)(2,1)} %param.9) | copy-start | bytes 3145732
  131.5 18.8 %all-to-all-start.3 = ((bf16[4,128,1024]{2,1,0:T(8,128)(2,1)}), bf16[4,128,1024]{2,1,0:T(8,128)(2,1)}, u32[]{:S(2)}, u32[]{:S(2)}) async-start(bf16[4,128,1024]{2,1,0:T(8,128)(2,1)} %all_to_all.30), calls=%async_computation.3 | async-start | bytes 2097152 | tf_op jit(solution)/shard_map/all_to_all | solution.py:65
  135.7 38.5 %reduce-scatter.13.cloned.1.call-start = ((), (), s32[]{:S(2)}) async-start(), calls=%async_computation.11 | async-start | bytes 327680
  135.8 0.7 copy-start.2
  154.5 66.3 %reduce-scatter.7.cloned.1.call-start = ((), (), s32[]{:S(2)}) async-start(), calls=%async_computation.8 | async-start | bytes 163840 | tf_op jit(solution)/shard_map/reduce_scatter | solution.py:25
  202.7 118.0 %reduce-scatter.9.cloned.1.call-start = ((), (), s32[]{:S(2)}) async-start(), calls=%async_computation.9 | async-start | bytes 163840 | tf_op jit(solution)/shard_map/reduce_scatter | solution.py:25
  301.7 119.0 %reduce-scatter.11.cloned.1.call-start = ((), (), s32[]{:S(2)}) async-start(), calls=%async_computation.10 | async-start | bytes 163840 | tf_op jit(solution)/shard_map/reduce_scatter | solution.py:25
Sparse Core Ops, SparseCore 0:
  154.6 19.4 reduce-scatter.12
  202.8 17.9 reduce-scatter.6
  301.9 18.8 reduce-scatter.8
  402.0 18.7 reduce-scatter.10
where the time goes:
time: 483 us; the launch traced here: 482 us
  blocking collectives  238 us (49%)
  waiting for transfers between devices  89 us (18%)
  local copies, waits for them, and re-layouts  61 us (13%)
  other arithmetic  50 us (10%)
  starting transfers between devices  18.8 us (4%)
  between operations  13.5 us (3%)
  matrix products  11.5 us (2%)
    psum x4, blocking collectives, orthonormalize(): total_gram = lax.psum(partial_gram, ('row', 'col'))  160 us
    all_gather x3, blocking collectives, direct_part(): lax.all_gather(vectors, 'row', axis=1, tiled=True)  78.5 us
    reduce_scatter x3, waiting for transfers between devices, collect_direct(): return lax.psum_scatter(term, 'col', scatter_dimension=1, tiled=True)  55.9 us
    gather x1, local copies, waits for them, and re-layouts, local(): jnp.take_along_axis(start_vectors, jnp.broadcast_to(cluster_order, start_...  50.7 us
    another operation x12, other arithmetic, orthonormalize(): factor = jnp.linalg.cholesky(total_gram)  26.1 us
    another operation x8, other arithmetic, orthonormalize(): return jax.scipy.linalg.solve_triangular(factor, panel_in, lower=True)  22.2 us
    unnamed x5, waiting for transfers between devices  14.2 us
    all_to_all x1, waiting for transfers between devices, local(): lax.all_to_all(lax.all_to_all(stored, 'row', split_axis=1, concat_axis=1,...  13.7 us
  transfers between devices with their start and end apart: 8, of which 7 were waited for; matrix products, arithmetic and copies ran while one was open for 14% of the time, Pallas kernels for 0%

commit v1 on v0

v1 whole, which is shorter than its diff:
```python
import math

import jax
import jax.numpy as jnp
from jax import lax
from jax.experimental import pallas as pl
from jax.experimental.pallas import tpu as pltpu
from jax.sharding import PartitionSpec as P

ITERS = 3
HIGHEST = lax.Precision.HIGHEST
F32 = jnp.float32
BF16 = jnp.bfloat16


def dot(a, b, contract, precision=None):
    return lax.dot_general(
        a, b, ((contract[0], contract[1]), ((), ())), precision=precision, preferred_element_type=F32
    )


def lanes(blocks):
    return jnp.concatenate(blocks, axis=1)


def inverse_factor(gram):
    k = gram.shape[0]
    rows = lax.broadcasted_iota(jnp.int32, (k, 1), 0)
    diagonal = rows == lax.broadcasted_iota(jnp.int32, (k, k), 1)
    work = lanes([gram, diagonal.astype(F32)])
    for step in range(k):
        ratio = work[:, step : step + 1] / work[step : step + 1, step : step + 1]
        work = work - jnp.where(rows > step, ratio, 0.0) * work[step : step + 1, :]
    pivots = jnp.sum(jnp.where(diagonal, work[:, :k], 0.0), axis=1, keepdims=True)
    return work[:, k:] * (1.0 / jnp.sqrt(pivots))


def prepare_kernel(width, mask_ref, stored_ref, start_ref, order_ref, by_row_ref, by_col_ref, piece_ref):
    cols, rows = mask_ref.shape
    here_row, here_col = lax.axis_index("row"), lax.axis_index("col")
    upper = (
        lax.broadcasted_iota(jnp.int32, (width, width), 0) < lax.broadcasted_iota(jnp.int32, (width, width), 1)
    ).astype(F32)
    for j in range(cols):
        row_block = here_row * cols + j
        for i in range(rows):
            col_block = i * cols + here_col
            whole = jnp.where((mask_ref[j, i] > 0) & (row_block < col_block), 1.0, 0.0)
            partly = jnp.where(row_block == col_block, 1.0, 0.0)
            keep = (whole + partly * upper).astype(BF16)
            block = stored_ref[j * width : (j + 1) * width, i * width : (i + 1) * width] * keep
            by_row_ref[j, :, i * width : (i + 1) * width] = block
            by_col_ref[i, j * width : (j + 1) * width, :] = block
    slots = lax.broadcasted_iota(jnp.int32, (width, width), 0)
    chosen = (slots == order_ref[...]).astype(F32)
    picked = dot(start_ref[...], chosen, ((1,), (0,)), HIGHEST)
    k = picked.shape[0]
    degrees = [
        dot(jnp.ones((8, cols * width), BF16), by_col_ref[i], ((1,), (0,)))[0:1] for i in range(rows)
    ] + [dot(jnp.ones((8, rows * width), BF16), by_row_ref[j], ((1,), (1,)))[0:1] for j in range(cols)]
    spare = piece_ref.shape[1] - k - rows - cols
    if spare:
        degrees.append(jnp.zeros((spare, width), F32))
    degrees = jnp.concatenate(degrees, axis=0)
    for i in range(rows):
        piece_ref[i, :k] = picked
        piece_ref[i, k:] = degrees


def first_kernel(k, all_ref, vectors_ref, roots_ref, own_ref):
    cols, rows, _, width = all_ref.shape
    here_row, here_col = lax.axis_index("row"), lax.axis_index("col")
    for c in range(cols):
        part = all_ref[c, 0, k : k + rows]
        for i in range(1, rows):
            part = part + all_ref[c, i, k : k + rows]
        for i in range(rows):
            other = all_ref[0, i, k + rows + c : k + rows + c + 1]
            for e in range(1, cols):
                other = other + all_ref[e, i, k + rows + c : k + rows + c + 1]
            roots_ref[c, i : i + 1] = 1.0 / jnp.sqrt(part[i : i + 1] + other)
    gram = jnp.zeros((k, k), F32)
    for c in range(cols):
        panel = lanes([all_ref[c, i, :k] for i in range(rows)])
        gram = gram + dot(panel, panel, ((1,), (1,)), HIGHEST)
    factor = inverse_factor(gram)
    for c in range(cols):
        panel = dot(factor, lanes([all_ref[c, i, :k] for i in range(rows)]), ((1,), (0,)), HIGHEST)
        for i in range(rows):
            vectors_ref[c, i] = (panel[:, i * width : (i + 1) * width] * roots_ref[c, i : i + 1]).astype(BF16)
    own_ref[...] = dot(factor, all_ref[here_col, here_row, :k], ((1,), (0,)), HIGHEST)


def product(vectors_of, by_row_ref, by_col_ref):
    cols, rows = by_row_ref.shape[0], by_col_ref.shape[0]
    total = None
    for c in range(cols):
        term = dot(lanes([vectors_of(c, i) for i in range(rows)]), by_row_ref[c], ((1,), (1,)))
        total = term if total is None else total + term
    for i in range(rows):
        total = total + dot(lanes([vectors_of(c, i) for c in range(cols)]), by_col_ref[i], ((1,), (0,)))
    return total


def own_root(roots_ref):
    here_row, here_col = lax.axis_index("row"), lax.axis_index("col")
    return roots_ref[here_col, pl.ds(here_row, 1)]


def step_one_kernel(vectors_ref, own_ref, roots_ref, by_row_ref, by_col_ref, out_ref):
    total = product(lambda c, i: vectors_ref[c, i], by_row_ref, by_col_ref)
    image = own_ref[...] + own_root(roots_ref) * total
    for i in range(out_ref.shape[0]):
        out_ref[i] = image


def raw_image(panel_ref, roots_ref, by_row_ref, by_col_ref, scratch):
    cols, rows, k, _ = panel_ref.shape
    here_row, here_col = lax.axis_index("row"), lax.axis_index("col")
    for c in range(cols):
        for i in range(rows):
            value = panel_ref[c, i] * roots_ref[c, i : i + 1]
            high = value.astype(BF16)
            scratch[c, i, :k] = high
            scratch[c, i, k:] = (value - high.astype(F32)).astype(BF16)
    total = product(lambda c, i: scratch[c, i], by_row_ref, by_col_ref)
    return panel_ref[here_col, here_row] + own_root(roots_ref) * (total[:k] + total[k:])


def step_kernel(panel_ref, roots_ref, by_row_ref, by_col_ref, out_ref, scratch):
    image = raw_image(panel_ref, roots_ref, by_row_ref, by_col_ref, scratch)
    for i in range(out_ref.shape[0]):
        out_ref[i] = image


def last_step_kernel(panel_ref, roots_ref, by_row_ref, by_col_ref, factor_ref, out_ref, gram_ref, scratch):
    image = raw_image(panel_ref, roots_ref, by_row_ref, by_col_ref, scratch)
    image = dot(factor_ref[...], image, ((1,), (0,)), HIGHEST)
    out_ref[...] = image
    gram = dot(image, image, ((1,), (1,)), HIGHEST)
    half = gram.shape[0] // 2
    gram = lanes([gram[:half], gram[half:]])
    for i in range(gram_ref.shape[0]):
        gram_ref[i] = gram


def panel_gram(panel_ref):
    cols, rows, k, _ = panel_ref.shape
    gram = jnp.zeros((k, k), F32)
    for c in range(cols):
        panel = lanes([panel_ref[c, i] for i in range(rows)])
        gram = gram + dot(panel, panel, ((1,), (1,)), HIGHEST)
    return gram


def congruent(factor, gram):
    half = dot(factor, gram, ((1,), (0,)), HIGHEST)
    return dot(half, factor, ((1,), (1,)), HIGHEST)


def factor_kernel(panel_ref, factor_ref):
    factor_ref[...] = inverse_factor(panel_gram(panel_ref))


def next_factor_kernel(panel_ref, before_ref, factor_ref):
    factor_ref[...] = inverse_factor(congruent(before_ref[...], panel_gram(panel_ref)))


def finish_kernel(scale, grams_ref, factor_ref, image_ref, out_ref):
    packed = grams_ref[0]
    for c in range(1, grams_ref.shape[0]):
        packed = packed + grams_ref[c]
    k = factor_ref.shape[0]
    gram = jnp.concatenate([packed[:, :k], packed[:, k:]], axis=0)
    factor = inverse_factor(congruent(factor_ref[...], gram))
    image = dot(factor_ref[...], image_ref[...], ((1,), (0,)), HIGHEST)
    out_ref[...] = scale * dot(factor, image, ((1,), (0,)), HIGHEST)


def kernel_call(body, outs, *operands, scratch=(), smem=0, flops=0):
    sizes = [math.prod(a.shape) * a.dtype.itemsize for a in (*operands, *outs)]
    spec = pl.BlockSpec(memory_space=pltpu.VMEM)
    held = sum(sizes) + sum(math.prod(s.shape) * 2 for s in scratch)
    single = len(outs) == 1
    return pl.pallas_call(
        body,
        out_shape=outs[0] if single else tuple(outs),
        in_specs=[pl.BlockSpec(memory_space=pltpu.SMEM)] * smem + [spec] * (len(operands) - smem),
        out_specs=spec if single else (spec,) * len(outs),
        scratch_shapes=list(scratch),
        cost_estimate=pl.CostEstimate(flops=flops, bytes_accessed=sum(sizes), transcendentals=0),
        compiler_params=pltpu.CompilerParams(vmem_limit_bytes=held + held // 4 + (8 << 20)),
    )(*operands)


def gather_all(copies):
    return lax.all_gather(lax.all_to_all(copies, "row", 0, 0, tiled=True), "col", axis=0, tiled=False)


def local(start_vectors, cluster_order, weights, block_mask):
    rows, cols = lax.axis_size("row"), lax.axis_size("col")
    k, width = start_vectors.shape
    shape = jax.ShapeDtypeStruct
    extra = -(-(rows + cols) // 8) * 8
    by_row, by_col, piece = kernel_call(
        lambda *refs: prepare_kernel(width, *refs),
        [
            shape((cols, width, rows * width), BF16),
            shape((rows, cols * width, width), BF16),
            shape((rows, k + extra, width), F32),
        ],
        block_mask[:, 0, :],
        weights[:, 0, :],
        start_vectors,
        cluster_order,
        smem=1,
    )
    by_row = lax.all_to_all(by_row, "col", 0, 0, tiled=True)
    by_col = lax.all_to_all(by_col, "row", 0, 0, tiled=True)
    vectors, roots, own = kernel_call(
        lambda *refs: first_kernel(k, *refs),
        [shape((cols, rows, k, width), BF16), shape((cols, rows, width), F32), shape((k, width), F32)],
        gather_all(piece),
    )
    copies = shape((rows, k, width), F32)
    factor_shape = shape((k, k), F32)
    split = [pltpu.VMEM((cols, rows, 2 * k, width), BF16)]
    panel = gather_all(kernel_call(step_one_kernel, [copies], vectors, own, roots, by_row, by_col))
    image = kernel_call(step_kernel, [copies], panel, roots, by_row, by_col, scratch=split)
    factor = kernel_call(factor_kernel, [factor_shape], panel)
    panel = gather_all(image)
    image, gram = kernel_call(
        last_step_kernel,
        [shape((k, width), F32), shape((rows, k // 2, 2 * k), F32)],
        panel,
        roots,
        by_row,
        by_col,
        factor,
        scratch=split,
    )
    factor = kernel_call(next_factor_kernel, [factor_shape], panel, factor)
    gram = lax.all_to_all(gram, "row", 0, 0, tiled=True).sum(axis=0)
    gram = lax.all_gather(gram, "col", axis=0, tiled=False)
    scale = math.sqrt(width * rows * cols)
    return kernel_call(
        lambda *refs: finish_kernel(scale, *refs), [shape((k, width), F32)], gram, factor, image
    )


def solution(mesh):
    placed = (
        P(None, ("row", "col")),
        P(("row", "col"), None),
        P("row", "col", None),
        P("row", "col", None),
    )
    return jax.shard_map(
        local, mesh=mesh, in_specs=placed, out_specs=P(None, ("row", "col")), check_vma=False
    )
```

time: 483 us -> 176 us (0.36)
  blocking collectives: 238 us -> 50.4 us
  local copies, waits for them, and re-layouts: 61 us -> 7.09 us
  other arithmetic: 50 us -> 0.01 us
  Pallas kernels: 0 us -> 34.3 us
  waiting for transfers between devices: 89 us -> 58.1 us
  matrix products: 11.5 us -> 0 us
  starting transfers between devices: 18.8 us -> 12.7 us
    psum x4 -> x0, blocking collectives: 160 us -> none  [orthonormalize(): total_gram = lax.psum(partial_gram, ('row', 'col'))]
    all_gather x3 -> x1, blocking collectives: 78.5 us -> 5.25 us  [local(): gram = lax.all_gather(gram, 'col', axis=0, tiled=False)]
    reduce_scatter x3 -> x0, waiting for transfers between devices: 55.9 us -> none  [collect_direct(): return lax.psum_scatter(term, 'col', scatter_dimension=1, tiled=True)]
    gather x1 -> x0, local copies, waits for them, and re-layouts: 50.7 us -> none  [local(): jnp.take_along_axis(start_vectors, jnp.broadcast_to(cluster_order, start_...]
    another operation x20 -> x0, other arithmetic: 48.2 us -> none  [the longest x12 26.1 us: orthonormalize(): factor = jnp.linalg.cholesky(total_gram)]
    all_to_all x0 -> x3, blocking collectives: none -> 45.2 us  [gather_all(): lax.all_to_all(copies, 'row', 0, 0, tiled=True)]
    pallas_call x0 -> x8, Pallas kernels: none -> 34.3 us  [kernel_call(): pl.pallas_call(body, out_shape=outs[0] if single else tuple(outs), in_spe...]
    all_gather x0 -> x3, waiting for transfers between devices: none -> 25.6 us  [gather_all(): lax.all_gather(lax.all_to_all(copies, 'row', 0, 0, tiled=True), 'col', ax...]
  transfers between devices with their start and end apart: 8 -> 6, of which waited for: 7 -> 6; matrix products, arithmetic and copies ran while one was open for 14% -> 0% of each run, Pallas kernels for 0% -> 13%
where the time goes in v1:
time: 176 us
  waiting for transfers between devices  58.1 us (33%)
  blocking collectives  50.4 us (29%)
  Pallas kernels  34.3 us (19%)
  between operations  13.2 us (8%)
  starting transfers between devices  12.7 us (7%)
  local copies, waits for them, and re-layouts  7.09 us (4%)
    all_to_all x3, blocking collectives, gather_all(): lax.all_to_all(copies, 'row', 0, 0, tiled=True)  45.2 us
    pallas_call x8, Pallas kernels, kernel_call(): pl.pallas_call(body, out_shape=outs[0] if single else tuple(outs), in_spe...  34.3 us
    all_gather x3, waiting for transfers between devices, gather_all(): lax.all_gather(lax.all_to_all(copies, 'row', 0, 0, tiled=True), 'col', ax...  25.6 us
    all_to_all x1, waiting for transfers between devices, local(): by_row = lax.all_to_all(by_row, 'col', 0, 0, tiled=True)  17.5 us
    all_to_all x1, waiting for transfers between devices, local(): by_col = lax.all_to_all(by_col, 'row', 0, 0, tiled=True)  13.7 us
    unnamed x18, local copies, waits for them, and re-layouts  7.09 us
    all_to_all x1, starting transfers between devices, local(): gram = lax.all_to_all(gram, 'row', 0, 0, tiled=True).sum(axis=0)  5.52 us
    all_gather x1, blocking collectives, local(): gram = lax.all_gather(gram, 'col', axis=0, tiled=False)  5.25 us
  transfers between devices with their start and end apart: 6, of which 6 were waited for; matrix products, arithmetic and copies ran while one was open for 0% of the time, Pallas kernels for 13%

profile of v1, /device:TPU:0, one launch (start us, length us, event | category | flops | bytes accessed | tf_op | source)
XLA Modules:
  0.0 175.8 jit_solution(13155439783512161457)
XLA Ops:
  6.5 1.2 copy-done.5
  7.8 0.8 copy-done.6
  8.5 0.7 copy-done.7
  9.2 0.7 copy-done.8
  9.9 2.4 %shard_map.46 = (bf16[4,128,1024]{2,1,0:T(8,128)(2,1)}, bf16[8,512,128]{2,1,0:T(8,128)(2,1)}, f32[8,80,128]{2,1,0:T(8,128)S(1)}) custom-call(s32[4,8]{1,0:T(4,128)S(1)} %bitcast.13, bf16[512,1024]{1,0:T(8,128)(2,1)S(1)} %bitcast.11, f32[64,128]{1,0:T(8,128)S(1)} %copy-done.6, s32[1,128]{1,0:T(1,128)S(1)} %copy-done.8), custom_call_target="tpu_custom_call" | custom-call | bytes 3506816 | tf_op jit(solution)/shard_map/pallas_call | solution.py:185
  12.3 18.1 %all_to_all.30 = f32[8,80,128]{2,1,0:T(8,128)} all-to-all(f32[8,80,128]{2,1,0:T(8,128)S(1)} %get-tuple-element.13), channel_id=1, replica_groups=mesh['row'=8,'col'=4] {'row'}, dimensions={0} | all-to-all | bytes 655360 | tf_op jit(solution)/shard_map/all_to_all | solution.py:197
  30.3 3.5 %all-to-all-start.1 = ((bf16[4,128,1024]{2,1,0:T(8,128)(2,1)}), bf16[4,128,1024]{2,1,0:T(8,128)(2,1)S(1)}, u32[]{:S(2)}, u32[]{:S(2)}) async-start(bf16[4,128,1024]{2,1,0:T(8,128)(2,1)} %get-tuple-element.17), calls=%async_computation.1 | async-start | bytes 2097152 | tf_op jit(solution)/shard_map/all_to_all | solution.py:218
  33.9 0.0 all-gather.8.cloned.1.call-start
  33.9 0.7 all-gather.8.cloned.1.call-update
  34.6 17.5 %all-to-all-done.1.by_row_ref = bf16[4,128,1024]{2,1,0:T(8,128)(2,1)S(1)} async-done(((bf16[4,128,1024]{2,1,0:T(8,128)(2,1)}), bf16[4,128,1024]{2,1,0:T(8,128)(2,1)S(1)}, u32[]{:S(2)}, u32[]{:S(2)}) %all-to-all-start.1) | async-done | bytes 1048608 | tf_op jit(solution)/shard_map/all_to_all | solution.py:218
  52.1 3.6 %all-to-all-start.2 = ((bf16[8,512,128]{2,1,0:T(8,128)(2,1)}), bf16[8,512,128]{2,1,0:T(8,128)(2,1)S(1)}, u32[]{:S(2)}, u32[]{:S(2)}) async-start(bf16[8,512,128]{2,1,0:T(8,128)(2,1)} %get-tuple-element.18), calls=%async_computation.2 | async-start | bytes 2097152 | tf_op jit(solution)/shard_map/all_to_all | solution.py:219
  55.6 0.0 all-gather.10.cloned.1.call-start
  55.7 1.1 all-gather.8.cloned.1.call-done
  56.8 1.3 copy-done.4
  58.1 8.9 %shard_map.47 = (bf16[4,8,64,128]{3,2,1,0:T(8,128)(2,1)S(1)}, f32[4,8,128]{2,1,0:T(8,128)S(1)}, f32[64,128]{1,0:T(8,128)S(1)}) custom-call(f32[4,8,80,128]{3,2,1,0:T(8,128)S(1)} %bitcast.10), custom_call_target="tpu_custom_call" | custom-call | bytes 1884160 | tf_op jit(solution)/shard_map/pallas_call | solution.py:185
  67.0 13.7 %all-to-all-done.2.by_col_ref = bf16[8,512,128]{2,1,0:T(8,128)(2,1)S(1)} async-done(((bf16[8,512,128]{2,1,0:T(8,128)(2,1)}), bf16[8,512,128]{2,1,0:T(8,128)(2,1)S(1)}, u32[]{:S(2)}, u32[]{:S(2)}) %all-to-all-start.2) | async-done | bytes 1048608 | tf_op jit(solution)/shard_map/all_to_all | solution.py:219
  80.8 0.6 shard_map.48
  81.4 12.4 %all_to_all.31 = f32[8,64,128]{2,1,0:T(8,128)} all-to-all(f32[8,64,128]{2,1,0:T(8,128)S(1)} %shard_map.48), channel_id=1, replica_groups=mesh['row'=8,'col'=4] {'row'}, dimensions={0} | all-to-all | bytes 524288 | tf_op jit(solution)/shard_map/all_to_all | solution.py:197
  93.8 0.0 all-gather.12.cloned.1.call-start
  93.9 15.3 %all-gather.10.cloned.1.call-done = f32[32,64,128]{2,1,0:T(8,128)} async-done(((f32[8,64,128]{2,1,0:T(8,128)}), f32[32,64,128]{2,1,0:T(8,128)}) %all-gather.10.cloned.1.call-update) | async-done | bytes 1048592 | tf_op jit(solution)/shard_map/all_gather | solution.py:197
  109.1 1.2 copy-done.2
  110.4 0.8 shard_map.49
  111.1 14.7 %all_to_all.32 = f32[8,64,128]{2,1,0:T(8,128)} all-to-all(f32[8,64,128]{2,1,0:T(8,128)S(1)} %shard_map.49), channel_id=1, replica_groups=mesh['row'=8,'col'=4] {'row'}, dimensions={0} | all-to-all | bytes 524288 | tf_op jit(solution)/shard_map/all_to_all | solution.py:197
  125.9 6.4 %shard_map.50.factor_ref.before_ref = f32[64,64]{1,0:T(8,128)S(1)} custom-call(f32[4,8,64,128]{3,2,1,0:T(8,128)S(1)} %bitcast.9), custom_call_target="tpu_custom_call" | custom-call | bytes 1064960 | tf_op jit(solution)/shard_map/pallas_call | solution.py:185
  132.3 9.2 %all-gather.12.cloned.1.call-done = f32[32,64,128]{2,1,0:T(8,128)} async-done(((f32[8,64,128]{2,1,0:T(8,128)}), f32[32,64,128]{2,1,0:T(8,128)}) %all-gather.12.cloned.1.call-update) | async-done | bytes 1048592 | tf_op jit(solution)/shard_map/all_gather | solution.py:197
  141.5 1.2 copy-done
  142.7 1.8 %shard_map.51 = (f32[64,128]{1,0:T(8,128)S(1)}, f32[8,32,128]{2,1,0:T(8,128)}) custom-call(f32[4,8,64,128]{3,2,1,0:T(8,128)S(1)} %bitcast.6, f32[4,8,128]{2,1,0:T(8,128)S(1)} %get-tuple-element.16.roots_ref, bf16[4,128,1024]{2,1,0:T(8,128)(2,1)S(1)} %all-to-all-done.1.by_row_ref, bf16[8,512,128]{2,1,0:T(8,128)(2,1)S(1)} %all-to-all-done.2.by_col_ref, ...), custom_call_target="tpu_custom_call" | custom-call | bytes 3342336 | tf_op jit(solution)/shard_map/pallas_call | solution.py:185
  144.5 5.5 %all-to-all-start.5 = ((f32[8,32,128]{2,1,0:T(8,128)}), f32[8,32,128]{2,1,0:T(8,128)S(1)}, u32[]{:S(2)}, u32[]{:S(2)}) async-start(f32[8,32,128]{2,1,0:T(8,128)} %get-tuple-element.19), calls=%async_computation.5 | async-start | bytes 262144 | tf_op jit(solution)/shard_map/all_to_all | solution.py:243
  150.0 6.8 %shard_map.52.refs_1_ = f32[64,64]{1,0:T(8,128)S(1)} custom-call(f32[4,8,64,128]{3,2,1,0:T(8,128)S(1)} %bitcast.7, f32[64,64]{1,0:T(8,128)S(1)} %shard_map.50.factor_ref.before_ref), custom_call_target="tpu_custom_call" | custom-call | bytes 1081344 | tf_op jit(solution)/shard_map/pallas_call | solution.py:185
  156.9 0.6 all-to-all-done.5
  157.4 5.2 %all-gather.3 = f32[128,128]{1,0:T(8,128)S(1)} all-gather(f32[32,128]{1,0:T(8,128)S(1)} %reduce_sum.9), channel_id=5, replica_groups=mesh['row'=8,'col'=4] {'col'}, dimensions={0}, use_global_device_ids=true | all-gather | bytes 81920 | tf_op jit(solution)/shard_map/all_gather | solution.py:244
  162.7 6.6 %shard_map.53 = f32[64,128]{1,0:T(8,128)} custom-call(f32[4,32,128]{2,1,0:T(8,128)S(1)} %bitcast.12, f32[64,64]{1,0:T(8,128)S(1)} %shard_map.52.refs_1_, f32[64,128]{1,0:T(8,128)S(1)} %get-tuple-element.20.refs_2_), custom_call_target="tpu_custom_call" | custom-call | bytes 147456 | tf_op jit(solution)/shard_map/pallas_call | solution.py:185
  (14 shorter events, 0.1 us)
Async XLA Ops:
  6.5 1.2 copy-start.5
  7.8 0.8 copy-start.6
  8.5 0.7 copy-start.7
  9.2 0.7 copy-start.8
  30.3 21.7 %all-to-all-start.1 = ((bf16[4,128,1024]{2,1,0:T(8,128)(2,1)}), bf16[4,128,1024]{2,1,0:T(8,128)(2,1)S(1)}, u32[]{:S(2)}, u32[]{:S(2)}) async-start(bf16[4,128,1024]{2,1,0:T(8,128)(2,1)} %get-tuple-element.17), calls=%async_computation.1 | async-start | bytes 2097152 | tf_op jit(solution)/shard_map/all_to_all | solution.py:218
  33.9 22.9 %all-gather.8.cloned.1.call-start = ((), (), s32[]{:S(2)}) async-start(), calls=%async_computation.6 | async-start | bytes 1638400 | tf_op jit(solution)/shard_map/all_gather | solution.py:197
  52.1 28.7 %all-to-all-start.2 = ((bf16[8,512,128]{2,1,0:T(8,128)(2,1)}), bf16[8,512,128]{2,1,0:T(8,128)(2,1)S(1)}, u32[]{:S(2)}, u32[]{:S(2)}) async-start(bf16[8,512,128]{2,1,0:T(8,128)(2,1)} %get-tuple-element.18), calls=%async_computation.2 | async-start | bytes 2097152 | tf_op jit(solution)/shard_map/all_to_all | solution.py:219
  55.6 53.5 %all-gather.10.cloned.1.call-start = ((), (), s32[]{:S(2)}) async-start(), calls=%async_computation.7 | async-start | bytes 1310720 | tf_op jit(solution)/shard_map/all_gather | solution.py:197
  56.8 1.3 copy-start.4
  93.8 47.6 %all-gather.12.cloned.1.call-start = ((), (), s32[]{:S(2)}) async-start(), calls=%async_computation.8 | async-start | bytes 1310720 | tf_op jit(solution)/shard_map/all_gather | solution.py:197
  109.1 1.2 copy-start.2
  110.4 15.5 %copy-start.3 = (f32[32,64,128]{2,1,0:T(8,128)S(1)}, f32[32,64,128]{2,1,0:T(8,128)}, u32[]{:S(2)}) copy-start(f32[32,64,128]{2,1,0:T(8,128)} %all-gather.10.cloned.1.call-done) | copy-start | bytes 3145732
  141.5 1.2 copy-start
  142.7 7.4 %copy-start.1 = (f32[32,64,128]{2,1,0:T(8,128)S(1)}, f32[32,64,128]{2,1,0:T(8,128)}, u32[]{:S(2)}) copy-start(f32[32,64,128]{2,1,0:T(8,128)} %all-gather.12.cloned.1.call-done) | copy-start | bytes 3145732
  144.5 12.9 %all-to-all-start.5 = ((f32[8,32,128]{2,1,0:T(8,128)}), f32[8,32,128]{2,1,0:T(8,128)S(1)}, u32[]{:S(2)}, u32[]{:S(2)}) async-start(f32[8,32,128]{2,1,0:T(8,128)} %get-tuple-element.19), calls=%async_computation.5 | async-start | bytes 262144 | tf_op jit(solution)/shard_map/all_to_all | solution.py:243
Sparse Core Ops, SparseCore 0:
  36.3 20.5 all-gather.7
  93.9 15.1 all-gather.9
  126.0 15.3 all-gather.11

commit v2 on v1

v2 whole, which is shorter than its diff:
```python
import math

import jax
import jax.numpy as jnp
from jax import lax
from jax.experimental import pallas as pl
from jax.experimental.pallas import tpu as pltpu
from jax.sharding import PartitionSpec as P

ITERS = 3
HIGHEST = lax.Precision.HIGHEST
F32 = jnp.float32
BF16 = jnp.bfloat16


def dot(a, b, contract, precision=None):
    return lax.dot_general(
        a, b, ((contract[0], contract[1]), ((), ())), precision=precision, preferred_element_type=F32
    )


def lanes(blocks):
    return jnp.concatenate(blocks, axis=1)


def inverse_factor(gram, tile=8):
    k = gram.shape[0]
    diagonal = lax.broadcasted_iota(jnp.int32, (k, k), 0) == lax.broadcasted_iota(jnp.int32, (k, k), 1)
    work = lanes([diagonal.astype(F32), gram])
    tiles = [work[at : at + tile] for at in range(0, k, tile)]
    row = lax.broadcasted_iota(jnp.int32, (tile, 2 * k), 0)

    def spread(part):
        return jnp.broadcast_to(part, (tile, 2 * k))

    done = []
    for b in range(len(tiles)):
        live = range(b, len(tiles))
        first = k + tile * b
        column = {
            (q, t): spread(tiles[t][:, first + q : first + q + 1]) for q in range(tile) for t in live
        }
        pivots = jnp.ones((tile, 2 * k), F32)
        for q in range(tile):
            pivot = spread(column[q, b][q : q + 1])
            pivots = jnp.where(row == q, pivot, pivots)
            inverse = 1.0 / pivot
            ratio = {t: column[q, t] * inverse for t in live}
            ratio[b] = jnp.where(row > q, ratio[b], 0.0)
            for later in range(q + 1, tile):
                entry = spread(column[later, b][q : q + 1])
                for t in live:
                    column[later, t] = column[later, t] - ratio[t] * entry
            line = spread(tiles[b][q : q + 1])
            for t in live:
                tiles[t] = tiles[t] - ratio[t] * line
        done.append((tiles[b] * (1.0 / jnp.sqrt(pivots)))[:, :k])
    return jnp.concatenate(done, axis=0)


def slots(cols):
    parity = lax.rem(lax.axis_index("col"), 2)
    return [2 * x + parity for x in range(cols // 2)] + [2 * x + 1 - parity for x in range(cols // 2)]


def slot_of(column, cols):
    other = lax.rem(column + lax.axis_index("col"), 2)
    return other * (cols // 2) + column // 2


def prepare_kernel(sizes, mask_hbm, stored_hbm, start_hbm, order_hbm, to_rows_ref, *refs):
    rows, cols, width = sizes
    to_cols, (piece_ref, picked_ref) = refs[:cols], refs[cols : cols + 2]
    mask_ref, stored_ref, start_ref, order_ref, arrived = refs[cols + 2 :]
    here_row, here_col = lax.axis_index("row"), lax.axis_index("col")
    columns = slots(cols)
    copies = [
        pltpu.make_async_copy(mask_hbm, mask_ref, arrived.at[cols]),
        pltpu.make_async_copy(start_hbm, start_ref, arrived.at[cols + 1]),
        pltpu.make_async_copy(order_hbm, order_ref, arrived.at[cols + 2]),
    ]
    lines = [
        pltpu.make_async_copy(
            stored_hbm.at[pl.ds(pl.multiple_of(columns[s] * width, width), width)], stored_ref.at[s], arrived.at[s]
        )
        for s in range(cols)
    ]
    for copy in copies + lines:
        copy.start()
    upper = (
        lax.broadcasted_iota(jnp.int32, (width, width), 0) < lax.broadcasted_iota(jnp.int32, (width, width), 1)
    ).astype(F32)
    node = lax.broadcasted_iota(jnp.int32, (width, width), 0)
    for copy in copies:
        copy.wait()
    picked = dot(start_ref[...], (node == order_ref[...]).astype(F32), ((1,), (0,)), HIGHEST)
    picked_ref[...] = picked
    ones = jnp.ones((8, rows * width), BF16)
    line_degrees = []
    for s in range(cols):
        lines[s].wait()
        row_block = here_row * cols + columns[s]
        line = []
        for i in range(rows):
            col_block = i * cols + here_col
            whole = jnp.where((mask_ref[columns[s], i] > 0) & (row_block < col_block), 1.0, 0.0)
            partly = jnp.where(row_block == col_block, 1.0, 0.0)
            keep = (whole + partly * upper).astype(BF16)
            line.append(stored_ref[s, :, i * width : (i + 1) * width] * keep)
            to_rows_ref[i, s * width : (s + 1) * width] = line[i]
        line_degrees.append(dot(ones, lanes(line), ((1,), (1,)))[0:1])
    for distance in range(cols):
        s = slot_of(lax.rem(here_col + distance, cols), cols)
        from_line = pl.ds(pl.multiple_of(s * width, width), width)
        for i in range(rows):
            to_cols[distance][:, i * width : (i + 1) * width] = to_rows_ref[i, from_line]
    degrees = [dot(ones[:, : cols * width], to_rows_ref[i], ((1,), (0,)))[0:1] for i in range(rows)]
    swapped = line_degrees[cols // 2 :] + line_degrees[: cols // 2]
    odd = lax.rem(here_col, 2) == 1
    for c in range(cols):
        s = c // 2 + (c % 2) * (cols // 2)
        degrees.append(jnp.where(odd, swapped[s], line_degrees[s]))
    k = picked.shape[0]
    extra = (piece_ref.shape[-2] - k) // 3
    if extra > rows + cols:
        degrees.append(jnp.zeros((extra - rows - cols, width), F32))
    left = jnp.concatenate(degrees, axis=0)
    planes = [picked.astype(BF16)]
    for _ in range(3):
        planes.append(left.astype(BF16))
        left = left - planes[-1].astype(F32)
    piece = jnp.concatenate(planes, axis=0)
    for i in range(rows):
        piece_ref[i] = piece


def product(vectors_of, parts, sizes):
    rows, cols, _ = sizes
    here_col = lax.axis_index("col")
    total = None
    for distance in range(cols):
        column = lax.rem(here_col + (cols - distance), cols)
        vectors = lanes([vectors_of(distance % 2, column // 2, i) for i in range(rows)])
        term = dot(vectors, parts[1 + distance][...], ((1,), (1,)))
        total = term if total is None else total + term
    for i in range(rows):
        vectors = lanes([vectors_of(s, x, i) for s in range(2) for x in range(cols // 2)])
        total = total + dot(vectors, parts[0][i], ((1,), (0,)))
    return total


def own_root(roots_ref):
    return roots_ref[lax.axis_index("col") // 2, pl.ds(lax.axis_index("row"), 1)]


def find_roots(sizes, k, all_ref, roots_ref):
    rows, cols, _ = sizes
    extra = (all_ref.shape[-2] - k) // 3

    def degrees(c, i):
        planes = [all_ref[c, i, k + n * extra : k + (n + 1) * extra].astype(F32) for n in range(3)]
        return (planes[0] + planes[1]) + planes[2]

    def summed(terms):
        total = terms[0]
        for term in terms[1:]:
            total = total + term
        return total

    sums = [[degrees(c, i) for i in range(rows)] for c in range(cols)]
    across = [summed([sums[c][i] for c in range(cols)]) for i in range(rows)]
    for c in range(cols):
        part = summed(sums[c])
        other = jnp.concatenate([across[i][rows + c : rows + c + 1] for i in range(rows)], axis=0)
        roots_ref[slot_of(c, cols)] = 1.0 / jnp.sqrt(part[:rows] + other)


def send(vectors, copies_ref):
    vectors = vectors.astype(BF16)
    for n in range(copies_ref.shape[0]):
        copies_ref[n] = vectors


def first_step_kernel(sizes, all_ref, picked_ref, *refs):
    rows, cols, _ = sizes
    parts, (copies_ref, own_ref, roots_ref, scratch) = refs[:-4], refs[-4:]
    k = own_ref.shape[0]
    half = cols // 2
    find_roots(sizes, k, all_ref, roots_ref)
    for c in range(cols):
        s = slot_of(c, cols)
        for i in range(rows):
            value = all_ref[c, i, :k].astype(F32) * roots_ref[s, i : i + 1]
            high = value.astype(BF16)
            scratch[s, i, :k] = high
            scratch[s, i, k:] = (value - high.astype(F32)).astype(BF16)
    total = product(lambda s, x, i: scratch[s * half + x, i], parts, sizes)
    root = own_root(roots_ref)
    image = picked_ref[...] + root * (total[:k] + total[k:])
    own_ref[...] = image
    send(root * image, copies_ref)


def next_image(sizes, same_ref, other_ref, before_ref, roots_ref, factor_ref, parts):
    half = sizes[1] // 2
    refs = (same_ref, other_ref)
    total = product(lambda s, x, i: refs[s][i * half + x], parts, sizes)
    image = before_ref[...] + own_root(roots_ref) * total
    return dot(factor_ref[...], image, ((1,), (0,)), HIGHEST)


def step_kernel(sizes, same_ref, other_ref, before_ref, roots_ref, factor_ref, *refs):
    parts, (copies_ref, own_ref) = refs[:-2], refs[-2:]
    image = next_image(sizes, same_ref, other_ref, before_ref, roots_ref, factor_ref, parts)
    own_ref[...] = image
    send(own_root(roots_ref) * image, copies_ref)


def last_step_kernel(sizes, same_ref, other_ref, before_ref, roots_ref, factor_ref, *refs):
    parts, (own_ref, gram_ref) = refs[:-2], refs[-2:]
    image = next_image(sizes, same_ref, other_ref, before_ref, roots_ref, factor_ref, parts)
    own_ref[...] = image
    gram = dot(image, image, ((1,), (1,)), HIGHEST)
    half = gram.shape[0] // 2
    gram = lanes([gram[:half], gram[half:]])
    for i in range(gram_ref.shape[0]):
        gram_ref[i] = gram


def congruent(factor, gram):
    half = dot(factor, gram, ((1,), (0,)), HIGHEST)
    return dot(half, factor, ((1,), (1,)), HIGHEST)


def first_factor_kernel(sizes, all_ref, factor_ref):
    rows, cols, _ = sizes
    k = factor_ref.shape[0]
    gram = jnp.zeros((k, k), F32)
    for c in range(cols):
        panel = lanes([all_ref[c, i, :k].astype(F32) for i in range(rows)])
        gram = gram + dot(panel, panel, ((1,), (1,)), HIGHEST)
    factor_ref[...] = inverse_factor(gram)


def factor_of(sizes, same_ref, other_ref, roots_ref, before_ref):
    rows, cols, _ = sizes
    half = cols // 2
    k = before_ref.shape[0]
    gram = jnp.zeros((k, k), F32)
    for s, ref in enumerate((same_ref, other_ref)):
        for x in range(half):
            panel = lanes([ref[i * half + x].astype(F32) / roots_ref[s * half + x, i : i + 1] for i in range(rows)])
            gram = gram + dot(panel, panel, ((1,), (1,)), HIGHEST)
    return inverse_factor(congruent(before_ref[...], gram))


def factor_kernel(sizes, same_ref, other_ref, roots_ref, before_ref, factor_ref):
    factor_ref[...] = factor_of(sizes, same_ref, other_ref, roots_ref, before_ref)


def last_factor_kernel(sizes, same_ref, other_ref, roots_ref, before_ref, image_ref, factor_ref, out_ref):
    factor = factor_of(sizes, same_ref, other_ref, roots_ref, before_ref)
    factor_ref[...] = factor
    out_ref[...] = dot(factor, image_ref[...], ((1,), (0,)), HIGHEST)


def finish_kernel(scale, grams_ref, factor_ref, image_ref, out_ref):
    packed = grams_ref[0]
    for c in range(1, grams_ref.shape[0]):
        packed = packed + grams_ref[c]
    k = factor_ref.shape[0]
    gram = jnp.concatenate([packed[:, :k], packed[:, k:]], axis=0)
    factor = inverse_factor(congruent(factor_ref[...], gram))
    out_ref[...] = scale * dot(factor, image_ref[...], ((1,), (0,)), HIGHEST)


def kernel_call(body, outs, *operands, scratch=(), space=pltpu.VMEM, limit=0):
    held = sum(math.prod(a.shape) * a.dtype.itemsize for a in (*operands, *outs))
    extra = sum(math.prod(s.shape) * 4 for s in scratch if hasattr(s, "shape"))
    spec = pl.BlockSpec(memory_space=pltpu.VMEM)
    single = len(outs) == 1
    return pl.pallas_call(
        body,
        out_shape=outs[0] if single else tuple(outs),
        in_specs=[pl.BlockSpec(memory_space=space)] * len(operands),
        out_specs=spec if single else (spec,) * len(outs),
        scratch_shapes=list(scratch),
        cost_estimate=pl.CostEstimate(flops=0, bytes_accessed=held, transcendentals=0),
        compiler_params=pltpu.CompilerParams(vmem_limit_bytes=limit or held + held // 4 + extra + (8 << 20)),
    )(*operands)


def gather_start(copies):
    return lax.all_gather(lax.all_to_all(copies, "row", 0, 0, tiled=True), "col", axis=0, tiled=False)


def gather_vectors(copies, rows, cols, factor):
    groups = [[r * cols + c for r in range(rows) for c in range(parity, cols, 2)] for parity in range(2)]
    same = lax.all_to_all(copies, ("row", "col"), 0, 0, tiled=True, axis_index_groups=groups)
    same, factor = lax.optimization_barrier((same, factor))
    return same, lax.ppermute(same, "col", [(c, c + 1 - 2 * (c % 2)) for c in range(cols)]), factor


def local(start_vectors, cluster_order, weights, block_mask):
    rows, cols = lax.axis_size("row"), lax.axis_size("col")
    k, width = start_vectors.shape
    sizes = (rows, cols, width)

    def bound(body):
        return lambda *refs: body(sizes, *refs)

    shape = jax.ShapeDtypeStruct
    extra = -(-(rows + cols) // 16) * 16
    to_rows, *to_cols, piece, picked = kernel_call(
        bound(prepare_kernel),
        [
            shape((rows, cols * width, width), BF16),
            *[shape((width, rows * width), BF16)] * cols,
            shape((rows, k + 3 * extra, width), BF16),
            shape((k, width), F32),
        ],
        block_mask[:, 0, :],
        weights[:, 0, :],
        start_vectors,
        cluster_order,
        scratch=[
            pltpu.SMEM((cols, rows), jnp.int32),
            pltpu.VMEM((cols, width, rows * width), BF16),
            pltpu.VMEM((k, width), F32),
            pltpu.VMEM((1, width), jnp.int32),
            pltpu.SemaphoreType.DMA((cols + 3,)),
        ],
        space=pltpu.HBM,
        limit=60 << 20,
    )
    everyone = gather_start(piece)
    parts = [lax.all_to_all(to_rows, "row", 0, 0, tiled=True), to_cols[0]]
    for distance in range(1, cols):
        parts.append(lax.ppermute(to_cols[distance], "col", [(c, (c + distance) % cols) for c in range(cols)]))
    copies, own_shape = shape((rows * cols // 2, k, width), BF16), shape((k, width), F32)
    factor_shape = shape((k, k), F32)
    factor = kernel_call(bound(first_factor_kernel), [factor_shape], everyone)
    everyone, factor = lax.optimization_barrier((everyone, factor))
    sent, own, roots = kernel_call(
        bound(first_step_kernel),
        [copies, own_shape, shape((cols, rows, width), F32)],
        everyone,
        picked,
        *parts,
        scratch=[pltpu.VMEM((cols, rows, 2 * k, width), BF16)],
    )
    for step in range(1, ITERS):
        same, other, factor = gather_vectors(sent, rows, cols, factor)
        if step < ITERS - 1:
            sent, own = kernel_call(
                bound(step_kernel), [copies, own_shape], same, other, own, roots, factor, *parts
            )
            factor = kernel_call(bound(factor_kernel), [factor_shape], same, other, roots, factor)
        else:
            own, gram = kernel_call(
                bound(last_step_kernel),
                [own_shape, shape((rows, k // 2, 2 * k), F32)],
                same,
                other,
                own,
                roots,
                factor,
                *parts,
            )
            factor, image = kernel_call(
                bound(last_factor_kernel), [factor_shape, own_shape], same, other, roots, factor, own
            )
    gram = lax.all_to_all(gram, "row", 0, 0, tiled=True).sum(axis=0)
    gram = lax.all_gather(gram, "col", axis=0, tiled=False)
    scale = math.sqrt(width * rows * cols)
    return kernel_call(lambda *refs: finish_kernel(scale, *refs), [own_shape], gram, factor, image)


def solution(mesh):
    placed = (
        P(None, ("row", "col")),
        P(("row", "col"), None),
        P("row", "col", None),
        P("row", "col", None),
    )
    return jax.shard_map(
        local, mesh=mesh, in_specs=placed, out_specs=P(None, ("row", "col")), check_vma=False
    )
```

time: 176 us -> 104 us (0.59)
  waiting for transfers between devices: 58.1 us -> 16.6 us
  Pallas kernels: 34.3 us -> 20.3 us
  between operations: 13.2 us -> 0.09 us
  local copies, waits for them, and re-layouts: 7.09 us -> 0.01 us
  blocking collectives: 50.4 us -> 53 us
    all_gather x3 -> x0, waiting for transfers between devices: 25.6 us -> none  [gather_all(): lax.all_gather(lax.all_to_all(copies, 'row', 0, 0, tiled=True), 'col', ax...]
    all_to_all x2, waiting for transfers between devices: 31.2 us -> 9.47 us  [the longest x1 7.11 us: gather_vectors(): lax.all_to_all(copies, ('row', 'col'), 0, 0, tiled=True, axis_index_group...]
    all_gather x0 -> x1, blocking collectives: none -> 17.3 us  [gather_start(): lax.all_gather(lax.all_to_all(copies, 'row', 0, 0, tiled=True), 'col', ax...]
    all_to_all x3 -> x2, blocking collectives: 45.2 us -> 30.5 us  [the longest x1 15.7 us: gather_start(): lax.all_to_all(copies, 'row', 0, 0, tiled=True)]
    pallas_call x8, Pallas kernels: 34.3 us -> 20.3 us  [kernel_call(): pl.pallas_call(body, out_shape=outs[0] if single else tuple(outs), in_spe...]
    unnamed x18 -> x6, local copies, waits for them, and re-layouts: 7.09 us -> 0.01 us
    all_to_all x1, waiting for transfers between devices: 0.56 us -> 4.02 us  [local(): gram = lax.all_to_all(gram, 'row', 0, 0, tiled=True).sum(axis=0)]
    ppermute x0 -> x5, waiting for transfers between devices: none -> 3.07 us  [the longest x2 3.07 us: gather_vectors(): lax.ppermute(same, 'col', [(c, c + 1 - 2 * (c % 2)) for c in range(cols)])]
  transfers between devices with their start and end apart: 6 -> 8, of which waited for: 6 -> 5; matrix products, arithmetic and copies ran while one was open for 0% -> 0% of each run, Pallas kernels for 13% -> 9%
where the time goes in v2:
time: 104 us
  blocking collectives  53 us (51%)
  Pallas kernels  20.3 us (20%)
  waiting for transfers between devices  16.6 us (16%)
  starting transfers between devices  13.6 us (13%)
    pallas_call x8, Pallas kernels, kernel_call(): pl.pallas_call(body, out_shape=outs[0] if single else tuple(outs), in_spe...  20.3 us
    all_gather x1, blocking collectives, gather_start(): lax.all_gather(lax.all_to_all(copies, 'row', 0, 0, tiled=True), 'col', ax...  17.3 us
    all_to_all x1, blocking collectives, gather_start(): lax.all_to_all(copies, 'row', 0, 0, tiled=True)  15.7 us
    all_to_all x1, blocking collectives, gather_vectors(): lax.all_to_all(copies, ('row', 'col'), 0, 0, tiled=True, axis_index_group...  14.8 us
    all_to_all x1, waiting for transfers between devices, gather_vectors(): lax.all_to_all(copies, ('row', 'col'), 0, 0, tiled=True, axis_index_group...  7.11 us
    all_gather x1, blocking collectives, local(): gram = lax.all_gather(gram, 'col', axis=0, tiled=False)  5.25 us
    all_to_all x1, waiting for transfers between devices, local(): gram = lax.all_to_all(gram, 'row', 0, 0, tiled=True).sum(axis=0)  4.02 us
    all_to_all x1, starting transfers between devices, local(): parts = [lax.all_to_all(to_rows, 'row', 0, 0, tiled=True), to_cols[0]]  3.69 us
  transfers between devices with their start and end apart: 8, of which 5 were waited for; matrix products, arithmetic and copies ran while one was open for 0% of the time, Pallas kernels for 9%

profile of v2, /device:TPU:0, one launch (start us, length us, event | category | flops | bytes accessed | tf_op | source)
XLA Modules:
  0.0 103.6 jit_solution(13334351993522550722)
XLA Ops:
  0.0 3.4 %shard_map.46 = (bf16[8,512,128]{2,1,0:T(8,128)(2,1)}, bf16[128,1024]{1,0:T(8,128)(2,1)}, bf16[128,1024]{1,0:T(8,128)(2,1)}, bf16[128,1024]{1,0:T(8,128)(2,1)}, ...) custom-call(s32[4,8]{1,0:T(4,128)} %bitcast.8, bf16[512,1024]{1,0:T(8,128)(2,1)} %bitcast.7, ...), custom_call_target="tpu_custom_call" | custom-call | bytes 3441280 | tf_op jit(solution)/shard_map/pallas_call | solution.py:282
  3.4 15.7 %all_to_all.25 = bf16[8,112,128]{2,1,0:T(8,128)(2,1)S(1)} all-to-all(bf16[8,112,128]{2,1,0:T(8,128)(2,1)} %get-tuple-element.27), channel_id=1, replica_groups=mesh['row'=8,'col'=4] {'row'}, dimensions={0} | all-to-all | bytes 458752 | tf_op jit(solution)/shard_map/all_to_all | solution.py:294
  19.1 0.0 copy-start.2
  19.1 3.7 %all-to-all-start.1 = ((bf16[8,512,128]{2,1,0:T(8,128)(2,1)}), bf16[8,512,128]{2,1,0:T(8,128)(2,1)S(1)}, u32[]{:S(2)}, u32[]{:S(2)}) async-start(bf16[8,512,128]{2,1,0:T(8,128)(2,1)} %get-tuple-element.30), calls=%async_computation.1 | async-start | bytes 2097152 | tf_op jit(solution)/shard_map/all_to_all | solution.py:337
  22.8 0.1 collective-permute-start
  22.9 1.6 %collective-permute-start.1 = (bf16[128,1024]{1,0:T(8,128)(2,1)}, bf16[128,1024]{1,0:T(8,128)(2,1)S(1)}, u32[]{:S(2)}, u32[]{:S(2)}) collective-permute-start(bf16[128,1024]{1,0:T(8,128)(2,1)} %get-tuple-element.33), channel_id=1, source_target_pairs={{0,2},{1,3},{2,0},{3,1},{4,6},{5,7},{6,4},{7,5},{8,10},{9,11},{10,... | collective-permute-start | bytes 786440 | tf_op jit(solution)/shard_map/ppermute | solution.py:339
  24.4 0.0 copy-done.2
  24.4 1.4 %collective-permute-start.2 = (bf16[128,1024]{1,0:T(8,128)(2,1)S(1)}, bf16[128,1024]{1,0:T(8,128)(2,1)S(1)}, u32[]{:S(2)}, u32[]{:S(2)}) collective-permute-start(bf16[128,1024]{1,0:T(8,128)(2,1)S(1)} %copy-done.2), channel_id=1, source_target_pairs={{0,3},{1,0},{2,1},{3,2},{4,7},{5,4},{6,5},{7,6},{8,11},{9,8},{10,9... | collective-permute-start | bytes 786440 | tf_op jit(solution)/shard_map/ppermute | solution.py:339
  25.8 17.3 %all-gather = bf16[32,112,128]{2,1,0:T(8,128)(2,1)S(1)} all-gather(bf16[8,112,128]{2,1,0:T(8,128)(2,1)S(1)} %all_to_all.25), channel_id=2, replica_groups=mesh['row'=8,'col'=4] {'col'}, dimensions={0}, use_global_device_ids=true | all-gather | bytes 1146880 | tf_op jit(solution)/shard_map/all_gather | solution.py:294
  43.1 2.8 %shard_map.47.refs_4_.refs_3_ = f32[64,64]{1,0:T(8,128)S(1)} custom-call(bf16[4,8,112,128]{3,2,1,0:T(8,128)(2,1)S(1)} %bitcast.4), custom_call_target="tpu_custom_call" | custom-call | bytes 933888 | tf_op jit(solution)/shard_map/pallas_call | solution.py:282
  45.9 0.0 collective-permute-done.refs_4_.refs_7_
  45.9 0.0 collective-permute-done.1.refs_5_.refs_8_
  45.9 0.0 collective-permute-done.2.refs_6_.refs_9_
  45.9 2.4 %all-to-all-done.1.refs_2_.refs_5_ = bf16[8,512,128]{2,1,0:T(8,128)(2,1)S(1)} async-done(((bf16[8,512,128]{2,1,0:T(8,128)(2,1)}), bf16[8,512,128]{2,1,0:T(8,128)(2,1)S(1)}, u32[]{:S(2)}, u32[]{:S(2)}) %all-to-all-start.1) | async-done | bytes 1048608 | tf_op jit(solution)/shard_map/all_to_all | solution.py:337
  48.3 0.0 copy-done
  48.3 0.0 copy-done.1
  48.3 1.0 shard_map.48
  49.3 14.8 %all_to_all.26.refs_0_ = bf16[16,64,128]{2,1,0:T(8,128)(2,1)S(1)} all-to-all(bf16[16,64,128]{2,1,0:T(8,128)(2,1)S(1)} %get-tuple-element.35), channel_id=1, replica_groups={{0,2,4,6,8,10,12,14,16,18,20,22,24,26,28,30},{1,3,5,7,9,11,13,15,17,19,..., dimensions={0} | all-to-all | bytes 524288 | tf_op jit(solution)/shard_map/all_to_all | solution.py:299
  64.1 0.0 collective-permute-start.3
  64.1 1.5 %collective-permute-done.3.refs_1_ = bf16[16,64,128]{2,1,0:T(8,128)(2,1)S(1)} collective-permute-done((bf16[16,64,128]{2,1,0:T(8,128)(2,1)S(1)}, bf16[16,64,128]{2,1,0:T(8,128)(2,1)S(1)}, u32[]{:S(2)}, u32[]{:S(2)}) %collective-permute-start.3) | collective-permute-done | bytes 262176 | tf_op jit(solution)/shard_map/ppermute | solution.py:301
  65.6 1.5 %shard_map.49 = (bf16[16,64,128]{2,1,0:T(8,128)(2,1)}, f32[64,128]{1,0:T(8,128)S(1)}) custom-call(bf16[16,64,128]{2,1,0:T(8,128)(2,1)S(1)} %all_to_all.26.refs_0_, bf16[16,64,128]{2,1,0:T(8,128)(2,1)S(1)} %collective-permute-done.3.refs_1_, f32[64,128]{1,0:T(8,128)S(1)} %get-tuple-element.38.refs_2_, f32[4,8,128]{2,1,0:T(8,128)S(1)} %get-tuple-element.39.refs_3_.refs_2_, ...), custom_call_target="tpu_custom_call" | custom-call | bytes 2981888 | tf_op jit(solution)/shard_map/pallas_call | solution.py:282
  67.1 3.5 %all-to-all-start.3 = ((bf16[16,64,128]{2,1,0:T(8,128)(2,1)}), bf16[16,64,128]{2,1,0:T(8,128)(2,1)S(1)}, u32[]{:S(2)}, u32[]{:S(2)}) async-start(bf16[16,64,128]{2,1,0:T(8,128)(2,1)} %get-tuple-element.41), calls=%async_computation.3 | async-start | bytes 524288 | tf_op jit(solution)/shard_map/all_to_all | solution.py:299
  70.7 3.3 %shard_map.50.refs_4_.refs_3_ = f32[64,64]{1,0:T(8,128)S(1)} custom-call(bf16[16,64,128]{2,1,0:T(8,128)(2,1)S(1)} %all_to_all.26.refs_0_, bf16[16,64,128]{2,1,0:T(8,128)(2,1)S(1)} %collective-permute-done.3.refs_1_, f32[4,8,128]{2,1,0:T(8,128)S(1)} %get-tuple-element.39.refs_3_.refs_2_, f32[64,64]{1,0:T(8,128)S(1)} %shard_map.47.refs_4_.refs_3_), custom_call_target="tpu_custom_call" | custom-call | bytes 573440 | tf_op jit(solution)/shard_map/pallas_call | solution.py:282
  74.0 7.1 %all-to-all-done.3.refs_0_ = bf16[16,64,128]{2,1,0:T(8,128)(2,1)S(1)} async-done(((bf16[16,64,128]{2,1,0:T(8,128)(2,1)}), bf16[16,64,128]{2,1,0:T(8,128)(2,1)S(1)}, u32[]{:S(2)}, u32[]{:S(2)}) %all-to-all-start.3) | async-done | bytes 262176 | tf_op jit(solution)/shard_map/all_to_all | solution.py:299
  81.1 0.0 collective-permute-start.4
  81.1 1.5 %collective-permute-done.4.refs_1_ = bf16[16,64,128]{2,1,0:T(8,128)(2,1)S(1)} collective-permute-done((bf16[16,64,128]{2,1,0:T(8,128)(2,1)S(1)}, bf16[16,64,128]{2,1,0:T(8,128)(2,1)S(1)}, u32[]{:S(2)}, u32[]{:S(2)}) %collective-permute-start.4) | collective-permute-done | bytes 262176 | tf_op jit(solution)/shard_map/ppermute | solution.py:301
  82.6 1.8 %shard_map.51 = (f32[64,128]{1,0:T(8,128)S(1)}, f32[8,32,128]{2,1,0:T(8,128)}) custom-call(bf16[16,64,128]{2,1,0:T(8,128)(2,1)S(1)} %all-to-all-done.3.refs_0_, bf16[16,64,128]{2,1,0:T(8,128)(2,1)S(1)} %collective-permute-done.4.refs_1_, f32[64,128]{1,0:T(8,128)S(1)} %get-tuple-element.43.refs_2_, f32[4,8,128]{2,1,0:T(8,128)S(1)} %get-tuple-element.39.refs_3_.refs_2_, ...), custom_call_target="tpu_custom_call" | custom-call | bytes 2850816 | tf_op jit(solution)/shard_map/pallas_call | solution.py:282
  84.4 3.4 %all-to-all-start.4 = ((f32[8,32,128]{2,1,0:T(8,128)}), f32[8,32,128]{2,1,0:T(8,128)S(1)}, u32[]{:S(2)}, u32[]{:S(2)}) async-start(f32[8,32,128]{2,1,0:T(8,128)} %get-tuple-element.45), calls=%async_computation.4 | async-start | bytes 262144 | tf_op jit(solution)/shard_map/all_to_all | solution.py:373
  87.8 3.5 %shard_map.52 = (f32[64,64]{1,0:T(8,128)S(1)}, f32[64,128]{1,0:T(8,128)S(1)}) custom-call(bf16[16,64,128]{2,1,0:T(8,128)(2,1)S(1)} %all-to-all-done.3.refs_0_, bf16[16,64,128]{2,1,0:T(8,128)(2,1)S(1)} %collective-permute-done.4.refs_1_, f32[4,8,128]{2,1,0:T(8,128)S(1)} %get-tuple-element.39.refs_3_.refs_2_, f32[64,64]{1,0:T(8,128)S(1)} %shard_map.50.refs_4_.refs_3_, ...), custom_call_target="tpu_custom_call" | custom-call | bytes 638976 | tf_op jit(solution)/shard_map/pallas_call | solution.py:282
  91.2 4.0 %all-to-all-done.4 = f32[8,32,128]{2,1,0:T(8,128)S(1)} async-done(((f32[8,32,128]{2,1,0:T(8,128)}), f32[8,32,128]{2,1,0:T(8,128)S(1)}, u32[]{:S(2)}, u32[]{:S(2)}) %all-to-all-start.4) | async-done | bytes 131104 | tf_op jit(solution)/shard_map/all_to_all | solution.py:373
  95.3 5.2 %all-gather.1 = f32[128,128]{1,0:T(8,128)S(1)} all-gather(f32[32,128]{1,0:T(8,128)S(1)} %reduce_sum.9), channel_id=3, replica_groups=mesh['row'=8,'col'=4] {'col'}, dimensions={0}, use_global_device_ids=true | all-gather | bytes 81920 | tf_op jit(solution)/shard_map/all_gather | solution.py:374
  100.5 3.1 %shard_map.53 = f32[64,128]{1,0:T(8,128)} custom-call(f32[4,32,128]{2,1,0:T(8,128)S(1)} %bitcast.6, f32[64,64]{1,0:T(8,128)S(1)} %get-tuple-element.47.refs_1_, f32[64,128]{1,0:T(8,128)S(1)} %get-tuple-element.48.refs_2_), custom_call_target="tpu_custom_call" | custom-call | bytes 147456 | tf_op jit(solution)/shard_map/pallas_call | solution.py:282
  (3 shorter events, 0.0 us)
Async XLA Ops:
  19.1 5.3 %copy-start.2 = (bf16[128,1024]{1,0:T(8,128)(2,1)S(1)}, bf16[128,1024]{1,0:T(8,128)(2,1)}, u32[]{:S(2)}) copy-start(bf16[128,1024]{1,0:T(8,128)(2,1)} %get-tuple-element.34) | copy-start | bytes 786436
  19.1 29.2 %all-to-all-start.1 = ((bf16[8,512,128]{2,1,0:T(8,128)(2,1)}), bf16[8,512,128]{2,1,0:T(8,128)(2,1)S(1)}, u32[]{:S(2)}, u32[]{:S(2)}) async-start(bf16[8,512,128]{2,1,0:T(8,128)(2,1)} %get-tuple-element.30), calls=%async_computation.1 | async-start | bytes 2097152 | tf_op jit(solution)/shard_map/all_to_all | solution.py:337
  22.8 23.1 %collective-permute-start = (bf16[128,1024]{1,0:T(8,128)(2,1)}, bf16[128,1024]{1,0:T(8,128)(2,1)S(1)}, u32[]{:S(2)}, u32[]{:S(2)}) collective-permute-start(bf16[128,1024]{1,0:T(8,128)(2,1)} %get-tuple-element.32), channel_id=1, source_target_pairs={{0,1},{1,2},{2,3},{3,0},{4,5},{5,6},{6,7},{7,4},{8,9},{9,10},{10,1... | collective-permute-start | bytes 786440 | tf_op jit(solution)/shard_map/ppermute | solution.py:339
  22.9 23.0 %collective-permute-start.1 = (bf16[128,1024]{1,0:T(8,128)(2,1)}, bf16[128,1024]{1,0:T(8,128)(2,1)S(1)}, u32[]{:S(2)}, u32[]{:S(2)}) collective-permute-start(bf16[128,1024]{1,0:T(8,128)(2,1)} %get-tuple-element.33), channel_id=1, source_target_pairs={{0,2},{1,3},{2,0},{3,1},{4,6},{5,7},{6,4},{7,5},{8,10},{9,11},{10,... | collective-permute-start | bytes 786440 | tf_op jit(solution)/shard_map/ppermute | solution.py:339
  24.4 21.5 %collective-permute-start.2 = (bf16[128,1024]{1,0:T(8,128)(2,1)S(1)}, bf16[128,1024]{1,0:T(8,128)(2,1)S(1)}, u32[]{:S(2)}, u32[]{:S(2)}) collective-permute-start(bf16[128,1024]{1,0:T(8,128)(2,1)S(1)} %copy-done.2), channel_id=1, source_target_pairs={{0,3},{1,0},{2,1},{3,2},{4,7},{5,4},{6,5},{7,6},{8,11},{9,8},{10,9... | collective-permute-start | bytes 786440 | tf_op jit(solution)/shard_map/ppermute | solution.py:339
  43.1 5.2 %copy-start = (bf16[128,1024]{1,0:T(8,128)(2,1)S(1)}, bf16[128,1024]{1,0:T(8,128)(2,1)}, u32[]{:S(2)}) copy-start(bf16[128,1024]{1,0:T(8,128)(2,1)} %get-tuple-element.31.refs_3_.refs_6_) | copy-start | bytes 786436
  43.1 5.2 %copy-start.1 = (f32[64,128]{1,0:T(8,128)S(1)}, f32[64,128]{1,0:T(8,128)}, u32[]{:S(2)}) copy-start(f32[64,128]{1,0:T(8,128)} %get-tuple-element.29.refs_1_) | copy-start | bytes 98308
  64.1 1.5 %collective-permute-start.3 = (bf16[16,64,128]{2,1,0:T(8,128)(2,1)S(1)}, bf16[16,64,128]{2,1,0:T(8,128)(2,1)S(1)}, u32[]{:S(2)}, u32[]{:S(2)}) collective-permute-start(bf16[16,64,128]{2,1,0:T(8,128)(2,1)S(1)} %all_to_all.26.refs_0_), channel_id=1, source_target_pairs={{0,1},{1,0},{2,3},{3,2},{4,5},{5,4},{6,7},{7,6},{8,9},{9,8},{10,11... | collective-permute-start | bytes 786440 | tf_op jit(solution)/shard_map/ppermute | solution.py:301
  67.1 13.9 %all-to-all-start.3 = ((bf16[16,64,128]{2,1,0:T(8,128)(2,1)}), bf16[16,64,128]{2,1,0:T(8,128)(2,1)S(1)}, u32[]{:S(2)}, u32[]{:S(2)}) async-start(bf16[16,64,128]{2,1,0:T(8,128)(2,1)} %get-tuple-element.41), calls=%async_computation.3 | async-start | bytes 524288 | tf_op jit(solution)/shard_map/all_to_all | solution.py:299
  81.1 1.5 %collective-permute-start.4 = (bf16[16,64,128]{2,1,0:T(8,128)(2,1)S(1)}, bf16[16,64,128]{2,1,0:T(8,128)(2,1)S(1)}, u32[]{:S(2)}, u32[]{:S(2)}) collective-permute-start(bf16[16,64,128]{2,1,0:T(8,128)(2,1)S(1)} %all-to-all-done.3.refs_0_), channel_id=1, source_target_pairs={{0,1},{1,0},{2,3},{3,2},{4,5},{5,4},{6,7},{7,6},{8,9},{9,8},{10,11... | collective-permute-start | bytes 786440 | tf_op jit(solution)/shard_map/ppermute | solution.py:301
  84.4 10.9 %all-to-all-start.4 = ((f32[8,32,128]{2,1,0:T(8,128)}), f32[8,32,128]{2,1,0:T(8,128)S(1)}, u32[]{:S(2)}, u32[]{:S(2)}) async-start(f32[8,32,128]{2,1,0:T(8,128)} %get-tuple-element.45), calls=%async_computation.4 | async-start | bytes 262144 | tf_op jit(solution)/shard_map/all_to_all | solution.py:373

commit v3 on v2

--- a/solution.py
+++ b/solution.py
@@ -220,11 +220,26 @@
     parts, (own_ref, gram_ref) = refs[:-2], refs[-2:]
     image = next_image(sizes, same_ref, other_ref, before_ref, roots_ref, factor_ref, parts)
     own_ref[...] = image
-    gram = dot(image, image, ((1,), (1,)), HIGHEST)
+    packed = pack_gram(dot(image, image, ((1,), (1,)), HIGHEST))
+    for n in range(gram_ref.shape[0]):
+        gram_ref[n] = packed
+
+
+def pack_gram(gram):
     half = gram.shape[0] // 2
-    gram = lanes([gram[:half], gram[half:]])
-    for i in range(gram_ref.shape[0]):
-        gram_ref[i] = gram
+    blocks = [gram[:half, :half], gram[half:, :half], gram[half:, half:]]
+    tile = half // 4
+    return jnp.concatenate([lanes([b[n * tile : (n + 1) * tile] for n in range(4)]) for b in blocks], axis=0)
+
+
+def unpack_gram(packed):
+    tile, half = packed.shape[0] // 3, packed.shape[1] // 4
+    upper, cross, lower = [
+        jnp.concatenate([packed[b * tile : (b + 1) * tile, n * half : (n + 1) * half] for n in range(4)], axis=0)
+        for b in range(3)
+    ]
+    across = lax.transpose(cross, (1, 0))
+    return jnp.concatenate([lanes([upper, across]), lanes([cross, lower])], axis=0)
 
 
 def congruent(factor, gram):
@@ -264,12 +279,8 @@
     out_ref[...] = dot(factor, image_ref[...], ((1,), (0,)), HIGHEST)
 
 
-def finish_kernel(scale, grams_ref, factor_ref, image_ref, out_ref):
-    packed = grams_ref[0]
-    for c in range(1, grams_ref.shape[0]):
-        packed = packed + grams_ref[c]
-    k = factor_ref.shape[0]
-    gram = jnp.concatenate([packed[:, :k], packed[:, k:]], axis=0)
+def finish_kernel(scale, same_ref, other_ref, factor_ref, image_ref, out_ref):
+    gram = unpack_gram(same_ref[...] + other_ref[...])
     factor = inverse_factor(congruent(factor_ref[...], gram))
     out_ref[...] = scale * dot(factor, image_ref[...], ((1,), (0,)), HIGHEST)
 
@@ -294,11 +305,18 @@
     return lax.all_gather(lax.all_to_all(copies, "row", 0, 0, tiled=True), "col", axis=0, tiled=False)
 
 
+def parities(rows, cols):
+    return [[r * cols + c for r in range(rows) for c in range(parity, cols, 2)] for parity in range(2)]
+
+
+def swap(cols):
+    return [(c, c + 1 - 2 * (c % 2)) for c in range(cols)]
+
+
 def gather_vectors(copies, rows, cols, factor):
-    groups = [[r * cols + c for r in range(rows) for c in range(parity, cols, 2)] for parity in range(2)]
-    same = lax.all_to_all(copies, ("row", "col"), 0, 0, tiled=True, axis_index_groups=groups)
+    same = lax.all_to_all(copies, ("row", "col"), 0, 0, tiled=True, axis_index_groups=parities(rows, cols))
     same, factor = lax.optimization_barrier((same, factor))
-    return same, lax.ppermute(same, "col", [(c, c + 1 - 2 * (c % 2)) for c in range(cols)]), factor
+    return same, lax.ppermute(same, "col", swap(cols)), factor
 
 
 def local(start_vectors, cluster_order, weights, block_mask):
@@ -359,7 +377,7 @@
         else:
             own, gram = kernel_call(
                 bound(last_step_kernel),
-                [own_shape, shape((rows, k // 2, 2 * k), F32)],
+                [own_shape, shape((rows * cols // 2, 3 * k // 8, 2 * k), F32)],
                 same,
                 other,
                 own,
@@ -370,10 +388,12 @@
             factor, image = kernel_call(
                 bound(last_factor_kernel), [factor_shape, own_shape], same, other, roots, factor, own
             )
-    gram = lax.all_to_all(gram, "row", 0, 0, tiled=True).sum(axis=0)
-    gram = lax.all_gather(gram, "col", axis=0, tiled=False)
+    gram = lax.all_to_all(gram, ("row", "col"), 0, 0, tiled=True, axis_index_groups=parities(rows, cols))
+    gram, factor = lax.optimization_barrier((gram, factor))
+    same = gram.sum(axis=0)
+    other = lax.ppermute(same, "col", swap(cols))
     scale = math.sqrt(width * rows * cols)
-    return kernel_call(lambda *refs: finish_kernel(scale, *refs), [own_shape], gram, factor, image)
+    return kernel_call(lambda *refs: finish_kernel(scale, *refs), [own_shape], same, other, factor, image)
 
 
 def solution(mesh):

time: 104 us -> 102 us (0.981)
  blocking collectives: 53 us -> 47.8 us
  waiting for transfers between devices: 16.6 us -> 18.9 us
    all_gather x1 -> x0, blocking collectives: 5.25 us -> none  [local(): gram = lax.all_gather(gram, 'col', axis=0, tiled=False)]
    all_to_all x1, waiting for transfers between devices: 4.02 us -> 5.23 us  [local(): lax.all_to_all(gram, ('row', 'col'), 0, 0, tiled=True, axis_index_groups=...]
    ppermute x2 -> x3, waiting for transfers between devices: 3.07 us -> 4.23 us  [the longest x2 3.07 us: gather_vectors(): return (same, lax.ppermute(same, 'col', swap(cols)), factor)]
  transfers between devices with their start and end apart: 8 -> 9, of which waited for: 5 -> 6; matrix products, arithmetic and copies ran while one was open for 0% -> 0% of each run, Pallas kernels for 9% -> 9%
where the time goes in v3:
time: 102 us; the launch traced here: 101 us
  blocking collectives  47.8 us (47%)
  Pallas kernels  20.4 us (20%)
  waiting for transfers between devices  18.9 us (19%)
  starting transfers between devices  14 us (14%)
    pallas_call x8, Pallas kernels, kernel_call(): pl.pallas_call(body, out_shape=outs[0] if single else tuple(outs), in_spe...  20.4 us
    all_gather x1, blocking collectives, gather_start(): lax.all_gather(lax.all_to_all(copies, 'row', 0, 0, tiled=True), 'col', ax...  17.3 us
    all_to_all x1, blocking collectives, gather_start(): lax.all_to_all(copies, 'row', 0, 0, tiled=True)  15.7 us
    all_to_all x1, blocking collectives, gather_vectors(): lax.all_to_all(copies, ('row', 'col'), 0, 0, tiled=True, axis_index_group...  14.8 us
    all_to_all x1, waiting for transfers between devices, gather_vectors(): lax.all_to_all(copies, ('row', 'col'), 0, 0, tiled=True, axis_index_group...  7.11 us
    all_to_all x1, waiting for transfers between devices, local(): lax.all_to_all(gram, ('row', 'col'), 0, 0, tiled=True, axis_index_groups=...  5.23 us
    all_to_all x1, starting transfers between devices, local(): lax.all_to_all(gram, ('row', 'col'), 0, 0, tiled=True, axis_index_groups=...  3.7 us
    all_to_all x1, starting transfers between devices, local(): parts = [lax.all_to_all(to_rows, 'row', 0, 0, tiled=True), to_cols[0]]  3.69 us
  transfers between devices with their start and end apart: 9, of which 6 were waited for; matrix products, arithmetic and copies ran while one was open for 0% of the time, Pallas kernels for 9%

profile of v3, /device:TPU:0, one launch (start us, length us, event | category | flops | bytes accessed | tf_op | source)
XLA Modules:
  0.0 101.3 jit_solution(7330549128095575509)
XLA Ops:
  0.0 3.4 %shard_map.46 = (bf16[8,512,128]{2,1,0:T(8,128)(2,1)}, bf16[128,1024]{1,0:T(8,128)(2,1)}, bf16[128,1024]{1,0:T(8,128)(2,1)}, bf16[128,1024]{1,0:T(8,128)(2,1)}, ...) custom-call(s32[4,8]{1,0:T(4,128)} %bitcast.6, bf16[512,1024]{1,0:T(8,128)(2,1)} %bitcast.5, ...), custom_call_target="tpu_custom_call" | custom-call | bytes 3441280 | tf_op jit(solution)/shard_map/pallas_call | solution.py:293
  3.4 15.7 %all_to_all.25 = bf16[8,112,128]{2,1,0:T(8,128)(2,1)S(1)} all-to-all(bf16[8,112,128]{2,1,0:T(8,128)(2,1)} %get-tuple-element.29), channel_id=1, replica_groups=mesh['row'=8,'col'=4] {'row'}, dimensions={0} | all-to-all | bytes 458752 | tf_op jit(solution)/shard_map/all_to_all | solution.py:305
  19.1 3.7 %all-to-all-start.1 = ((bf16[8,512,128]{2,1,0:T(8,128)(2,1)}), bf16[8,512,128]{2,1,0:T(8,128)(2,1)S(1)}, u32[]{:S(2)}, u32[]{:S(2)}) async-start(bf16[8,512,128]{2,1,0:T(8,128)(2,1)} %get-tuple-element.32), calls=%async_computation.1 | async-start | bytes 2097152 | tf_op jit(solution)/shard_map/all_to_all | solution.py:355
  22.8 0.1 collective-permute-start
  22.9 1.6 %collective-permute-start.1 = (bf16[128,1024]{1,0:T(8,128)(2,1)}, bf16[128,1024]{1,0:T(8,128)(2,1)S(1)}, u32[]{:S(2)}, u32[]{:S(2)}) collective-permute-start(bf16[128,1024]{1,0:T(8,128)(2,1)} %get-tuple-element.35), channel_id=1, source_target_pairs={{0,2},{1,3},{2,0},{3,1},{4,6},{5,7},{6,4},{7,5},{8,10},{9,11},{10,... | collective-permute-start | bytes 786440 | tf_op jit(solution)/shard_map/ppermute | solution.py:357
  24.4 0.0 copy-done.2
  24.4 1.4 %collective-permute-start.2 = (bf16[128,1024]{1,0:T(8,128)(2,1)S(1)}, bf16[128,1024]{1,0:T(8,128)(2,1)S(1)}, u32[]{:S(2)}, u32[]{:S(2)}) collective-permute-start(bf16[128,1024]{1,0:T(8,128)(2,1)S(1)} %copy-done.2), channel_id=1, source_target_pairs={{0,3},{1,0},{2,1},{3,2},{4,7},{5,4},{6,5},{7,6},{8,11},{9,8},{10,9... | collective-permute-start | bytes 786440 | tf_op jit(solution)/shard_map/ppermute | solution.py:357
  25.8 17.3 %all-gather = bf16[32,112,128]{2,1,0:T(8,128)(2,1)S(1)} all-gather(bf16[8,112,128]{2,1,0:T(8,128)(2,1)S(1)} %all_to_all.25), channel_id=2, replica_groups=mesh['row'=8,'col'=4] {'col'}, dimensions={0}, use_global_device_ids=true | all-gather | bytes 1146880 | tf_op jit(solution)/shard_map/all_gather | solution.py:305
  43.1 2.8 %shard_map.47.refs_4_.refs_3_ = f32[64,64]{1,0:T(8,128)S(1)} custom-call(bf16[4,8,112,128]{3,2,1,0:T(8,128)(2,1)S(1)} %bitcast.3), custom_call_target="tpu_custom_call" | custom-call | bytes 933888 | tf_op jit(solution)/shard_map/pallas_call | solution.py:293
  45.9 0.0 collective-permute-done.refs_4_.refs_7_
  45.9 0.0 collective-permute-done.1.refs_5_.refs_8_
  45.9 0.0 collective-permute-done.2.refs_6_.refs_9_
  45.9 2.4 %all-to-all-done.1.refs_2_.refs_5_ = bf16[8,512,128]{2,1,0:T(8,128)(2,1)S(1)} async-done(((bf16[8,512,128]{2,1,0:T(8,128)(2,1)}), bf16[8,512,128]{2,1,0:T(8,128)(2,1)S(1)}, u32[]{:S(2)}, u32[]{:S(2)}) %all-to-all-start.1) | async-done | bytes 1048608 | tf_op jit(solution)/shard_map/all_to_all | solution.py:355
  48.3 0.0 copy-done
  48.3 0.0 copy-done.1
  48.3 1.0 shard_map.48
  49.3 14.8 %all_to_all.26.refs_0_ = bf16[16,64,128]{2,1,0:T(8,128)(2,1)S(1)} all-to-all(bf16[16,64,128]{2,1,0:T(8,128)(2,1)S(1)} %get-tuple-element.37), channel_id=1, replica_groups={{0,2,4,6,8,10,12,14,16,18,20,22,24,26,28,30},{1,3,5,7,9,11,13,15,17,19,..., dimensions={0} | all-to-all | bytes 524288 | tf_op jit(solution)/shard_map/all_to_all | solution.py:317
  64.1 0.0 collective-permute-start.3
  64.1 1.5 %collective-permute-done.3.refs_1_ = bf16[16,64,128]{2,1,0:T(8,128)(2,1)S(1)} collective-permute-done((bf16[16,64,128]{2,1,0:T(8,128)(2,1)S(1)}, bf16[16,64,128]{2,1,0:T(8,128)(2,1)S(1)}, u32[]{:S(2)}, u32[]{:S(2)}) %collective-permute-start.3) | collective-permute-done | bytes 262176 | tf_op jit(solution)/shard_map/ppermute | solution.py:319
  65.6 1.5 %shard_map.49 = (bf16[16,64,128]{2,1,0:T(8,128)(2,1)}, f32[64,128]{1,0:T(8,128)S(1)}) custom-call(bf16[16,64,128]{2,1,0:T(8,128)(2,1)S(1)} %all_to_all.26.refs_0_, bf16[16,64,128]{2,1,0:T(8,128)(2,1)S(1)} %collective-permute-done.3.refs_1_, f32[64,128]{1,0:T(8,128)S(1)} %get-tuple-element.40.refs_2_, f32[4,8,128]{2,1,0:T(8,128)S(1)} %get-tuple-element.41.refs_3_.refs_2_, ...), custom_call_target="tpu_custom_call" | custom-call | bytes 2981888 | tf_op jit(solution)/shard_map/pallas_call | solution.py:293
  67.1 3.5 %all-to-all-start.3 = ((bf16[16,64,128]{2,1,0:T(8,128)(2,1)}), bf16[16,64,128]{2,1,0:T(8,128)(2,1)S(1)}, u32[]{:S(2)}, u32[]{:S(2)}) async-start(bf16[16,64,128]{2,1,0:T(8,128)(2,1)} %get-tuple-element.43), calls=%async_computation.3 | async-start | bytes 524288 | tf_op jit(solution)/shard_map/all_to_all | solution.py:317
  70.7 3.3 %shard_map.50.refs_4_.refs_3_ = f32[64,64]{1,0:T(8,128)S(1)} custom-call(bf16[16,64,128]{2,1,0:T(8,128)(2,1)S(1)} %all_to_all.26.refs_0_, bf16[16,64,128]{2,1,0:T(8,128)(2,1)S(1)} %collective-permute-done.3.refs_1_, f32[4,8,128]{2,1,0:T(8,128)S(1)} %get-tuple-element.41.refs_3_.refs_2_, f32[64,64]{1,0:T(8,128)S(1)} %shard_map.47.refs_4_.refs_3_), custom_call_target="tpu_custom_call" | custom-call | bytes 573440 | tf_op jit(solution)/shard_map/pallas_call | solution.py:293
  73.9 7.1 %all-to-all-done.3.refs_0_ = bf16[16,64,128]{2,1,0:T(8,128)(2,1)S(1)} async-done(((bf16[16,64,128]{2,1,0:T(8,128)(2,1)}), bf16[16,64,128]{2,1,0:T(8,128)(2,1)S(1)}, u32[]{:S(2)}, u32[]{:S(2)}) %all-to-all-start.3) | async-done | bytes 262176 | tf_op jit(solution)/shard_map/all_to_all | solution.py:317
  81.1 0.0 collective-permute-start.4
  81.1 1.5 %collective-permute-done.4.refs_1_ = bf16[16,64,128]{2,1,0:T(8,128)(2,1)S(1)} collective-permute-done((bf16[16,64,128]{2,1,0:T(8,128)(2,1)S(1)}, bf16[16,64,128]{2,1,0:T(8,128)(2,1)S(1)}, u32[]{:S(2)}, u32[]{:S(2)}) %collective-permute-start.4) | collective-permute-done | bytes 262176 | tf_op jit(solution)/shard_map/ppermute | solution.py:319
  82.6 1.8 %shard_map.51 = (f32[64,128]{1,0:T(8,128)S(1)}, f32[16,24,128]{2,1,0:T(8,128)}) custom-call(bf16[16,64,128]{2,1,0:T(8,128)(2,1)S(1)} %all-to-all-done.3.refs_0_, bf16[16,64,128]{2,1,0:T(8,128)(2,1)S(1)} %collective-permute-done.4.refs_1_, f32[64,128]{1,0:T(8,128)S(1)} %get-tuple-element.45.refs_2_, f32[4,8,128]{2,1,0:T(8,128)S(1)} %get-tuple-element.41.refs_3_.refs_2_, ...), custom_call_target="tpu_custom_call" | custom-call | bytes 2916352 | tf_op jit(solution)/shard_map/pallas_call | solution.py:293
  84.4 3.7 %all-to-all-start.4 = ((f32[16,24,128]{2,1,0:T(8,128)}), f32[16,24,128]{2,1,0:T(8,128)S(1)}, u32[]{:S(2)}, u32[]{:S(2)}) async-start(f32[16,24,128]{2,1,0:T(8,128)} %get-tuple-element.47), calls=%async_computation.4 | async-start | bytes 393216 | tf_op jit(solution)/shard_map/all_to_all | solution.py:391
  88.1 3.5 %shard_map.52 = (f32[64,64]{1,0:T(8,128)S(1)}, f32[64,128]{1,0:T(8,128)S(1)}) custom-call(bf16[16,64,128]{2,1,0:T(8,128)(2,1)S(1)} %all-to-all-done.3.refs_0_, bf16[16,64,128]{2,1,0:T(8,128)(2,1)S(1)} %collective-permute-done.4.refs_1_, f32[4,8,128]{2,1,0:T(8,128)S(1)} %get-tuple-element.41.refs_3_.refs_2_, f32[64,64]{1,0:T(8,128)S(1)} %shard_map.50.refs_4_.refs_3_, ...), custom_call_target="tpu_custom_call" | custom-call | bytes 638976 | tf_op jit(solution)/shard_map/pallas_call | solution.py:293
  91.6 5.2 %all-to-all-done.4 = f32[16,24,128]{2,1,0:T(8,128)S(1)} async-done(((f32[16,24,128]{2,1,0:T(8,128)}), f32[16,24,128]{2,1,0:T(8,128)S(1)}, u32[]{:S(2)}, u32[]{:S(2)}) %all-to-all-start.4) | async-done | bytes 196640 | tf_op jit(solution)/shard_map/all_to_all | solution.py:391
  96.8 0.1 collective-permute-start.5
  96.9 1.2 %collective-permute-done.5.refs_1_ = f32[24,128]{1,0:T(8,128)S(1)} collective-permute-done((f32[24,128]{1,0:T(8,128)S(1)}, f32[24,128]{1,0:T(8,128)S(1)}, u32[]{:S(2)}, u32[]{:S(2)}) %collective-permute-start.5) | collective-permute-done | bytes 12320 | tf_op jit(solution)/shard_map/ppermute | solution.py:394
  98.1 3.2 %shard_map.53 = f32[64,128]{1,0:T(8,128)} custom-call(f32[24,128]{1,0:T(8,128)S(1)} %reduce_sum.9.refs_0_, f32[24,128]{1,0:T(8,128)S(1)} %collective-permute-done.5.refs_1_, f32[64,64]{1,0:T(8,128)S(1)} %get-tuple-element.51.refs_2_, f32[64,128]{1,0:T(8,128)S(1)} %get-tuple-element.52.refs_3_), custom_call_target="tpu_custom_call" | custom-call | bytes 106496 | tf_op jit(solution)/shard_map/pallas_call | solution.py:293
  (4 shorter events, 0.0 us)
Async XLA Ops:
  19.1 5.3 %copy-start.2 = (bf16[128,1024]{1,0:T(8,128)(2,1)S(1)}, bf16[128,1024]{1,0:T(8,128)(2,1)}, u32[]{:S(2)}) copy-start(bf16[128,1024]{1,0:T(8,128)(2,1)} %get-tuple-element.36) | copy-start | bytes 786436
  19.1 29.2 %all-to-all-start.1 = ((bf16[8,512,128]{2,1,0:T(8,128)(2,1)}), bf16[8,512,128]{2,1,0:T(8,128)(2,1)S(1)}, u32[]{:S(2)}, u32[]{:S(2)}) async-start(bf16[8,512,128]{2,1,0:T(8,128)(2,1)} %get-tuple-element.32), calls=%async_computation.1 | async-start | bytes 2097152 | tf_op jit(solution)/shard_map/all_to_all | solution.py:355
  22.8 23.1 %collective-permute-start = (bf16[128,1024]{1,0:T(8,128)(2,1)}, bf16[128,1024]{1,0:T(8,128)(2,1)S(1)}, u32[]{:S(2)}, u32[]{:S(2)}) collective-permute-start(bf16[128,1024]{1,0:T(8,128)(2,1)} %get-tuple-element.34), channel_id=1, source_target_pairs={{0,1},{1,2},{2,3},{3,0},{4,5},{5,6},{6,7},{7,4},{8,9},{9,10},{10,1... | collective-permute-start | bytes 786440 | tf_op jit(solution)/shard_map/ppermute | solution.py:357
  22.9 23.0 %collective-permute-start.1 = (bf16[128,1024]{1,0:T(8,128)(2,1)}, bf16[128,1024]{1,0:T(8,128)(2,1)S(1)}, u32[]{:S(2)}, u32[]{:S(2)}) collective-permute-start(bf16[128,1024]{1,0:T(8,128)(2,1)} %get-tuple-element.35), channel_id=1, source_target_pairs={{0,2},{1,3},{2,0},{3,1},{4,6},{5,7},{6,4},{7,5},{8,10},{9,11},{10,... | collective-permute-start | bytes 786440 | tf_op jit(solution)/shard_map/ppermute | solution.py:357
  24.4 21.5 %collective-permute-start.2 = (bf16[128,1024]{1,0:T(8,128)(2,1)S(1)}, bf16[128,1024]{1,0:T(8,128)(2,1)S(1)}, u32[]{:S(2)}, u32[]{:S(2)}) collective-permute-start(bf16[128,1024]{1,0:T(8,128)(2,1)S(1)} %copy-done.2), channel_id=1, source_target_pairs={{0,3},{1,0},{2,1},{3,2},{4,7},{5,4},{6,5},{7,6},{8,11},{9,8},{10,9... | collective-permute-start | bytes 786440 | tf_op jit(solution)/shard_map/ppermute | solution.py:357
  43.1 5.2 %copy-start = (bf16[128,1024]{1,0:T(8,128)(2,1)S(1)}, bf16[128,1024]{1,0:T(8,128)(2,1)}, u32[]{:S(2)}) copy-start(bf16[128,1024]{1,0:T(8,128)(2,1)} %get-tuple-element.33.refs_3_.refs_6_) | copy-start | bytes 786436
  43.1 5.2 %copy-start.1 = (f32[64,128]{1,0:T(8,128)S(1)}, f32[64,128]{1,0:T(8,128)}, u32[]{:S(2)}) copy-start(f32[64,128]{1,0:T(8,128)} %get-tuple-element.31.refs_1_) | copy-start | bytes 98308
  64.1 1.5 %collective-permute-start.3 = (bf16[16,64,128]{2,1,0:T(8,128)(2,1)S(1)}, bf16[16,64,128]{2,1,0:T(8,128)(2,1)S(1)}, u32[]{:S(2)}, u32[]{:S(2)}) collective-permute-start(bf16[16,64,128]{2,1,0:T(8,128)(2,1)S(1)} %all_to_all.26.refs_0_), channel_id=1, source_target_pairs={{0,1},{1,0},{2,3},{3,2},{4,5},{5,4},{6,7},{7,6},{8,9},{9,8},{10,11... | collective-permute-start | bytes 786440 | tf_op jit(solution)/shard_map/ppermute | solution.py:319
  67.1 13.9 %all-to-all-start.3 = ((bf16[16,64,128]{2,1,0:T(8,128)(2,1)}), bf16[16,64,128]{2,1,0:T(8,128)(2,1)S(1)}, u32[]{:S(2)}, u32[]{:S(2)}) async-start(bf16[16,64,128]{2,1,0:T(8,128)(2,1)} %get-tuple-element.43), calls=%async_computation.3 | async-start | bytes 524288 | tf_op jit(solution)/shard_map/all_to_all | solution.py:317
  81.1 1.5 %collective-permute-start.4 = (bf16[16,64,128]{2,1,0:T(8,128)(2,1)S(1)}, bf16[16,64,128]{2,1,0:T(8,128)(2,1)S(1)}, u32[]{:S(2)}, u32[]{:S(2)}) collective-permute-start(bf16[16,64,128]{2,1,0:T(8,128)(2,1)S(1)} %all-to-all-done.3.refs_0_), channel_id=1, source_target_pairs={{0,1},{1,0},{2,3},{3,2},{4,5},{5,4},{6,7},{7,6},{8,9},{9,8},{10,11... | collective-permute-start | bytes 786440 | tf_op jit(solution)/shard_map/ppermute | solution.py:319
  84.4 12.4 %all-to-all-start.4 = ((f32[16,24,128]{2,1,0:T(8,128)}), f32[16,24,128]{2,1,0:T(8,128)S(1)}, u32[]{:S(2)}, u32[]{:S(2)}) async-start(f32[16,24,128]{2,1,0:T(8,128)} %get-tuple-element.47), calls=%async_computation.4 | async-start | bytes 393216 | tf_op jit(solution)/shard_map/all_to_all | solution.py:391
  96.8 1.2 %collective-permute-start.5 = (f32[24,128]{1,0:T(8,128)S(1)}, f32[24,128]{1,0:T(8,128)S(1)}, u32[]{:S(2)}, u32[]{:S(2)}) collective-permute-start(f32[24,128]{1,0:T(8,128)S(1)} %reduce_sum.9.refs_0_), channel_id=1, source_target_pairs={{0,1},{1,0},{2,3},{3,2},{4,5},{5,4},{6,7},{7,6},{8,9},{9,8},{10,11... | collective-permute-start | bytes 36872 | tf_op jit(solution)/shard_map/ppermute | solution.py:394

commit v4 on v3

--- a/solution.py
+++ b/solution.py
@@ -8,6 +8,7 @@
 from jax.sharding import PartitionSpec as P
 
 ITERS = 3
+PLANES = 3
 HIGHEST = lax.Precision.HIGHEST
 F32 = jnp.float32
 BF16 = jnp.bfloat16
@@ -68,10 +69,10 @@
     return other * (cols // 2) + column // 2
 
 
-def prepare_kernel(sizes, mask_hbm, stored_hbm, start_hbm, order_hbm, to_rows_ref, *refs):
+def prepare_kernel(sizes, mask_hbm, stored_hbm, start_hbm, order_hbm, *refs):
     rows, cols, width = sizes
-    to_cols, (piece_ref, picked_ref) = refs[:cols], refs[cols : cols + 2]
-    mask_ref, stored_ref, start_ref, order_ref, arrived = refs[cols + 2 :]
+    to_rows, to_cols_ref = refs[:rows], refs[rows]
+    piece_ref, picked_ref, mask_ref, stored_ref, start_ref, order_ref, sums_ref, arrived = refs[rows + 1 :]
     here_row, here_col = lax.axis_index("row"), lax.axis_index("col")
     columns = slots(cols)
     copies = [
@@ -101,51 +102,52 @@
         lines[s].wait()
         row_block = here_row * cols + columns[s]
         line = []
-        for i in range(rows):
+        for distance in range(rows):
+            i = lax.rem(here_row + distance, rows)
             col_block = i * cols + here_col
             whole = jnp.where((mask_ref[columns[s], i] > 0) & (row_block < col_block), 1.0, 0.0)
             partly = jnp.where(row_block == col_block, 1.0, 0.0)
             keep = (whole + partly * upper).astype(BF16)
-            line.append(stored_ref[s, :, i * width : (i + 1) * width] * keep)
-            to_rows_ref[i, s * width : (s + 1) * width] = line[i]
+            line.append(stored_ref[s, :, pl.ds(pl.multiple_of(i * width, width), width)] * keep)
+            to_rows[distance][s * width : (s + 1) * width] = line[-1]
+            to_cols_ref[columns[s], :, distance * width : (distance + 1) * width] = line[-1]
         line_degrees.append(dot(ones, lanes(line), ((1,), (1,)))[0:1])
-    for distance in range(cols):
-        s = slot_of(lax.rem(here_col + distance, cols), cols)
-        from_line = pl.ds(pl.multiple_of(s * width, width), width)
-        for i in range(rows):
-            to_cols[distance][:, i * width : (i + 1) * width] = to_rows_ref[i, from_line]
-    degrees = [dot(ones[:, : cols * width], to_rows_ref[i], ((1,), (0,)))[0:1] for i in range(rows)]
+    for distance in range(rows):
+        part = dot(ones[:, : cols * width], to_rows[distance][...], ((1,), (0,)))
+        sums_ref[pl.ds(lax.rem(here_row + distance, rows), 1)] = part[0:1]
+    degrees = [sums_ref[...]]
     swapped = line_degrees[cols // 2 :] + line_degrees[: cols // 2]
     odd = lax.rem(here_col, 2) == 1
     for c in range(cols):
         s = c // 2 + (c % 2) * (cols // 2)
         degrees.append(jnp.where(odd, swapped[s], line_degrees[s]))
     k = picked.shape[0]
-    extra = (piece_ref.shape[-2] - k) // 3
+    extra = (piece_ref.shape[-2] - k) // PLANES
     if extra > rows + cols:
         degrees.append(jnp.zeros((extra - rows - cols, width), F32))
     left = jnp.concatenate(degrees, axis=0)
     planes = [picked.astype(BF16)]
-    for _ in range(3):
+    for _ in range(PLANES):
         planes.append(left.astype(BF16))
         left = left - planes[-1].astype(F32)
     piece = jnp.concatenate(planes, axis=0)
-    for i in range(rows):
-        piece_ref[i] = piece
+    piece_ref[...] = piece
 
 
 def product(vectors_of, parts, sizes):
     rows, cols, _ = sizes
-    here_col = lax.axis_index("col")
+    here_row, here_col = lax.axis_index("row"), lax.axis_index("col")
     total = None
     for distance in range(cols):
         column = lax.rem(here_col + (cols - distance), cols)
-        vectors = lanes([vectors_of(distance % 2, column // 2, i) for i in range(rows)])
-        term = dot(vectors, parts[1 + distance][...], ((1,), (1,)))
+        sources = [lax.rem(here_row + i, rows) for i in range(rows)]
+        vectors = lanes([vectors_of(distance % 2, column // 2, i) for i in sources])
+        term = dot(vectors, parts[rows][column], ((1,), (1,)))
         total = term if total is None else total + term
-    for i in range(rows):
+    for distance in range(rows):
+        i = lax.rem(here_row + (rows - distance), rows)
         vectors = lanes([vectors_of(s, x, i) for s in range(2) for x in range(cols // 2)])
-        total = total + dot(vectors, parts[0][i], ((1,), (0,)))
+        total = total + dot(vectors, parts[distance][...], ((1,), (0,)))
     return total
 
 
@@ -153,12 +155,21 @@
     return roots_ref[lax.axis_index("col") // 2, pl.ds(lax.axis_index("row"), 1)]
 
 
+def slot_rows(rows):
+    here = lax.axis_index("row")
+    found = []
+    for distance in range(0, rows, 2):
+        row = lax.rem(here + (rows - distance), rows)
+        found += [row, row + 1 - 2 * lax.rem(row, 2)]
+    return found
+
+
 def find_roots(sizes, k, all_ref, roots_ref):
     rows, cols, _ = sizes
-    extra = (all_ref.shape[-2] - k) // 3
+    extra = (all_ref.shape[-2] - k) // PLANES
 
     def degrees(c, i):
-        planes = [all_ref[c, i, k + n * extra : k + (n + 1) * extra].astype(F32) for n in range(3)]
+        planes = [all_ref[c, i, k + n * extra : k + (n + 1) * extra].astype(F32) for n in range(PLANES)]
         return (planes[0] + planes[1]) + planes[2]
 
     def summed(terms):
@@ -168,11 +179,12 @@
         return total
 
     sums = [[degrees(c, i) for i in range(rows)] for c in range(cols)]
-    across = [summed([sums[c][i] for c in range(cols)]) for i in range(rows)]
+    across = [summed([sums[c][n] for c in range(cols)]) for n in range(rows)]
     for c in range(cols):
-        part = summed(sums[c])
-        other = jnp.concatenate([across[i][rows + c : rows + c + 1] for i in range(rows)], axis=0)
-        roots_ref[slot_of(c, cols)] = 1.0 / jnp.sqrt(part[:rows] + other)
+        s = slot_of(c, cols)
+        for n, place in enumerate(slot_rows(rows)):
+            roots_ref[s, pl.ds(place, 1)] = across[n][rows + c : rows + c + 1]
+        roots_ref[s] = 1.0 / jnp.sqrt(roots_ref[s] + summed(sums[c])[:rows])
 
 
 def send(vectors, copies_ref):
@@ -189,11 +201,11 @@
     find_roots(sizes, k, all_ref, roots_ref)
     for c in range(cols):
         s = slot_of(c, cols)
-        for i in range(rows):
-            value = all_ref[c, i, :k].astype(F32) * roots_ref[s, i : i + 1]
+        for n, place in enumerate(slot_rows(rows)):
+            value = all_ref[c, n, :k].astype(F32) * roots_ref[s, pl.ds(place, 1)]
             high = value.astype(BF16)
-            scratch[s, i, :k] = high
-            scratch[s, i, k:] = (value - high.astype(F32)).astype(BF16)
+            scratch[s, place, :k] = high
+            scratch[s, place, k:] = (value - high.astype(F32)).astype(BF16)
     total = product(lambda s, x, i: scratch[s * half + x, i], parts, sizes)
     root = own_root(roots_ref)
     image = picked_ref[...] + root * (total[:k] + total[k:])
@@ -301,8 +313,12 @@
     )(*operands)
 
 
-def gather_start(copies):
-    return lax.all_gather(lax.all_to_all(copies, "row", 0, 0, tiled=True), "col", axis=0, tiled=False)
+def pass_start(piece, rows):
+    pieces = jnp.stack([piece, lax.ppermute(piece, "row", [(i, i + 1 - 2 * (i % 2)) for i in range(rows)])])
+    return [pieces] + [
+        lax.ppermute(pieces, "row", [(i, (i + distance) % rows) for i in range(rows)])
+        for distance in range(2, rows, 2)
+    ]
 
 
 def parities(rows, cols):
@@ -319,6 +335,18 @@
     return same, lax.ppermute(same, "col", swap(cols)), factor
 
 
+def move_up(part, rows, distance):
+    return lax.ppermute(part, "row", [(i, i + distance) for i in range(rows - distance)])
+
+
+def exchange(parts, rows, cols, near):
+    parts = list(parts)
+    for distance in range(near + 1, rows):
+        parts[distance] = move_up(parts[distance], rows, distance)
+    parts[rows] = lax.all_to_all(parts[rows], "col", 0, 0, tiled=True)
+    return parts
+
+
 def local(start_vectors, cluster_order, weights, block_mask):
     rows, cols = lax.axis_size("row"), lax.axis_size("col")
     k, width = start_vectors.shape
@@ -329,12 +357,12 @@
 
     shape = jax.ShapeDtypeStruct
     extra = -(-(rows + cols) // 16) * 16
-    to_rows, *to_cols, piece, picked = kernel_call(
+    *parts, piece, picked = kernel_call(
         bound(prepare_kernel),
         [
-            shape((rows, cols * width, width), BF16),
-            *[shape((width, rows * width), BF16)] * cols,
-            shape((rows, k + 3 * extra, width), BF16),
+            *[shape((cols * width, width), BF16)] * rows,
+            shape((cols, width, rows * width), BF16),
+            shape((k + PLANES * extra, width), BF16),
             shape((k, width), F32),
         ],
         block_mask[:, 0, :],
@@ -346,15 +374,21 @@
             pltpu.VMEM((cols, width, rows * width), BF16),
             pltpu.VMEM((k, width), F32),
             pltpu.VMEM((1, width), jnp.int32),
+            pltpu.VMEM((rows, width), F32),
             pltpu.SemaphoreType.DMA((cols + 3,)),
         ],
         space=pltpu.HBM,
         limit=60 << 20,
     )
-    everyone = gather_start(piece)
-    parts = [lax.all_to_all(to_rows, "row", 0, 0, tiled=True), to_cols[0]]
-    for distance in range(1, cols):
-        parts.append(lax.ppermute(to_cols[distance], "col", [(c, (c + distance) % cols) for c in range(cols)]))
+    groups = pass_start(piece, rows)
+    parts = list(parts)
+    groups[0], *tied = lax.optimization_barrier([groups[0], *parts[1:rows]])
+    parts[1:rows] = tied
+    near = 2
+    parts = exchange(parts, rows, cols, near)
+    everyone = lax.all_gather(jnp.concatenate(groups), "col", axis=0, tiled=False)
+    everyone, *tied = lax.optimization_barrier([everyone, *parts[1 : near + 1]])
+    parts[1 : near + 1] = [move_up(part, rows, 1 + n) for n, part in enumerate(tied)]
     copies, own_shape = shape((rows * cols // 2, k, width), BF16), shape((k, width), F32)
     factor_shape = shape((k, k), F32)
     factor = kernel_call(bound(first_factor_kernel), [factor_shape], everyone)

time: 102 us -> 99.1 us (0.972)
  blocking collectives: 47.8 us -> 27.9 us
  starting transfers between devices: 14 us -> 33.3 us
  waiting for transfers between devices: 18.9 us -> 16.6 us
    ppermute x3 -> x11, starting transfers between devices: 3 us -> 22.3 us  [the longest x7 14.6 us: move_up(): lax.ppermute(part, 'row', [(i, i + distance) for i in range(rows - distan...]
    all_to_all x1 -> x0, blocking collectives: 15.7 us -> none  [gather_start(): lax.all_to_all(copies, 'row', 0, 0, tiled=True)]
    all_gather x1, blocking collectives: 17.3 us -> 9.92 us  [local(): lax.all_gather(jnp.concatenate(groups), 'col', axis=0, tiled=False)]
    all_to_all x1, blocking collectives: 14.8 us -> 18 us  [gather_vectors(): lax.all_to_all(copies, ('row', 'col'), 0, 0, tiled=True, axis_index_group...]
    all_to_all x1, waiting for transfers between devices: 2.35 us -> 0.01 us  [exchange(): parts[rows] = lax.all_to_all(parts[rows], 'col', 0, 0, tiled=True)]
  transfers between devices with their start and end apart: 9 -> 17, of which waited for: 6 -> 5; matrix products, arithmetic and copies ran while one was open for 0% -> 0% of each run, Pallas kernels for 9% -> 10%
where the time goes in v4:
time: 99.1 us; the launch traced here: 98.6 us
  starting transfers between devices  33.3 us (34%)
  blocking collectives  27.9 us (28%)
  Pallas kernels  20.4 us (21%)
  waiting for transfers between devices  16.6 us (17%)
    pallas_call x8, Pallas kernels, kernel_call(): pl.pallas_call(body, out_shape=outs[0] if single else tuple(outs), in_spe...  20.4 us
    all_to_all x1, blocking collectives, gather_vectors(): lax.all_to_all(copies, ('row', 'col'), 0, 0, tiled=True, axis_index_group...  18 us
    ppermute x7, starting transfers between devices, move_up(): lax.ppermute(part, 'row', [(i, i + distance) for i in range(rows - distan...  14.6 us
    all_gather x1, blocking collectives, local(): lax.all_gather(jnp.concatenate(groups), 'col', axis=0, tiled=False)  9.92 us
    all_to_all x1, waiting for transfers between devices, gather_vectors(): lax.all_to_all(copies, ('row', 'col'), 0, 0, tiled=True, axis_index_group...  7.11 us
    all_to_all x1, waiting for transfers between devices, local(): lax.all_to_all(gram, ('row', 'col'), 0, 0, tiled=True, axis_index_groups=...  5.23 us
    ppermute x3, starting transfers between devices, pass_start(): lax.ppermute(pieces, 'row', [(i, (i + distance) % rows) for i in range(ro...  4.66 us
    all_to_all x1, starting transfers between devices, local(): lax.all_to_all(gram, ('row', 'col'), 0, 0, tiled=True, axis_index_groups=...  3.7 us
  transfers between devices with their start and end apart: 17, of which 5 were waited for; matrix products, arithmetic and copies ran while one was open for 0% of the time, Pallas kernels for 10%

profile of v4, /device:TPU:0, one launch (start us, length us, event | category | flops | bytes accessed | tf_op | source)
XLA Modules:
  0.0 98.6 jit_solution(349909349058716820)
XLA Ops:
  0.0 3.2 %shard_map.46 = (bf16[512,128]{1,0:T(8,128)(2,1)}, bf16[512,128]{1,0:T(8,128)(2,1)}, bf16[512,128]{1,0:T(8,128)(2,1)}, bf16[512,128]{1,0:T(8,128)(2,1)}, bf16[51...) custom-call(s32[4,8]{1,0:T(4,128)} %bitcast.10, ...), custom_call_target="tpu_custom_call" | custom-call | bytes 3240576 | tf_op jit(solution)/shard_map/pallas_call | solution.py:305
  3.3 3.0 %collective-permute-start = (bf16[112,128]{1,0:T(8,128)(2,1)}, bf16[112,128]{1,0:T(8,128)(2,1)S(1)}, u32[]{:S(2)}, u32[]{:S(2)}) collective-permute-start(bf16[112,128]{1,0:T(8,128)(2,1)} %get-tuple-element.44), channel_id=1, source_target_pairs={{0,4},{4,0},{8,12},{12,8},{16,20},{20,16},{24,28},{28,24},{1,5},{5... | collective-permute-start | bytes 86024 | tf_op jit(solution)/shard_map/ppermute | solution.py:317
  6.3 3.7 %all-to-all-start = ((bf16[4,128,1024]{2,1,0:T(8,128)(2,1)}), bf16[4,128,1024]{2,1,0:T(8,128)(2,1)S(1)}, u32[]{:S(2)}, u32[]{:S(2)}) async-start(bf16[4,128,1024]{2,1,0:T(8,128)(2,1)} %get-tuple-element.66), calls=%async_computation | async-start | bytes 2097152 | tf_op jit(solution)/shard_map/all_to_all | solution.py:346
  10.0 0.0 collective-permute-done
  10.0 3.7 %collective-permute-start.3 = (bf16[2,112,128]{2,1,0:T(8,128)(2,1)S(1)}, bf16[2,112,128]{2,1,0:T(8,128)(2,1)S(1)}, u32[]{:S(2)}, u32[]{:S(2)}) collective-permute-start(bf16[2,112,128]{2,1,0:T(8,128)(2,1)S(1)} %pad_maximum_fusion.1), channel_id=1, source_target_pairs={{0,24},{4,28},{8,0},{12,4},{16,8},{20,12},{24,16},{28,20},{1,25},{... | collective-permute-start | bytes 172040 | tf_op jit(solution)/shard_map/ppermute | solution.py:319
  13.7 0.0 collective-permute-start.2
  13.7 1.0 %collective-permute-start.1 = (bf16[2,112,128]{2,1,0:T(8,128)(2,1)S(1)}, bf16[2,112,128]{2,1,0:T(8,128)(2,1)S(1)}, u32[]{:S(2)}, u32[]{:S(2)}) collective-permute-start(bf16[2,112,128]{2,1,0:T(8,128)(2,1)S(1)} %pad_maximum_fusion.1), channel_id=1, source_target_pairs={{0,8},{4,12},{8,16},{12,20},{16,24},{20,28},{24,0},{28,4},{1,9},{5... | collective-permute-start | bytes 172040 | tf_op jit(solution)/shard_map/ppermute | solution.py:319
  14.7 4.3 %collective-permute-start.6 = (bf16[512,128]{1,0:T(8,128)(2,1)S(1)}, bf16[512,128]{1,0:T(8,128)(2,1)S(1)}, u32[]{:S(2)}, u32[]{:S(2)}) collective-permute-start(bf16[512,128]{1,0:T(8,128)(2,1)S(1)} %copy-done.9), channel_id=1, source_target_pairs={{0,12},{4,16},{8,20},{12,24},{16,28},{1,13},{5,17},{9,21},{13,25},... | collective-permute-start | bytes 393224 | tf_op jit(solution)/shard_map/ppermute | solution.py:339
  19.0 2.8 %collective-permute-start.7 = (bf16[512,128]{1,0:T(8,128)(2,1)S(1)}, bf16[512,128]{1,0:T(8,128)(2,1)S(1)}, u32[]{:S(2)}, u32[]{:S(2)}) collective-permute-start(bf16[512,128]{1,0:T(8,128)(2,1)S(1)} %copy-done.8), channel_id=1, source_target_pairs={{0,16},{4,20},{8,24},{12,28},{1,17},{5,21},{9,25},{13,29},{2,18},{... | collective-permute-start | bytes 393224 | tf_op jit(solution)/shard_map/ppermute | solution.py:339
  21.8 0.0 collective-permute-done.3
  21.9 1.3 %collective-permute-start.8 = (bf16[512,128]{1,0:T(8,128)(2,1)S(1)}, bf16[512,128]{1,0:T(8,128)(2,1)S(1)}, u32[]{:S(2)}, u32[]{:S(2)}) collective-permute-start(bf16[512,128]{1,0:T(8,128)(2,1)S(1)} %copy-done.7), channel_id=1, source_target_pairs={{0,20},{4,24},{8,28},{1,21},{5,25},{9,29},{2,22},{6,26},{10,30},{3... | collective-permute-start | bytes 393224 | tf_op jit(solution)/shard_map/ppermute | solution.py:339
  23.2 1.3 %collective-permute-start.9 = (bf16[512,128]{1,0:T(8,128)(2,1)S(1)}, bf16[512,128]{1,0:T(8,128)(2,1)S(1)}, u32[]{:S(2)}, u32[]{:S(2)}) collective-permute-start(bf16[512,128]{1,0:T(8,128)(2,1)S(1)} %copy-done.6), channel_id=1, source_target_pairs={{0,24},{4,28},{1,25},{5,29},{2,26},{6,30},{3,27},{7,31}} | collective-permute-start | bytes 393224 | tf_op jit(solution)/shard_map/ppermute | solution.py:339
  24.5 1.3 %collective-permute-start.10 = (bf16[512,128]{1,0:T(8,128)(2,1)S(1)}, bf16[512,128]{1,0:T(8,128)(2,1)S(1)}, u32[]{:S(2)}, u32[]{:S(2)}) collective-permute-start(bf16[512,128]{1,0:T(8,128)(2,1)S(1)} %copy-done.5), channel_id=1, source_target_pairs={{0,28},{1,29},{2,30},{3,31}} | collective-permute-start | bytes 393224 | tf_op jit(solution)/shard_map/ppermute | solution.py:339
  25.9 9.9 %all-gather = bf16[32,112,128]{2,1,0:T(8,128)(2,1)S(1)} all-gather(bf16[8,112,128]{2,1,0:T(8,128)(2,1)S(1)} %pad_maximum_fusion), channel_id=2, replica_groups=mesh['row'=8,'col'=4] {'col'}, dimensions={0}, use_global_device_ids=true | all-gather | bytes 1146880 | tf_op jit(solution)/shard_map/all_gather | solution.py:389
  35.8 1.9 %collective-permute-start.4 = (bf16[512,128]{1,0:T(8,128)(2,1)S(1)}, bf16[512,128]{1,0:T(8,128)(2,1)S(1)}, u32[]{:S(2)}, u32[]{:S(2)}) collective-permute-start(bf16[512,128]{1,0:T(8,128)(2,1)S(1)} %copy-done.4), channel_id=1, source_target_pairs={{0,4},{4,8},{8,12},{12,16},{16,20},{20,24},{24,28},{1,5},{5,9},{9,... | collective-permute-start | bytes 393224 | tf_op jit(solution)/shard_map/ppermute | solution.py:339
  37.7 1.7 %collective-permute-start.5 = (bf16[512,128]{1,0:T(8,128)(2,1)S(1)}, bf16[512,128]{1,0:T(8,128)(2,1)S(1)}, u32[]{:S(2)}, u32[]{:S(2)}) collective-permute-start(bf16[512,128]{1,0:T(8,128)(2,1)S(1)} %copy-done.3), channel_id=1, source_target_pairs={{0,8},{4,12},{8,16},{12,20},{16,24},{20,28},{1,9},{5,13},{9,17},{1... | collective-permute-start | bytes 393224 | tf_op jit(solution)/shard_map/ppermute | solution.py:339
  39.4 2.8 %shard_map.47.refs_4_.refs_3_ = f32[64,64]{1,0:T(8,128)S(1)} custom-call(bf16[4,8,112,128]{3,2,1,0:T(8,128)(2,1)S(1)} %bitcast.5), custom_call_target="tpu_custom_call" | custom-call | bytes 933888 | tf_op jit(solution)/shard_map/pallas_call | solution.py:305
  42.3 1.0 %shard_map.48 = (bf16[16,64,128]{2,1,0:T(8,128)(2,1)S(1)}, f32[64,128]{1,0:T(8,128)S(1)}, f32[4,8,128]{2,1,0:T(8,128)S(1)}) custom-call(bf16[4,8,112,128]{3,2,1,0:T(8,128)(2,1)S(1)} %bitcast.6, f32[64,128]{1,0:T(8,128)S(1)} %copy-done.1, bf16[512,128]{1,0:T(8,128)(2,1)S(1)} %copy-done, bf16[512,128]{1,0:T(8,128)(2,1)S(1)} %collective-permute-done.4.refs_3_.refs_6_, ...), custom_call_target="tpu_custom_call" | custom-call | bytes 3358720 | tf_op jit(solution)/shard_map/pallas_call | solution.py:305
  43.3 18.0 %all_to_all.20.refs_0_ = bf16[16,64,128]{2,1,0:T(8,128)(2,1)S(1)} all-to-all(bf16[16,64,128]{2,1,0:T(8,128)(2,1)S(1)} %get-tuple-element.67), channel_id=1, replica_groups={{0,2,4,6,8,10,12,14,16,18,20,22,24,26,28,30},{1,3,5,7,9,11,13,15,17,19,..., dimensions={0} | all-to-all | bytes 524288 | tf_op jit(solution)/shard_map/all_to_all | solution.py:333
  61.3 1.5 %collective-permute-done.11.refs_1_ = bf16[16,64,128]{2,1,0:T(8,128)(2,1)S(1)} collective-permute-done((bf16[16,64,128]{2,1,0:T(8,128)(2,1)S(1)}, bf16[16,64,128]{2,1,0:T(8,128)(2,1)S(1)}, u32[]{:S(2)}, u32[]{:S(2)}) %collective-permute-start.11) | collective-permute-done | bytes 262176 | tf_op jit(solution)/shard_map/ppermute | solution.py:335
  62.9 1.5 %shard_map.49 = (bf16[16,64,128]{2,1,0:T(8,128)(2,1)}, f32[64,128]{1,0:T(8,128)S(1)}) custom-call(bf16[16,64,128]{2,1,0:T(8,128)(2,1)S(1)} %all_to_all.20.refs_0_, bf16[16,64,128]{2,1,0:T(8,128)(2,1)S(1)} %collective-permute-done.11.refs_1_, f32[64,128]{1,0:T(8,128)S(1)} %get-tuple-element.70.refs_2_, f32[4,8,128]{2,1,0:T(8,128)S(1)} %get-tuple-element.71.refs_3_.refs_2_, ...), custom_call_target="tpu_custom_call" | custom-call | bytes 2981888 | tf_op jit(solution)/shard_map/pallas_call | solution.py:305
  64.4 3.5 %all-to-all-start.2 = ((bf16[16,64,128]{2,1,0:T(8,128)(2,1)}), bf16[16,64,128]{2,1,0:T(8,128)(2,1)S(1)}, u32[]{:S(2)}, u32[]{:S(2)}) async-start(bf16[16,64,128]{2,1,0:T(8,128)(2,1)} %get-tuple-element.73), calls=%async_computation.2 | async-start | bytes 524288 | tf_op jit(solution)/shard_map/all_to_all | solution.py:333
  68.0 3.3 %shard_map.50.refs_4_.refs_3_ = f32[64,64]{1,0:T(8,128)S(1)} custom-call(bf16[16,64,128]{2,1,0:T(8,128)(2,1)S(1)} %all_to_all.20.refs_0_, bf16[16,64,128]{2,1,0:T(8,128)(2,1)S(1)} %collective-permute-done.11.refs_1_, f32[4,8,128]{2,1,0:T(8,128)S(1)} %get-tuple-element.71.refs_3_.refs_2_, f32[64,64]{1,0:T(8,128)S(1)} %shard_map.47.refs_4_.refs_3_), custom_call_target="tpu_custom_call" | custom-call | bytes 573440 | tf_op jit(solution)/shard_map/pallas_call | solution.py:305
  71.2 7.1 %all-to-all-done.2.refs_0_ = bf16[16,64,128]{2,1,0:T(8,128)(2,1)S(1)} async-done(((bf16[16,64,128]{2,1,0:T(8,128)(2,1)}), bf16[16,64,128]{2,1,0:T(8,128)(2,1)S(1)}, u32[]{:S(2)}, u32[]{:S(2)}) %all-to-all-start.2) | async-done | bytes 262176 | tf_op jit(solution)/shard_map/all_to_all | solution.py:333
  78.3 1.5 %collective-permute-done.12.refs_1_ = bf16[16,64,128]{2,1,0:T(8,128)(2,1)S(1)} collective-permute-done((bf16[16,64,128]{2,1,0:T(8,128)(2,1)S(1)}, bf16[16,64,128]{2,1,0:T(8,128)(2,1)S(1)}, u32[]{:S(2)}, u32[]{:S(2)}) %collective-permute-start.12) | collective-permute-done | bytes 262176 | tf_op jit(solution)/shard_map/ppermute | solution.py:335
  79.9 1.8 %shard_map.51 = (f32[64,128]{1,0:T(8,128)S(1)}, f32[16,24,128]{2,1,0:T(8,128)}) custom-call(bf16[16,64,128]{2,1,0:T(8,128)(2,1)S(1)} %all-to-all-done.2.refs_0_, bf16[16,64,128]{2,1,0:T(8,128)(2,1)S(1)} %collective-permute-done.12.refs_1_, f32[64,128]{1,0:T(8,128)S(1)} %get-tuple-element.75.refs_2_, f32[4,8,128]{2,1,0:T(8,128)S(1)} %get-tuple-element.71.refs_3_.refs_2_, ...), custom_call_target="tpu_custom_call" | custom-call | bytes 2916352 | tf_op jit(solution)/shard_map/pallas_call | solution.py:305
  81.7 3.7 %all-to-all-start.3 = ((f32[16,24,128]{2,1,0:T(8,128)}), f32[16,24,128]{2,1,0:T(8,128)S(1)}, u32[]{:S(2)}, u32[]{:S(2)}) async-start(f32[16,24,128]{2,1,0:T(8,128)} %get-tuple-element.77), calls=%async_computation.3 | async-start | bytes 393216 | tf_op jit(solution)/shard_map/all_to_all | solution.py:425
  85.4 3.5 %shard_map.52 = (f32[64,64]{1,0:T(8,128)S(1)}, f32[64,128]{1,0:T(8,128)S(1)}) custom-call(bf16[16,64,128]{2,1,0:T(8,128)(2,1)S(1)} %all-to-all-done.2.refs_0_, bf16[16,64,128]{2,1,0:T(8,128)(2,1)S(1)} %collective-permute-done.12.refs_1_, f32[4,8,128]{2,1,0:T(8,128)S(1)} %get-tuple-element.71.refs_3_.refs_2_, f32[64,64]{1,0:T(8,128)S(1)} %shard_map.50.refs_4_.refs_3_, ...), custom_call_target="tpu_custom_call" | custom-call | bytes 638976 | tf_op jit(solution)/shard_map/pallas_call | solution.py:305
  88.9 5.2 %all-to-all-done.3 = f32[16,24,128]{2,1,0:T(8,128)S(1)} async-done(((f32[16,24,128]{2,1,0:T(8,128)}), f32[16,24,128]{2,1,0:T(8,128)S(1)}, u32[]{:S(2)}, u32[]{:S(2)}) %all-to-all-start.3) | async-done | bytes 196640 | tf_op jit(solution)/shard_map/all_to_all | solution.py:425
  94.1 0.1 collective-permute-start.13
  94.2 1.2 %collective-permute-done.13.refs_1_ = f32[24,128]{1,0:T(8,128)S(1)} collective-permute-done((f32[24,128]{1,0:T(8,128)S(1)}, f32[24,128]{1,0:T(8,128)S(1)}, u32[]{:S(2)}, u32[]{:S(2)}) %collective-permute-start.13) | collective-permute-done | bytes 12320 | tf_op jit(solution)/shard_map/ppermute | solution.py:428
  95.3 3.2 %shard_map.53 = f32[64,128]{1,0:T(8,128)} custom-call(f32[24,128]{1,0:T(8,128)S(1)} %reduce_sum.9.refs_0_, f32[24,128]{1,0:T(8,128)S(1)} %collective-permute-done.13.refs_1_, f32[64,64]{1,0:T(8,128)S(1)} %get-tuple-element.81.refs_2_, f32[64,128]{1,0:T(8,128)S(1)} %get-tuple-element.82.refs_3_), custom_call_target="tpu_custom_call" | custom-call | bytes 106496 | tf_op jit(solution)/shard_map/pallas_call | solution.py:305
  (35 shorter events, 0.1 us)
Async XLA Ops:
  3.3 6.7 %collective-permute-start = (bf16[112,128]{1,0:T(8,128)(2,1)}, bf16[112,128]{1,0:T(8,128)(2,1)S(1)}, u32[]{:S(2)}, u32[]{:S(2)}) collective-permute-start(bf16[112,128]{1,0:T(8,128)(2,1)} %get-tuple-element.44), channel_id=1, source_target_pairs={{0,4},{4,0},{8,12},{12,8},{16,20},{20,16},{24,28},{28,24},{1,5},{5... | collective-permute-start | bytes 86024 | tf_op jit(solution)/shard_map/ppermute | solution.py:317
  6.3 3.7 %copy-start.2 = (bf16[112,128]{1,0:T(8,128)(2,1)S(1)}, bf16[112,128]{1,0:T(8,128)(2,1)}, u32[]{:S(2)}) copy-start(bf16[112,128]{1,0:T(8,128)(2,1)} %get-tuple-element.44) | copy-start | bytes 86020
  6.3 8.4 %copy-start.9 = (bf16[512,128]{1,0:T(8,128)(2,1)S(1)}, bf16[512,128]{1,0:T(8,128)(2,1)}, u32[]{:S(2)}) copy-start(bf16[512,128]{1,0:T(8,128)(2,1)} %get-tuple-element.61) | copy-start | bytes 393220
  6.3 12.7 %copy-start.8 = (bf16[512,128]{1,0:T(8,128)(2,1)S(1)}, bf16[512,128]{1,0:T(8,128)(2,1)}, u32[]{:S(2)}) copy-start(bf16[512,128]{1,0:T(8,128)(2,1)} %get-tuple-element.62) | copy-start | bytes 393220
  6.3 15.6 %copy-start.7 = (bf16[512,128]{1,0:T(8,128)(2,1)S(1)}, bf16[512,128]{1,0:T(8,128)(2,1)}, u32[]{:S(2)}) copy-start(bf16[512,128]{1,0:T(8,128)(2,1)} %get-tuple-element.63) | copy-start | bytes 393220
  6.3 16.9 %copy-start.6 = (bf16[512,128]{1,0:T(8,128)(2,1)S(1)}, bf16[512,128]{1,0:T(8,128)(2,1)}, u32[]{:S(2)}) copy-start(bf16[512,128]{1,0:T(8,128)(2,1)} %get-tuple-element.64) | copy-start | bytes 393220
  6.3 36.0 %all-to-all-start = ((bf16[4,128,1024]{2,1,0:T(8,128)(2,1)}), bf16[4,128,1024]{2,1,0:T(8,128)(2,1)S(1)}, u32[]{:S(2)}, u32[]{:S(2)}) async-start(bf16[4,128,1024]{2,1,0:T(8,128)(2,1)} %get-tuple-element.66), calls=%async_computation | async-start | bytes 2097152 | tf_op jit(solution)/shard_map/all_to_all | solution.py:346
  10.0 14.5 %copy-start.5 = (bf16[512,128]{1,0:T(8,128)(2,1)S(1)}, bf16[512,128]{1,0:T(8,128)(2,1)}, u32[]{:S(2)}) copy-start(bf16[512,128]{1,0:T(8,128)(2,1)} %get-tuple-element.65) | copy-start | bytes 393220
  10.0 11.8 %collective-permute-start.3 = (bf16[2,112,128]{2,1,0:T(8,128)(2,1)S(1)}, bf16[2,112,128]{2,1,0:T(8,128)(2,1)S(1)}, u32[]{:S(2)}, u32[]{:S(2)}) collective-permute-start(bf16[2,112,128]{2,1,0:T(8,128)(2,1)S(1)} %pad_maximum_fusion.1), channel_id=1, source_target_pairs={{0,24},{4,28},{8,0},{12,4},{16,8},{20,12},{24,16},{28,20},{1,25},{... | collective-permute-start | bytes 172040 | tf_op jit(solution)/shard_map/ppermute | solution.py:319
  13.7 9.5 %collective-permute-start.2 = (bf16[2,112,128]{2,1,0:T(8,128)(2,1)S(1)}, bf16[2,112,128]{2,1,0:T(8,128)(2,1)S(1)}, u32[]{:S(2)}, u32[]{:S(2)}) collective-permute-start(bf16[2,112,128]{2,1,0:T(8,128)(2,1)S(1)} %pad_maximum_fusion.1), channel_id=1, source_target_pairs={{0,16},{4,20},{8,24},{12,28},{16,0},{20,4},{24,8},{28,12},{1,17},{... | collective-permute-start | bytes 172040 | tf_op jit(solution)/shard_map/ppermute | solution.py:319
  13.7 10.8 %collective-permute-start.1 = (bf16[2,112,128]{2,1,0:T(8,128)(2,1)S(1)}, bf16[2,112,128]{2,1,0:T(8,128)(2,1)S(1)}, u32[]{:S(2)}, u32[]{:S(2)}) collective-permute-start(bf16[2,112,128]{2,1,0:T(8,128)(2,1)S(1)} %pad_maximum_fusion.1), channel_id=1, source_target_pairs={{0,8},{4,12},{8,16},{12,20},{16,24},{20,28},{24,0},{28,4},{1,9},{5... | collective-permute-start | bytes 172040 | tf_op jit(solution)/shard_map/ppermute | solution.py:319
  14.7 21.1 %collective-permute-start.6 = (bf16[512,128]{1,0:T(8,128)(2,1)S(1)}, bf16[512,128]{1,0:T(8,128)(2,1)S(1)}, u32[]{:S(2)}, u32[]{:S(2)}) collective-permute-start(bf16[512,128]{1,0:T(8,128)(2,1)S(1)} %copy-done.9), channel_id=1, source_target_pairs={{0,12},{4,16},{8,20},{12,24},{16,28},{1,13},{5,17},{9,21},{13,25},... | collective-permute-start | bytes 393224 | tf_op jit(solution)/shard_map/ppermute | solution.py:339
  19.0 18.7 %collective-permute-start.7 = (bf16[512,128]{1,0:T(8,128)(2,1)S(1)}, bf16[512,128]{1,0:T(8,128)(2,1)S(1)}, u32[]{:S(2)}, u32[]{:S(2)}) collective-permute-start(bf16[512,128]{1,0:T(8,128)(2,1)S(1)} %copy-done.8), channel_id=1, source_target_pairs={{0,16},{4,20},{8,24},{12,28},{1,17},{5,21},{9,25},{13,29},{2,18},{... | collective-permute-start | bytes 393224 | tf_op jit(solution)/shard_map/ppermute | solution.py:339
  21.9 20.3 %collective-permute-start.8 = (bf16[512,128]{1,0:T(8,128)(2,1)S(1)}, bf16[512,128]{1,0:T(8,128)(2,1)S(1)}, u32[]{:S(2)}, u32[]{:S(2)}) collective-permute-start(bf16[512,128]{1,0:T(8,128)(2,1)S(1)} %copy-done.7), channel_id=1, source_target_pairs={{0,20},{4,24},{8,28},{1,21},{5,25},{9,29},{2,22},{6,26},{10,30},{3... | collective-permute-start | bytes 393224 | tf_op jit(solution)/shard_map/ppermute | solution.py:339
  23.2 19.0 %collective-permute-start.9 = (bf16[512,128]{1,0:T(8,128)(2,1)S(1)}, bf16[512,128]{1,0:T(8,128)(2,1)S(1)}, u32[]{:S(2)}, u32[]{:S(2)}) collective-permute-start(bf16[512,128]{1,0:T(8,128)(2,1)S(1)} %copy-done.6), channel_id=1, source_target_pairs={{0,24},{4,28},{1,25},{5,29},{2,26},{6,30},{3,27},{7,31}} | collective-permute-start | bytes 393224 | tf_op jit(solution)/shard_map/ppermute | solution.py:339
  24.5 17.7 %collective-permute-start.10 = (bf16[512,128]{1,0:T(8,128)(2,1)S(1)}, bf16[512,128]{1,0:T(8,128)(2,1)S(1)}, u32[]{:S(2)}, u32[]{:S(2)}) collective-permute-start(bf16[512,128]{1,0:T(8,128)(2,1)S(1)} %copy-done.5), channel_id=1, source_target_pairs={{0,28},{1,29},{2,30},{3,31}} | collective-permute-start | bytes 393224 | tf_op jit(solution)/shard_map/ppermute | solution.py:339
  25.9 9.9 %copy-start.4 = (bf16[512,128]{1,0:T(8,128)(2,1)S(1)}, bf16[512,128]{1,0:T(8,128)(2,1)}, u32[]{:S(2)}) copy-start(bf16[512,128]{1,0:T(8,128)(2,1)} %get-tuple-element.59) | copy-start | bytes 393220
  25.9 11.8 %copy-start.3 = (bf16[512,128]{1,0:T(8,128)(2,1)S(1)}, bf16[512,128]{1,0:T(8,128)(2,1)}, u32[]{:S(2)}) copy-start(bf16[512,128]{1,0:T(8,128)(2,1)} %get-tuple-element.60) | copy-start | bytes 393220
  35.8 6.5 %copy-start = (bf16[512,128]{1,0:T(8,128)(2,1)S(1)}, bf16[512,128]{1,0:T(8,128)(2,1)}, u32[]{:S(2)}) copy-start(bf16[512,128]{1,0:T(8,128)(2,1)} %get-tuple-element.58.refs_2_.refs_5_) | copy-start | bytes 393220
  35.8 6.5 %copy-start.1 = (f32[64,128]{1,0:T(8,128)S(1)}, f32[64,128]{1,0:T(8,128)}, u32[]{:S(2)}) copy-start(f32[64,128]{1,0:T(8,128)} %get-tuple-element.57.refs_1_) | copy-start | bytes 98308
  35.8 6.4 %collective-permute-start.4 = (bf16[512,128]{1,0:T(8,128)(2,1)S(1)}, bf16[512,128]{1,0:T(8,128)(2,1)S(1)}, u32[]{:S(2)}, u32[]{:S(2)}) collective-permute-start(bf16[512,128]{1,0:T(8,128)(2,1)S(1)} %copy-done.4), channel_id=1, source_target_pairs={{0,4},{4,8},{8,12},{12,16},{16,20},{20,24},{24,28},{1,5},{5,9},{9,... | collective-permute-start | bytes 393224 | tf_op jit(solution)/shard_map/ppermute | solution.py:339
  37.7 4.6 %collective-permute-start.5 = (bf16[512,128]{1,0:T(8,128)(2,1)S(1)}, bf16[512,128]{1,0:T(8,128)(2,1)S(1)}, u32[]{:S(2)}, u32[]{:S(2)}) collective-permute-start(bf16[512,128]{1,0:T(8,128)(2,1)S(1)} %copy-done.3), channel_id=1, source_target_pairs={{0,8},{4,12},{8,16},{12,20},{16,24},{20,28},{1,9},{5,13},{9,17},{1... | collective-permute-start | bytes 393224 | tf_op jit(solution)/shard_map/ppermute | solution.py:339
  61.3 1.5 %collective-permute-start.11 = (bf16[16,64,128]{2,1,0:T(8,128)(2,1)S(1)}, bf16[16,64,128]{2,1,0:T(8,128)(2,1)S(1)}, u32[]{:S(2)}, u32[]{:S(2)}) collective-permute-start(bf16[16,64,128]{2,1,0:T(8,128)(2,1)S(1)} %all_to_all.20.refs_0_), channel_id=1, source_target_pairs={{0,1},{1,0},{2,3},{3,2},{4,5},{5,4},{6,7},{7,6},{8,9},{9,8},{10,11... | collective-permute-start | bytes 786440 | tf_op jit(solution)/shard_map/ppermute | solution.py:335
  64.4 13.9 %all-to-all-start.2 = ((bf16[16,64,128]{2,1,0:T(8,128)(2,1)}), bf16[16,64,128]{2,1,0:T(8,128)(2,1)S(1)}, u32[]{:S(2)}, u32[]{:S(2)}) async-start(bf16[16,64,128]{2,1,0:T(8,128)(2,1)} %get-tuple-element.73), calls=%async_computation.2 | async-start | bytes 524288 | tf_op jit(solution)/shard_map/all_to_all | solution.py:333
  78.3 1.5 %collective-permute-start.12 = (bf16[16,64,128]{2,1,0:T(8,128)(2,1)S(1)}, bf16[16,64,128]{2,1,0:T(8,128)(2,1)S(1)}, u32[]{:S(2)}, u32[]{:S(2)}) collective-permute-start(bf16[16,64,128]{2,1,0:T(8,128)(2,1)S(1)} %all-to-all-done.2.refs_0_), channel_id=1, source_target_pairs={{0,1},{1,0},{2,3},{3,2},{4,5},{5,4},{6,7},{7,6},{8,9},{9,8},{10,11... | collective-permute-start | bytes 786440 | tf_op jit(solution)/shard_map/ppermute | solution.py:335
  81.7 12.4 %all-to-all-start.3 = ((f32[16,24,128]{2,1,0:T(8,128)}), f32[16,24,128]{2,1,0:T(8,128)S(1)}, u32[]{:S(2)}, u32[]{:S(2)}) async-start(f32[16,24,128]{2,1,0:T(8,128)} %get-tuple-element.77), calls=%async_computation.3 | async-start | bytes 393216 | tf_op jit(solution)/shard_map/all_to_all | solution.py:425
  94.1 1.2 %collective-permute-start.13 = (f32[24,128]{1,0:T(8,128)S(1)}, f32[24,128]{1,0:T(8,128)S(1)}, u32[]{:S(2)}, u32[]{:S(2)}) collective-permute-start(f32[24,128]{1,0:T(8,128)S(1)} %reduce_sum.9.refs_0_), channel_id=1, source_target_pairs={{0,1},{1,0},{2,3},{3,2},{4,5},{5,4},{6,7},{7,6},{8,9},{9,8},{10,11... | collective-permute-start | bytes 36872 | tf_op jit(solution)/shard_map/ppermute | solution.py:428

commit v5 on v3

--- a/solution.py
+++ b/solution.py
@@ -121,17 +121,13 @@
         s = c // 2 + (c % 2) * (cols // 2)
         degrees.append(jnp.where(odd, swapped[s], line_degrees[s]))
     k = picked.shape[0]
-    extra = (piece_ref.shape[-2] - k) // 3
-    if extra > rows + cols:
-        degrees.append(jnp.zeros((extra - rows - cols, width), F32))
-    left = jnp.concatenate(degrees, axis=0)
-    planes = [picked.astype(BF16)]
-    for _ in range(3):
-        planes.append(left.astype(BF16))
-        left = left - planes[-1].astype(F32)
-    piece = jnp.concatenate(planes, axis=0)
+    spare = piece_ref.shape[-2] - k - rows - cols
+    if spare:
+        degrees.append(jnp.zeros((spare, width), F32))
+    degrees = jnp.concatenate(degrees, axis=0)
     for i in range(rows):
-        piece_ref[i] = piece
+        piece_ref[i, :k] = picked
+        piece_ref[i, k:] = degrees
 
 
 def product(vectors_of, parts, sizes):
@@ -153,13 +149,8 @@
     return roots_ref[lax.axis_index("col") // 2, pl.ds(lax.axis_index("row"), 1)]
 
 
-def find_roots(sizes, k, all_ref, roots_ref):
+def find_roots(sizes, k, block_of, roots_ref):
     rows, cols, _ = sizes
-    extra = (all_ref.shape[-2] - k) // 3
-
-    def degrees(c, i):
-        planes = [all_ref[c, i, k + n * extra : k + (n + 1) * extra].astype(F32) for n in range(3)]
-        return (planes[0] + planes[1]) + planes[2]
 
     def summed(terms):
         total = terms[0]
@@ -167,7 +158,7 @@
             total = total + term
         return total
 
-    sums = [[degrees(c, i) for i in range(rows)] for c in range(cols)]
+    sums = [[block_of(c, i)[k:] for i in range(rows)] for c in range(cols)]
     across = [summed([sums[c][i] for c in range(cols)]) for i in range(rows)]
     for c in range(cols):
         part = summed(sums[c])
@@ -175,54 +166,84 @@
         roots_ref[slot_of(c, cols)] = 1.0 / jnp.sqrt(part[:rows] + other)
 
 
-def send(vectors, copies_ref):
-    vectors = vectors.astype(BF16)
+def send(value, copies_ref):
     for n in range(copies_ref.shape[0]):
-        copies_ref[n] = vectors
-
-
-def first_step_kernel(sizes, all_ref, picked_ref, *refs):
-    rows, cols, _ = sizes
-    parts, (copies_ref, own_ref, roots_ref, scratch) = refs[:-4], refs[-4:]
+        copies_ref[n] = value
+
+
+def panel_gram(panels):
+    gram = None
+    for panel in panels:
+        term = dot(panel, panel, ((1,), (1,)), HIGHEST)
+        gram = term if gram is None else gram + term
+    return gram
+
+
+def start_kernel(sizes, low_ref, high_ref, picked_ref, vectors_ref, own_ref, roots_ref):
+    rows, cols, width = sizes
     k = own_ref.shape[0]
-    half = cols // 2
-    find_roots(sizes, k, all_ref, roots_ref)
+    half = low_ref.shape[1]
+
+    def block_of(c, i):
+        return low_ref.at[c, i] if i < half else high_ref.at[c, i - half]
+
+    find_roots(sizes, k, block_of, roots_ref)
+
+    def panel_of(c):
+        return lanes([block_of(c, i)[:k] for i in range(rows)])
+
+    factor = inverse_factor(panel_gram([panel_of(c) for c in range(cols)]))
     for c in range(cols):
         s = slot_of(c, cols)
+        panel = dot(factor, panel_of(c), ((1,), (0,)), HIGHEST)
         for i in range(rows):
-            value = all_ref[c, i, :k].astype(F32) * roots_ref[s, i : i + 1]
-            high = value.astype(BF16)
-            scratch[s, i, :k] = high
-            scratch[s, i, k:] = (value - high.astype(F32)).astype(BF16)
+            vectors_ref[s, i] = (roots_ref[s, i : i + 1] * panel[:, i * width : (i + 1) * width]).astype(BF16)
+    own_ref[...] = dot(factor, picked_ref[...], ((1,), (0,)), HIGHEST)
+
+
+def first_step_kernel(sizes, vectors_ref, own_ref, roots_ref, *refs):
+    parts, copies_ref = refs[:-1], refs[-1]
+    half = sizes[1] // 2
+    total = product(lambda s, x, i: vectors_ref[s * half + x, i], parts, sizes)
+    send(own_ref[...] + own_root(roots_ref) * total, copies_ref)
+
+
+def half_gram_kernel(sizes, same_ref, gram_ref):
+    rows, cols, _ = sizes
+    half = cols // 2
+    gram_ref[...] = panel_gram([lanes([same_ref[i * half + x] for i in range(rows)]) for x in range(half)])
+
+
+def next_image(sizes, same_ref, other_ref, gram_ref, roots_ref, parts, scratch):
+    rows, cols, width = sizes
+    half = cols // 2
+    refs = (same_ref, other_ref)
+
+    def panel_of(s, x):
+        return lanes([refs[s][i * half + x] for i in range(rows)])
+
+    factor = inverse_factor(gram_ref[...] + panel_gram([panel_of(1, x) for x in range(half)]))
+    for s in range(2):
+        for x in range(half):
+            panel = dot(factor, panel_of(s, x), ((1,), (0,)), HIGHEST)
+            for i in range(rows):
+                root = roots_ref[s * half + x, i : i + 1]
+                scratch[s * half + x, i] = (root * panel[:, i * width : (i + 1) * width]).astype(BF16)
     total = product(lambda s, x, i: scratch[s * half + x, i], parts, sizes)
-    root = own_root(roots_ref)
-    image = picked_ref[...] + root * (total[:k] + total[k:])
+    here = lax.axis_index("row") * half + lax.axis_index("col") // 2
+    return dot(factor, same_ref[here], ((1,), (0,)), HIGHEST) + own_root(roots_ref) * total
+
+
+def step_kernel(sizes, same_ref, other_ref, gram_ref, roots_ref, *refs):
+    parts, (copies_ref, scratch) = refs[:-2], refs[-2:]
+    send(next_image(sizes, same_ref, other_ref, gram_ref, roots_ref, parts, scratch), copies_ref)
+
+
+def last_step_kernel(sizes, same_ref, other_ref, gram_ref, roots_ref, *refs):
+    parts, (own_ref, grams_ref, scratch) = refs[:-3], refs[-3:]
+    image = next_image(sizes, same_ref, other_ref, gram_ref, roots_ref, parts, scratch)
     own_ref[...] = image
-    send(root * image, copies_ref)
-
-
-def next_image(sizes, same_ref, other_ref, before_ref, roots_ref, factor_ref, parts):
-    half = sizes[1] // 2
-    refs = (same_ref, other_ref)
-    total = product(lambda s, x, i: refs[s][i * half + x], parts, sizes)
-    image = before_ref[...] + own_root(roots_ref) * total
-    return dot(factor_ref[...], image, ((1,), (0,)), HIGHEST)
-
-
-def step_kernel(sizes, same_ref, other_ref, before_ref, roots_ref, factor_ref, *refs):
-    parts, (copies_ref, own_ref) = refs[:-2], refs[-2:]
-    image = next_image(sizes, same_ref, other_ref, before_ref, roots_ref, factor_ref, parts)
-    own_ref[...] = image
-    send(own_root(roots_ref) * image, copies_ref)
-
-
-def last_step_kernel(sizes, same_ref, other_ref, before_ref, roots_ref, factor_ref, *refs):
-    parts, (own_ref, gram_ref) = refs[:-2], refs[-2:]
-    image = next_image(sizes, same_ref, other_ref, before_ref, roots_ref, factor_ref, parts)
-    own_ref[...] = image
-    packed = pack_gram(dot(image, image, ((1,), (1,)), HIGHEST))
-    for n in range(gram_ref.shape[0]):
-        gram_ref[n] = packed
+    send(pack_gram(dot(image, image, ((1,), (1,)), HIGHEST)), grams_ref)
 
 
 def pack_gram(gram):
@@ -242,46 +263,8 @@
     return jnp.concatenate([lanes([upper, across]), lanes([cross, lower])], axis=0)
 
 
-def congruent(factor, gram):
-    half = dot(factor, gram, ((1,), (0,)), HIGHEST)
-    return dot(half, factor, ((1,), (1,)), HIGHEST)
-
-
-def first_factor_kernel(sizes, all_ref, factor_ref):
-    rows, cols, _ = sizes
-    k = factor_ref.shape[0]
-    gram = jnp.zeros((k, k), F32)
-    for c in range(cols):
-        panel = lanes([all_ref[c, i, :k].astype(F32) for i in range(rows)])
-        gram = gram + dot(panel, panel, ((1,), (1,)), HIGHEST)
-    factor_ref[...] = inverse_factor(gram)
-
-
-def factor_of(sizes, same_ref, other_ref, roots_ref, before_ref):
-    rows, cols, _ = sizes
-    half = cols // 2
-    k = before_ref.shape[0]
-    gram = jnp.zeros((k, k), F32)
-    for s, ref in enumerate((same_ref, other_ref)):
-        for x in range(half):
-            panel = lanes([ref[i * half + x].astype(F32) / roots_ref[s * half + x, i : i + 1] for i in range(rows)])
-            gram = gram + dot(panel, panel, ((1,), (1,)), HIGHEST)
-    return inverse_factor(congruent(before_ref[...], gram))
-
-
-def factor_kernel(sizes, same_ref, other_ref, roots_ref, before_ref, factor_ref):
-    factor_ref[...] = factor_of(sizes, same_ref, other_ref, roots_ref, before_ref)
-
-
-def last_factor_kernel(sizes, same_ref, other_ref, roots_ref, before_ref, image_ref, factor_ref, out_ref):
-    factor = factor_of(sizes, same_ref, other_ref, roots_ref, before_ref)
-    factor_ref[...] = factor
-    out_ref[...] = dot(factor, image_ref[...], ((1,), (0,)), HIGHEST)
-
-
-def finish_kernel(scale, same_ref, other_ref, factor_ref, image_ref, out_ref):
-    gram = unpack_gram(same_ref[...] + other_ref[...])
-    factor = inverse_factor(congruent(factor_ref[...], gram))
+def finish_kernel(scale, same_ref, other_ref, image_ref, out_ref):
+    factor = inverse_factor(unpack_gram(same_ref[...] + other_ref[...]))
     out_ref[...] = scale * dot(factor, image_ref[...], ((1,), (0,)), HIGHEST)
 
 
@@ -301,8 +284,10 @@
     )(*operands)
 
 
-def gather_start(copies):
-    return lax.all_gather(lax.all_to_all(copies, "row", 0, 0, tiled=True), "col", axis=0, tiled=False)
+def gather_start(copies, rows):
+    pieces = lax.all_to_all(copies, "row", 0, 0, tiled=True)
+    half = rows // 2
+    return [lax.all_gather(part, "col", axis=0, tiled=False) for part in (pieces[:half], pieces[half:])]
 
 
 def parities(rows, cols):
@@ -313,10 +298,9 @@
     return [(c, c + 1 - 2 * (c % 2)) for c in range(cols)]
 
 
-def gather_vectors(copies, rows, cols, factor):
+def gather_images(copies, rows, cols):
     same = lax.all_to_all(copies, ("row", "col"), 0, 0, tiled=True, axis_index_groups=parities(rows, cols))
-    same, factor = lax.optimization_barrier((same, factor))
-    return same, lax.ppermute(same, "col", swap(cols)), factor
+    return same, lax.ppermute(same, "col", swap(cols))
 
 
 def local(start_vectors, cluster_order, weights, block_mask):
@@ -328,13 +312,13 @@
         return lambda *refs: body(sizes, *refs)
 
     shape = jax.ShapeDtypeStruct
-    extra = -(-(rows + cols) // 16) * 16
+    extra = -(-(rows + cols) // 8) * 8
     to_rows, *to_cols, piece, picked = kernel_call(
         bound(prepare_kernel),
         [
             shape((rows, cols * width, width), BF16),
             *[shape((width, rows * width), BF16)] * cols,
-            shape((rows, k + 3 * extra, width), BF16),
+            shape((rows, k + extra, width), F32),
             shape((k, width), F32),
         ],
         block_mask[:, 0, :],
@@ -351,49 +335,40 @@
         space=pltpu.HBM,
         limit=60 << 20,
     )
-    everyone = gather_start(piece)
+    everyone = gather_start(piece, rows)
     parts = [lax.all_to_all(to_rows, "row", 0, 0, tiled=True), to_cols[0]]
     for distance in range(1, cols):
         parts.append(lax.ppermute(to_cols[distance], "col", [(c, (c + distance) % cols) for c in range(cols)]))
-    copies, own_shape = shape((rows * cols // 2, k, width), BF16), shape((k, width), F32)
-    factor_shape = shape((k, k), F32)
-    factor = kernel_call(bound(first_factor_kernel), [factor_shape], everyone)
-    everyone, factor = lax.optimization_barrier((everyone, factor))
-    sent, own, roots = kernel_call(
-        bound(first_step_kernel),
-        [copies, own_shape, shape((cols, rows, width), F32)],
-        everyone,
-        picked,
-        *parts,
-        scratch=[pltpu.VMEM((cols, rows, 2 * k, width), BF16)],
-    )
+    copies, own_shape = shape((rows * cols // 2, k, width), F32), shape((k, width), F32)
+    vectors_shape = shape((cols, rows, k, width), BF16)
+    vectors, own, roots = kernel_call(
+        bound(start_kernel), [vectors_shape, own_shape, shape((cols, rows, width), F32)], *everyone, picked
+    )
+    sent = kernel_call(bound(first_step_kernel), [copies], vectors, own, roots, *parts)
+    scratch = [pltpu.VMEM(vectors_shape.shape, BF16)]
     for step in range(1, ITERS):
-        same, other, factor = gather_vectors(sent, rows, cols, factor)
+        same, other = gather_images(sent, rows, cols)
+        gram = kernel_call(bound(half_gram_kernel), [shape((k, k), F32)], same)
         if step < ITERS - 1:
-            sent, own = kernel_call(
-                bound(step_kernel), [copies, own_shape], same, other, own, roots, factor, *parts
+            sent = kernel_call(
+                bound(step_kernel), [copies], same, other, gram, roots, *parts, scratch=scratch
             )
-            factor = kernel_call(bound(factor_kernel), [factor_shape], same, other, roots, factor)
         else:
-            own, gram = kernel_call(
+            own, grams = kernel_call(
                 bound(last_step_kernel),
                 [own_shape, shape((rows * cols // 2, 3 * k // 8, 2 * k), F32)],
                 same,
                 other,
-                own,
+                gram,
                 roots,
-                factor,
                 *parts,
+                scratch=scratch,
             )
-            factor, image = kernel_call(
-                bound(last_factor_kernel), [factor_shape, own_shape], same, other, roots, factor, own
-            )
-    gram = lax.all_to_all(gram, ("row", "col"), 0, 0, tiled=True, axis_index_groups=parities(rows, cols))
-    gram, factor = lax.optimization_barrier((gram, factor))
-    same = gram.sum(axis=0)
+    grams = lax.all_to_all(grams, ("row", "col"), 0, 0, tiled=True, axis_index_groups=parities(rows, cols))
+    same = grams.sum(axis=0)
     other = lax.ppermute(same, "col", swap(cols))
     scale = math.sqrt(width * rows * cols)
-    return kernel_call(lambda *refs: finish_kernel(scale, *refs), [own_shape], same, other, factor, image)
+    return kernel_call(lambda *refs: finish_kernel(scale, *refs), [own_shape], same, other, own)
 
 
 def solution(mesh):

time: 102 us -> 129 us (1.26)
  blocking collectives: 47.8 us -> 96.1 us
  waiting for transfers between devices: 18.9 us -> 3.86 us
  starting transfers between devices: 14 us -> 6.76 us
  Pallas kernels: 20.4 us -> 22.1 us
    all_to_all x2 -> x4, blocking collectives: 30.5 us -> 72.3 us  [the longest x2 41.5 us: gather_images(): lax.all_to_all(copies, ('row', 'col'), 0, 0, tiled=True, axis_index_group...]
    all_to_all x2 -> x0, waiting for transfers between devices: 12.3 us -> none  [the longest x1 7.11 us: gather_vectors(): lax.all_to_all(copies, ('row', 'col'), 0, 0, tiled=True, axis_index_group...]
    all_to_all x2 -> x0, starting transfers between devices: 7.25 us -> none  [the longest x1 3.7 us: local(): lax.all_to_all(gram, ('row', 'col'), 0, 0, tiled=True, axis_index_groups=...]
    all_gather x1 -> x2, blocking collectives: 17.3 us -> 23.7 us  [gather_start(): lax.all_gather(part, 'col', axis=0, tiled=False)]
    all_to_all x1, waiting for transfers between devices: 2.35 us -> 0.01 us  [local(): parts = [lax.all_to_all(to_rows, 'row', 0, 0, tiled=True), to_cols[0]]]
    pallas_call x8, Pallas kernels: 20.4 us -> 22.1 us  [kernel_call(): pl.pallas_call(body, out_shape=outs[0] if single else tuple(outs), in_spe...]
  transfers between devices with their start and end apart: 9 -> 7, of which waited for: 6 -> 3; matrix products, arithmetic and copies ran while one was open for 0% -> 0% of each run, Pallas kernels for 9% -> 5%
where the time goes in v5:
time: 129 us
  blocking collectives  96.1 us (74%)
  Pallas kernels  22.1 us (17%)
  starting transfers between devices  6.76 us (5%)
  waiting for transfers between devices  3.86 us (3%)
    all_to_all x2, blocking collectives, gather_images(): lax.all_to_all(copies, ('row', 'col'), 0, 0, tiled=True, axis_index_group...  41.5 us
    all_gather x2, blocking collectives, gather_start(): lax.all_gather(part, 'col', axis=0, tiled=False)  23.7 us
    pallas_call x8, Pallas kernels, kernel_call(): pl.pallas_call(body, out_shape=outs[0] if single else tuple(outs), in_spe...  22.1 us
    all_to_all x1, blocking collectives, gather_start(): pieces = lax.all_to_all(copies, 'row', 0, 0, tiled=True)  18.2 us
    all_to_all x1, blocking collectives, local(): lax.all_to_all(grams, ('row', 'col'), 0, 0, tiled=True, axis_index_groups...  12.7 us
    all_to_all x1, starting transfers between devices, local(): parts = [lax.all_to_all(to_rows, 'row', 0, 0, tiled=True), to_cols[0]]  3.69 us
    ppermute x3, starting transfers between devices, local(): lax.ppermute(to_cols[distance], 'col', [(c, (c + distance) % cols) for c...  2.99 us
    ppermute x2, waiting for transfers between devices, gather_images(): return (same, lax.ppermute(same, 'col', swap(cols)))  2.69 us
  transfers between devices with their start and end apart: 7, of which 3 were waited for; matrix products, arithmetic and copies ran while one was open for 0% of the time, Pallas kernels for 5%

profile of v5, /device:TPU:0, one launch (start us, length us, event | category | flops | bytes accessed | tf_op | source)
XLA Modules:
  0.0 129.0 jit_solution(14777611477945274830)
XLA Ops:
  0.0 3.5 %shard_map.46 = (bf16[8,512,128]{2,1,0:T(8,128)(2,1)}, bf16[128,1024]{1,0:T(8,128)(2,1)}, bf16[128,1024]{1,0:T(8,128)(2,1)}, bf16[128,1024]{1,0:T(8,128)(2,1)}, ...) custom-call(s32[4,8]{1,0:T(4,128)} %bitcast.7, bf16[512,1024]{1,0:T(8,128)(2,1)} %bitcast.6, ...), custom_call_target="tpu_custom_call" | custom-call | bytes 3539584 | tf_op jit(solution)/shard_map/pallas_call | solution.py:276
  3.5 18.2 %all_to_all.25 = f32[8,80,128]{2,1,0:T(8,128)S(1)} all-to-all(f32[8,80,128]{2,1,0:T(8,128)} %get-tuple-element.17), channel_id=1, replica_groups=mesh['row'=8,'col'=4] {'row'}, dimensions={0} | all-to-all | bytes 655360 | tf_op jit(solution)/shard_map/all_to_all | solution.py:288
  21.7 3.7 %all-to-all-start.1 = ((bf16[8,512,128]{2,1,0:T(8,128)(2,1)}), bf16[8,512,128]{2,1,0:T(8,128)(2,1)S(1)}, u32[]{:S(2)}, u32[]{:S(2)}) async-start(bf16[8,512,128]{2,1,0:T(8,128)(2,1)} %get-tuple-element.22), calls=%async_computation.1 | async-start | bytes 2097152 | tf_op jit(solution)/shard_map/all_to_all | solution.py:339
  25.4 0.0 copy-done.4
  25.4 0.1 collective-permute-start
  25.5 0.0 copy-done.3
  25.5 1.6 %collective-permute-start.1 = (bf16[128,1024]{1,0:T(8,128)(2,1)S(1)}, bf16[128,1024]{1,0:T(8,128)(2,1)S(1)}, u32[]{:S(2)}, u32[]{:S(2)}) collective-permute-start(bf16[128,1024]{1,0:T(8,128)(2,1)S(1)} %copy-done.3), channel_id=1, source_target_pairs={{0,2},{1,3},{2,0},{3,1},{4,6},{5,7},{6,4},{7,5},{8,10},{9,11},{10,... | collective-permute-start | bytes 786440 | tf_op jit(solution)/shard_map/ppermute | solution.py:341
  27.0 0.0 copy-done.2
  27.0 1.4 %collective-permute-start.2 = (bf16[128,1024]{1,0:T(8,128)(2,1)S(1)}, bf16[128,1024]{1,0:T(8,128)(2,1)S(1)}, u32[]{:S(2)}, u32[]{:S(2)}) collective-permute-start(bf16[128,1024]{1,0:T(8,128)(2,1)S(1)} %copy-done.2), channel_id=1, source_target_pairs={{0,3},{1,0},{2,1},{3,2},{4,7},{5,4},{6,5},{7,6},{8,11},{9,8},{10,9... | collective-permute-start | bytes 786440 | tf_op jit(solution)/shard_map/ppermute | solution.py:341
  28.4 15.6 %all-gather.1 = f32[16,80,128]{2,1,0:T(8,128)S(1)} all-gather(f32[4,80,128]{2,1,0:T(8,128)S(1)} %get-tuple-element.29), channel_id=3, replica_groups=mesh['row'=8,'col'=4] {'col'}, dimensions={0}, use_global_device_ids=true | all-gather | bytes 819200 | tf_op jit(solution)/shard_map/all_gather | solution.py:290
  44.1 8.1 %all-gather = f32[16,80,128]{2,1,0:T(8,128)S(1)} all-gather(f32[4,80,128]{2,1,0:T(8,128)S(1)} %get-tuple-element.30), channel_id=2, replica_groups=mesh['row'=8,'col'=4] {'col'}, dimensions={0}, use_global_device_ids=true | all-gather | bytes 819200 | tf_op jit(solution)/shard_map/all_gather | solution.py:290
  52.2 0.0 copy-done.1
  52.2 5.4 %shard_map.47 = (bf16[4,8,64,128]{3,2,1,0:T(8,128)(2,1)S(1)}, f32[64,128]{1,0:T(8,128)S(1)}, f32[4,8,128]{2,1,0:T(8,128)S(1)}) custom-call(f32[4,4,80,128]{3,2,1,0:T(8,128)S(1)} %bitcast.5, f32[4,4,80,128]{3,2,1,0:T(8,128)S(1)} %bitcast.4, f32[64,128]{1,0:T(8,128)S(1)} %copy-done.1), custom_call_target="tpu_custom_call" | custom-call | bytes 1916928 | tf_op jit(solution)/shard_map/pallas_call | solution.py:276
  57.5 0.0 collective-permute-done.refs_5_.refs_6_
  57.5 0.0 collective-permute-done.1.refs_6_.refs_7_
  57.6 0.0 collective-permute-done.2.refs_7_.refs_8_
  57.6 0.0 all-to-all-done.1.refs_3_.refs_4_
  57.6 0.7 shard_map.48
  58.3 22.2 %all_to_all.26.refs_0_ = f32[16,64,128]{2,1,0:T(8,128)S(1)} all-to-all(f32[16,64,128]{2,1,0:T(8,128)S(1)} %shard_map.48), channel_id=1, replica_groups={{0,2,4,6,8,10,12,14,16,18,20,22,24,26,28,30},{1,3,5,7,9,11,13,15,17,19,..., dimensions={0} | all-to-all | bytes 1048576 | tf_op jit(solution)/shard_map/all_to_all | solution.py:302
  80.5 0.0 collective-permute-start.3
  80.5 0.6 shard_map.49.refs_2_
  81.0 1.3 %collective-permute-done.3.refs_1_ = f32[16,64,128]{2,1,0:T(8,128)S(1)} collective-permute-done((f32[16,64,128]{2,1,0:T(8,128)S(1)}, f32[16,64,128]{2,1,0:T(8,128)S(1)}, u32[]{:S(2)}, u32[]{:S(2)}) %collective-permute-start.3) | collective-permute-done | bytes 524320 | tf_op jit(solution)/shard_map/ppermute | solution.py:303
  82.4 4.1 %shard_map.50 = f32[16,64,128]{2,1,0:T(8,128)S(1)} custom-call(f32[16,64,128]{2,1,0:T(8,128)S(1)} %all_to_all.26.refs_0_, f32[16,64,128]{2,1,0:T(8,128)S(1)} %collective-permute-done.3.refs_1_, f32[64,64]{1,0:T(8,128)S(1)} %shard_map.49.refs_2_, f32[4,8,128]{2,1,0:T(8,128)S(1)} %get-tuple-element.21.refs_2_.refs_3_, ...), custom_call_target="tpu_custom_call" | custom-call | bytes 3702784 | tf_op jit(solution)/shard_map/pallas_call | solution.py:276
  86.5 19.3 %all_to_all.27.refs_0_ = f32[16,64,128]{2,1,0:T(8,128)S(1)} all-to-all(f32[16,64,128]{2,1,0:T(8,128)S(1)} %shard_map.50), channel_id=1, replica_groups={{0,2,4,6,8,10,12,14,16,18,20,22,24,26,28,30},{1,3,5,7,9,11,13,15,17,19,..., dimensions={0} | all-to-all | bytes 1048576 | tf_op jit(solution)/shard_map/all_to_all | solution.py:302
  105.7 0.0 collective-permute-start.4
  105.8 0.6 shard_map.51.refs_2_
  106.3 1.3 %collective-permute-done.4.refs_1_ = f32[16,64,128]{2,1,0:T(8,128)S(1)} collective-permute-done((f32[16,64,128]{2,1,0:T(8,128)S(1)}, f32[16,64,128]{2,1,0:T(8,128)S(1)}, u32[]{:S(2)}, u32[]{:S(2)}) %collective-permute-start.4) | collective-permute-done | bytes 524320 | tf_op jit(solution)/shard_map/ppermute | solution.py:303
  107.7 4.3 %shard_map.52 = (f32[64,128]{1,0:T(8,128)S(1)}, f32[16,24,128]{2,1,0:T(8,128)S(1)}) custom-call(f32[16,64,128]{2,1,0:T(8,128)S(1)} %all_to_all.27.refs_0_, f32[16,64,128]{2,1,0:T(8,128)S(1)} %collective-permute-done.4.refs_1_, f32[64,64]{1,0:T(8,128)S(1)} %shard_map.51.refs_2_, f32[4,8,128]{2,1,0:T(8,128)S(1)} %get-tuple-element.21.refs_2_.refs_3_, ...), custom_call_target="tpu_custom_call" | custom-call | bytes 3407872 | tf_op jit(solution)/shard_map/pallas_call | solution.py:276
  112.0 12.7 %all_to_all.28 = f32[16,24,128]{2,1,0:T(8,128)S(1)} all-to-all(f32[16,24,128]{2,1,0:T(8,128)S(1)} %get-tuple-element.27), channel_id=1, replica_groups={{0,2,4,6,8,10,12,14,16,18,20,22,24,26,28,30},{1,3,5,7,9,11,13,15,17,19,..., dimensions={0} | all-to-all | bytes 393216 | tf_op jit(solution)/shard_map/all_to_all | solution.py:367
  124.7 0.1 collective-permute-start.5
  124.8 1.2 collective-permute-done.5.refs_1_
  126.0 3.0 %shard_map.53 = f32[64,128]{1,0:T(8,128)} custom-call(f32[24,128]{1,0:T(8,128)S(1)} %reduce_sum.9.refs_0_, f32[24,128]{1,0:T(8,128)S(1)} %collective-permute-done.5.refs_1_, f32[64,128]{1,0:T(8,128)S(1)} %get-tuple-element.28.refs_2_), custom_call_target="tpu_custom_call" | custom-call | bytes 90112 | tf_op jit(solution)/shard_map/pallas_call | solution.py:276
  (8 shorter events, 0.1 us)
Async XLA Ops:
  21.7 3.7 %copy-start.4 = (bf16[128,1024]{1,0:T(8,128)(2,1)S(1)}, bf16[128,1024]{1,0:T(8,128)(2,1)}, u32[]{:S(2)}) copy-start(bf16[128,1024]{1,0:T(8,128)(2,1)} %get-tuple-element.24) | copy-start | bytes 786436
  21.7 3.8 %copy-start.3 = (bf16[128,1024]{1,0:T(8,128)(2,1)S(1)}, bf16[128,1024]{1,0:T(8,128)(2,1)}, u32[]{:S(2)}) copy-start(bf16[128,1024]{1,0:T(8,128)(2,1)} %get-tuple-element.25) | copy-start | bytes 786436
  21.7 5.3 %copy-start.2 = (bf16[128,1024]{1,0:T(8,128)(2,1)S(1)}, bf16[128,1024]{1,0:T(8,128)(2,1)}, u32[]{:S(2)}) copy-start(bf16[128,1024]{1,0:T(8,128)(2,1)} %get-tuple-element.26) | copy-start | bytes 786436
  21.7 35.9 %all-to-all-start.1 = ((bf16[8,512,128]{2,1,0:T(8,128)(2,1)}), bf16[8,512,128]{2,1,0:T(8,128)(2,1)S(1)}, u32[]{:S(2)}, u32[]{:S(2)}) async-start(bf16[8,512,128]{2,1,0:T(8,128)(2,1)} %get-tuple-element.22), calls=%async_computation.1 | async-start | bytes 2097152 | tf_op jit(solution)/shard_map/all_to_all | solution.py:339
  25.4 32.1 %collective-permute-start = (bf16[128,1024]{1,0:T(8,128)(2,1)S(1)}, bf16[128,1024]{1,0:T(8,128)(2,1)S(1)}, u32[]{:S(2)}, u32[]{:S(2)}) collective-permute-start(bf16[128,1024]{1,0:T(8,128)(2,1)S(1)} %copy-done.4), channel_id=1, source_target_pairs={{0,1},{1,2},{2,3},{3,0},{4,5},{5,6},{6,7},{7,4},{8,9},{9,10},{10,1... | collective-permute-start | bytes 786440 | tf_op jit(solution)/shard_map/ppermute | solution.py:341
  25.5 32.1 %collective-permute-start.1 = (bf16[128,1024]{1,0:T(8,128)(2,1)S(1)}, bf16[128,1024]{1,0:T(8,128)(2,1)S(1)}, u32[]{:S(2)}, u32[]{:S(2)}) collective-permute-start(bf16[128,1024]{1,0:T(8,128)(2,1)S(1)} %copy-done.3), channel_id=1, source_target_pairs={{0,2},{1,3},{2,0},{3,1},{4,6},{5,7},{6,4},{7,5},{8,10},{9,11},{10,... | collective-permute-start | bytes 786440 | tf_op jit(solution)/shard_map/ppermute | solution.py:341
  27.0 30.5 %collective-permute-start.2 = (bf16[128,1024]{1,0:T(8,128)(2,1)S(1)}, bf16[128,1024]{1,0:T(8,128)(2,1)S(1)}, u32[]{:S(2)}, u32[]{:S(2)}) collective-permute-start(bf16[128,1024]{1,0:T(8,128)(2,1)S(1)} %copy-done.2), channel_id=1, source_target_pairs={{0,3},{1,0},{2,1},{3,2},{4,7},{5,4},{6,5},{7,6},{8,11},{9,8},{10,9... | collective-permute-start | bytes 786440 | tf_op jit(solution)/shard_map/ppermute | solution.py:341
  44.1 8.1 %copy-start.1 = (f32[64,128]{1,0:T(8,128)S(1)}, f32[64,128]{1,0:T(8,128)}, u32[]{:S(2)}) copy-start(f32[64,128]{1,0:T(8,128)} %get-tuple-element.18.refs_2_) | copy-start | bytes 98308
  52.2 5.4 %copy-start = (bf16[128,1024]{1,0:T(8,128)(2,1)S(1)}, bf16[128,1024]{1,0:T(8,128)(2,1)}, u32[]{:S(2)}) copy-start(bf16[128,1024]{1,0:T(8,128)(2,1)} %get-tuple-element.23.refs_4_.refs_5_) | copy-start | bytes 786436
  80.5 1.9 %collective-permute-start.3 = (f32[16,64,128]{2,1,0:T(8,128)S(1)}, f32[16,64,128]{2,1,0:T(8,128)S(1)}, u32[]{:S(2)}, u32[]{:S(2)}) collective-permute-start(f32[16,64,128]{2,1,0:T(8,128)S(1)} %all_to_all.26.refs_0_), channel_id=1, source_target_pairs={{0,1},{1,0},{2,3},{3,2},{4,5},{5,4},{6,7},{7,6},{8,9},{9,8},{10,11... | collective-permute-start | bytes 1572872 | tf_op jit(solution)/shard_map/ppermute | solution.py:303
  105.7 1.9 %collective-permute-start.4 = (f32[16,64,128]{2,1,0:T(8,128)S(1)}, f32[16,64,128]{2,1,0:T(8,128)S(1)}, u32[]{:S(2)}, u32[]{:S(2)}) collective-permute-start(f32[16,64,128]{2,1,0:T(8,128)S(1)} %all_to_all.27.refs_0_), channel_id=1, source_target_pairs={{0,1},{1,0},{2,3},{3,2},{4,5},{5,4},{6,7},{7,6},{8,9},{9,8},{10,11... | collective-permute-start | bytes 1572872 | tf_op jit(solution)/shard_map/ppermute | solution.py:303
  124.7 1.2 collective-permute-start.5

commit v6 on v5

--- a/solution.py
+++ b/solution.py
@@ -68,10 +68,10 @@
     return other * (cols // 2) + column // 2
 
 
-def prepare_kernel(sizes, mask_hbm, stored_hbm, start_hbm, order_hbm, to_rows_ref, *refs):
+def prepare_kernel(sizes, mask_hbm, stored_hbm, start_hbm, order_hbm, *refs):
     rows, cols, width = sizes
-    to_cols, (piece_ref, picked_ref) = refs[:cols], refs[cols : cols + 2]
-    mask_ref, stored_ref, start_ref, order_ref, arrived = refs[cols + 2 :]
+    to_rows, to_cols_ref = refs[:rows], refs[rows]
+    piece_ref, picked_ref, mask_ref, stored_ref, start_ref, order_ref, sums_ref, arrived = refs[rows + 1 :]
     here_row, here_col = lax.axis_index("row"), lax.axis_index("col")
     columns = slots(cols)
     copies = [
@@ -101,20 +101,20 @@
         lines[s].wait()
         row_block = here_row * cols + columns[s]
         line = []
-        for i in range(rows):
+        for distance in range(rows):
+            i = lax.rem(here_row + distance, rows)
             col_block = i * cols + here_col
             whole = jnp.where((mask_ref[columns[s], i] > 0) & (row_block < col_block), 1.0, 0.0)
             partly = jnp.where(row_block == col_block, 1.0, 0.0)
             keep = (whole + partly * upper).astype(BF16)
-            line.append(stored_ref[s, :, i * width : (i + 1) * width] * keep)
-            to_rows_ref[i, s * width : (s + 1) * width] = line[i]
+            line.append(stored_ref[s, :, pl.ds(pl.multiple_of(i * width, width), width)] * keep)
+            to_rows[distance][s * width : (s + 1) * width] = line[-1]
+            to_cols_ref[columns[s], :, distance * width : (distance + 1) * width] = line[-1]
         line_degrees.append(dot(ones, lanes(line), ((1,), (1,)))[0:1])
-    for distance in range(cols):
-        s = slot_of(lax.rem(here_col + distance, cols), cols)
-        from_line = pl.ds(pl.multiple_of(s * width, width), width)
-        for i in range(rows):
-            to_cols[distance][:, i * width : (i + 1) * width] = to_rows_ref[i, from_line]
-    degrees = [dot(ones[:, : cols * width], to_rows_ref[i], ((1,), (0,)))[0:1] for i in range(rows)]
+    for distance in range(rows):
+        part = dot(ones[:, : cols * width], to_rows[distance][...], ((1,), (0,)))
+        sums_ref[pl.ds(lax.rem(here_row + distance, rows), 1)] = part[0:1]
+    degrees = [sums_ref[...]]
     swapped = line_degrees[cols // 2 :] + line_degrees[: cols // 2]
     odd = lax.rem(here_col, 2) == 1
     for c in range(cols):
@@ -124,29 +124,38 @@
     spare = piece_ref.shape[-2] - k - rows - cols
     if spare:
         degrees.append(jnp.zeros((spare, width), F32))
-    degrees = jnp.concatenate(degrees, axis=0)
-    for i in range(rows):
-        piece_ref[i, :k] = picked
-        piece_ref[i, k:] = degrees
+    piece_ref[:k] = picked
+    piece_ref[k:] = jnp.concatenate(degrees, axis=0)
 
 
 def product(vectors_of, parts, sizes):
     rows, cols, _ = sizes
-    here_col = lax.axis_index("col")
+    here_row, here_col = lax.axis_index("row"), lax.axis_index("col")
     total = None
     for distance in range(cols):
         column = lax.rem(here_col + (cols - distance), cols)
-        vectors = lanes([vectors_of(distance % 2, column // 2, i) for i in range(rows)])
-        term = dot(vectors, parts[1 + distance][...], ((1,), (1,)))
+        sources = [lax.rem(here_row + i, rows) for i in range(rows)]
+        vectors = lanes([vectors_of(distance % 2, column // 2, i) for i in sources])
+        term = dot(vectors, parts[rows][column], ((1,), (1,)))
         total = term if total is None else total + term
-    for i in range(rows):
+    for distance in range(rows):
+        i = lax.rem(here_row + (rows - distance), rows)
         vectors = lanes([vectors_of(s, x, i) for s in range(2) for x in range(cols // 2)])
-        total = total + dot(vectors, parts[0][i], ((1,), (0,)))
+        total = total + dot(vectors, parts[distance][...], ((1,), (0,)))
     return total
 
 
 def own_root(roots_ref):
     return roots_ref[lax.axis_index("col") // 2, pl.ds(lax.axis_index("row"), 1)]
+
+
+def slot_rows(rows):
+    here = lax.axis_index("row")
+    found = []
+    for distance in range(0, rows, 2):
+        row = lax.rem(here + (rows - distance), rows)
+        found += [row, row + 1 - 2 * lax.rem(row, 2)]
+    return found
 
 
 def find_roots(sizes, k, block_of, roots_ref):
@@ -158,12 +167,13 @@
             total = total + term
         return total
 
-    sums = [[block_of(c, i)[k:] for i in range(rows)] for c in range(cols)]
-    across = [summed([sums[c][i] for c in range(cols)]) for i in range(rows)]
+    sums = [[block_of(c, n)[k:] for n in range(rows)] for c in range(cols)]
+    across = [summed([sums[c][n] for c in range(cols)]) for n in range(rows)]
     for c in range(cols):
-        part = summed(sums[c])
-        other = jnp.concatenate([across[i][rows + c : rows + c + 1] for i in range(rows)], axis=0)
-        roots_ref[slot_of(c, cols)] = 1.0 / jnp.sqrt(part[:rows] + other)
+        s = slot_of(c, cols)
+        for n, place in enumerate(slot_rows(rows)):
+            roots_ref[s, pl.ds(place, 1)] = across[n][rows + c : rows + c + 1]
+        roots_ref[s] = 1.0 / jnp.sqrt(roots_ref[s] + summed(sums[c])[:rows])
 
 
 def send(value, copies_ref):
@@ -179,9 +189,10 @@
     return gram
 
 
-def start_kernel(sizes, low_ref, high_ref, picked_ref, vectors_ref, own_ref, roots_ref):
+def first_step_kernel(sizes, low_ref, high_ref, picked_ref, *refs):
     rows, cols, width = sizes
-    k = own_ref.shape[0]
+    parts, (copies_ref, roots_ref, vectors_ref) = refs[:-3], refs[-3:]
+    k = picked_ref.shape[0]
     half = low_ref.shape[1]
 
     def block_of(c, i):
@@ -196,16 +207,12 @@
     for c in range(cols):
         s = slot_of(c, cols)
         panel = dot(factor, panel_of(c), ((1,), (0,)), HIGHEST)
-        for i in range(rows):
-            vectors_ref[s, i] = (roots_ref[s, i : i + 1] * panel[:, i * width : (i + 1) * width]).astype(BF16)
-    own_ref[...] = dot(factor, picked_ref[...], ((1,), (0,)), HIGHEST)
-
-
-def first_step_kernel(sizes, vectors_ref, own_ref, roots_ref, *refs):
-    parts, copies_ref = refs[:-1], refs[-1]
-    half = sizes[1] // 2
-    total = product(lambda s, x, i: vectors_ref[s * half + x, i], parts, sizes)
-    send(own_ref[...] + own_root(roots_ref) * total, copies_ref)
+        for n, place in enumerate(slot_rows(rows)):
+            root = roots_ref[s, pl.ds(place, 1)]
+            vectors_ref[s, place] = (root * panel[:, n * width : (n + 1) * width]).astype(BF16)
+    total = product(lambda s, x, i: vectors_ref[s * (cols // 2) + x, i], parts, sizes)
+    own = dot(factor, picked_ref[...], ((1,), (0,)), HIGHEST)
+    send(own + own_root(roots_ref) * total, copies_ref)
 
 
 def half_gram_kernel(sizes, same_ref, gram_ref):
@@ -284,10 +291,12 @@
     )(*operands)
 
 
-def gather_start(copies, rows):
-    pieces = lax.all_to_all(copies, "row", 0, 0, tiled=True)
-    half = rows // 2
-    return [lax.all_gather(part, "col", axis=0, tiled=False) for part in (pieces[:half], pieces[half:])]
+def pass_start(piece, rows):
+    pieces = jnp.stack([piece, lax.ppermute(piece, "row", [(i, i + 1 - 2 * (i % 2)) for i in range(rows)])])
+    return [pieces] + [
+        lax.ppermute(pieces, "row", [(i, (i + distance) % rows) for i in range(rows)])
+        for distance in range(2, rows, 2)
+    ]
 
 
 def parities(rows, cols):
@@ -301,6 +310,18 @@
 def gather_images(copies, rows, cols):
     same = lax.all_to_all(copies, ("row", "col"), 0, 0, tiled=True, axis_index_groups=parities(rows, cols))
     return same, lax.ppermute(same, "col", swap(cols))
+
+
+def move_up(part, rows, distance):
+    return lax.ppermute(part, "row", [(i, i + distance) for i in range(rows - distance)])
+
+
+def exchange(parts, rows, cols, near):
+    parts = list(parts)
+    for distance in range(near + 1, rows):
+        parts[distance] = move_up(parts[distance], rows, distance)
+    parts[rows] = lax.all_to_all(parts[rows], "col", 0, 0, tiled=True)
+    return parts
 
 
 def local(start_vectors, cluster_order, weights, block_mask):
@@ -313,12 +334,12 @@
 
     shape = jax.ShapeDtypeStruct
     extra = -(-(rows + cols) // 8) * 8
-    to_rows, *to_cols, piece, picked = kernel_call(
+    *parts, piece, picked = kernel_call(
         bound(prepare_kernel),
         [
-            shape((rows, cols * width, width), BF16),
-            *[shape((width, rows * width), BF16)] * cols,
-            shape((rows, k + extra, width), F32),
+            *[shape((cols * width, width), BF16)] * rows,
+            shape((cols, width, rows * width), BF16),
+            shape((k + extra, width), F32),
             shape((k, width), F32),
         ],
         block_mask[:, 0, :],
@@ -330,22 +351,29 @@
             pltpu.VMEM((cols, width, rows * width), BF16),
             pltpu.VMEM((k, width), F32),
             pltpu.VMEM((1, width), jnp.int32),
+            pltpu.VMEM((rows, width), F32),
             pltpu.SemaphoreType.DMA((cols + 3,)),
         ],
         space=pltpu.HBM,
         limit=60 << 20,
     )
-    everyone = gather_start(piece, rows)
-    parts = [lax.all_to_all(to_rows, "row", 0, 0, tiled=True), to_cols[0]]
-    for distance in range(1, cols):
-        parts.append(lax.ppermute(to_cols[distance], "col", [(c, (c + distance) % cols) for c in range(cols)]))
+    groups = pass_start(piece, rows)
+    parts = list(parts)
+    groups[0], *tied = lax.optimization_barrier([groups[0], *parts[1:rows]])
+    parts[1:rows] = tied
+    near = 2
+    parts = exchange(parts, rows, cols, near)
+    middle = len(groups) // 2
+    everyone = [
+        lax.all_gather(jnp.concatenate(part), "col", axis=0, tiled=False) for part in (groups[:middle], groups[middle:])
+    ]
+    everyone[0], *tied = lax.optimization_barrier([everyone[0], *parts[1 : near + 1]])
+    parts[1 : near + 1] = [move_up(part, rows, 1 + n) for n, part in enumerate(tied)]
     copies, own_shape = shape((rows * cols // 2, k, width), F32), shape((k, width), F32)
-    vectors_shape = shape((cols, rows, k, width), BF16)
-    vectors, own, roots = kernel_call(
-        bound(start_kernel), [vectors_shape, own_shape, shape((cols, rows, width), F32)], *everyone, picked
+    scratch = [pltpu.VMEM((cols, rows, k, width), BF16)]
+    sent, roots = kernel_call(
+        bound(first_step_kernel), [copies, shape((cols, rows, width), F32)], *everyone, picked, *parts, scratch=scratch
     )
-    sent = kernel_call(bound(first_step_kernel), [copies], vectors, own, roots, *parts)
-    scratch = [pltpu.VMEM(vectors_shape.shape, BF16)]
     for step in range(1, ITERS):
         same, other = gather_images(sent, rows, cols)
         gram = kernel_call(bound(half_gram_kernel), [shape((k, k), F32)], same)

time: 129 us -> 125 us (0.969)
  blocking collectives: 96.1 us -> 66.9 us
  starting transfers between devices: 6.76 us -> 28.9 us
  waiting for transfers between devices: 3.86 us -> 6.07 us
    ppermute x3 -> x11, starting transfers between devices: 2.99 us -> 25.2 us  [the longest x7 17 us: move_up(): lax.ppermute(part, 'row', [(i, i + distance) for i in range(rows - distan...]
    all_to_all x1 -> x0, blocking collectives: 18.2 us -> none  [gather_start(): pieces = lax.all_to_all(copies, 'row', 0, 0, tiled=True)]
    all_gather x2, blocking collectives: 23.7 us -> 15.9 us  [local(): lax.all_gather(jnp.concatenate(part), 'col', axis=0, tiled=False)]
    all_to_all x2, blocking collectives: 41.5 us -> 38.3 us  [gather_images(): lax.all_to_all(copies, ('row', 'col'), 0, 0, tiled=True, axis_index_group...]
    ppermute x3 -> x11, waiting for transfers between devices: 0.01 us -> 2.22 us  [the longest x1 2.19 us: pass_start(): lax.ppermute(piece, 'row', [(i, i + 1 - 2 * (i % 2)) for i in range(rows)])]
    pallas_call x8 -> x7, Pallas kernels: 22.1 us -> 21.8 us  [kernel_call(): pl.pallas_call(body, out_shape=outs[0] if single else tuple(outs), in_spe...]
  transfers between devices with their start and end apart: 7 -> 15, of which waited for: 3 -> 4; matrix products, arithmetic and copies ran while one was open for 0% -> 0% of each run, Pallas kernels for 5% -> 1%
where the time goes in v6:
time: 125 us
  blocking collectives  66.9 us (54%)
  starting transfers between devices  28.9 us (23%)
  Pallas kernels  21.8 us (17%)
  waiting for transfers between devices  6.07 us (5%)
    all_to_all x2, blocking collectives, gather_images(): lax.all_to_all(copies, ('row', 'col'), 0, 0, tiled=True, axis_index_group...  38.3 us
    pallas_call x7, Pallas kernels, kernel_call(): pl.pallas_call(body, out_shape=outs[0] if single else tuple(outs), in_spe...  21.8 us
    ppermute x7, starting transfers between devices, move_up(): lax.ppermute(part, 'row', [(i, i + distance) for i in range(rows - distan...  17 us
    all_gather x2, blocking collectives, local(): lax.all_gather(jnp.concatenate(part), 'col', axis=0, tiled=False)  15.9 us
    all_to_all x1, blocking collectives, local(): lax.all_to_all(grams, ('row', 'col'), 0, 0, tiled=True, axis_index_groups...  12.7 us
    ppermute x3, starting transfers between devices, pass_start(): lax.ppermute(pieces, 'row', [(i, (i + distance) % rows) for i in range(ro...  5.17 us
    all_to_all x1, starting transfers between devices, exchange(): parts[rows] = lax.all_to_all(parts[rows], 'col', 0, 0, tiled=True)  3.65 us
    ppermute x1, starting transfers between devices, pass_start(): lax.ppermute(piece, 'row', [(i, i + 1 - 2 * (i % 2)) for i in range(rows)])  3.04 us
  transfers between devices with their start and end apart: 15, of which 4 were waited for; matrix products, arithmetic and copies ran while one was open for 0% of the time, Pallas kernels for 1%

profile of v6, /device:TPU:0, one launch (start us, length us, event | category | flops | bytes accessed | tf_op | source)
XLA Modules:
  0.0 124.9 jit_solution(15467488123467068774)
XLA Ops:
  0.0 3.3 %shard_map.46 = (bf16[512,128]{1,0:T(8,128)(2,1)}, bf16[512,128]{1,0:T(8,128)(2,1)}, bf16[512,128]{1,0:T(8,128)(2,1)}, bf16[512,128]{1,0:T(8,128)(2,1)}, bf16[51...) custom-call(s32[4,8]{1,0:T(4,128)} %bitcast.11, ...), custom_call_target="tpu_custom_call" | custom-call | bytes 3252864 | tf_op jit(solution)/shard_map/pallas_call | solution.py:283
  3.3 3.0 %collective-permute-start = (f32[80,128]{1,0:T(8,128)}, f32[80,128]{1,0:T(8,128)S(1)}, u32[]{:S(2)}, u32[]{:S(2)}) collective-permute-start(f32[80,128]{1,0:T(8,128)} %get-tuple-element.31), channel_id=1, source_target_pairs={{0,4},{4,0},{8,12},{12,8},{16,20},{20,16},{24,28},{28,24},{1,5},{5... | collective-permute-start | bytes 122888 | tf_op jit(solution)/shard_map/ppermute | solution.py:295
  6.3 2.2 %collective-permute-done = f32[80,128]{1,0:T(8,128)S(1)} collective-permute-done((f32[80,128]{1,0:T(8,128)}, f32[80,128]{1,0:T(8,128)S(1)}, u32[]{:S(2)}, u32[]{:S(2)}) %collective-permute-start) | collective-permute-done | bytes 40992 | tf_op jit(solution)/shard_map/ppermute | solution.py:295
  8.5 0.8 pad_maximum_fusion.2
  9.3 2.1 %collective-permute-start.1 = (f32[2,80,128]{2,1,0:T(8,128)S(1)}, f32[2,80,128]{2,1,0:T(8,128)S(1)}, u32[]{:S(2)}, u32[]{:S(2)}) collective-permute-start(f32[2,80,128]{2,1,0:T(8,128)S(1)} %pad_maximum_fusion.2), channel_id=1, source_target_pairs={{0,8},{4,12},{8,16},{12,20},{16,24},{20,28},{24,0},{28,4},{1,9},{5... | collective-permute-start | bytes 245768 | tf_op jit(solution)/shard_map/ppermute | solution.py:297
  11.4 3.6 %all-to-all-start = ((bf16[4,128,1024]{2,1,0:T(8,128)(2,1)}), bf16[4,128,1024]{2,1,0:T(8,128)(2,1)S(1)}, u32[]{:S(2)}, u32[]{:S(2)}) async-start(bf16[4,128,1024]{2,1,0:T(8,128)(2,1)} %get-tuple-element.52), calls=%async_computation | async-start | bytes 2097152 | tf_op jit(solution)/shard_map/all_to_all | solution.py:323
  15.0 2.1 %collective-permute-start.3 = (f32[2,80,128]{2,1,0:T(8,128)S(1)}, f32[2,80,128]{2,1,0:T(8,128)S(1)}, u32[]{:S(2)}, u32[]{:S(2)}) collective-permute-start(f32[2,80,128]{2,1,0:T(8,128)S(1)} %pad_maximum_fusion.2), channel_id=1, source_target_pairs={{0,24},{4,28},{8,0},{12,4},{16,8},{20,12},{24,16},{28,20},{1,25},{... | collective-permute-start | bytes 245768 | tf_op jit(solution)/shard_map/ppermute | solution.py:297
  17.1 1.0 collective-permute-start.2
  18.1 4.4 %collective-permute-start.6 = (bf16[512,128]{1,0:T(8,128)(2,1)S(1)}, bf16[512,128]{1,0:T(8,128)(2,1)S(1)}, u32[]{:S(2)}, u32[]{:S(2)}) collective-permute-start(bf16[512,128]{1,0:T(8,128)(2,1)S(1)} %copy-done.7), channel_id=1, source_target_pairs={{0,12},{4,16},{8,20},{12,24},{16,28},{1,13},{5,17},{9,21},{13,25},... | collective-permute-start | bytes 393224 | tf_op jit(solution)/shard_map/ppermute | solution.py:316
  22.6 2.3 %collective-permute-start.7 = (bf16[512,128]{1,0:T(8,128)(2,1)S(1)}, bf16[512,128]{1,0:T(8,128)(2,1)S(1)}, u32[]{:S(2)}, u32[]{:S(2)}) collective-permute-start(bf16[512,128]{1,0:T(8,128)(2,1)S(1)} %copy-done.6), channel_id=1, source_target_pairs={{0,16},{4,20},{8,24},{12,28},{1,17},{5,21},{9,25},{13,29},{2,18},{... | collective-permute-start | bytes 393224 | tf_op jit(solution)/shard_map/ppermute | solution.py:316
  24.8 1.3 %collective-permute-start.8 = (bf16[512,128]{1,0:T(8,128)(2,1)}, bf16[512,128]{1,0:T(8,128)(2,1)S(1)}, u32[]{:S(2)}, u32[]{:S(2)}) collective-permute-start(bf16[512,128]{1,0:T(8,128)(2,1)} %get-tuple-element.49), channel_id=1, source_target_pairs={{0,20},{4,24},{8,28},{1,21},{5,25},{9,29},{2,22},{6,26},{10,30},{3... | collective-permute-start | bytes 393224 | tf_op jit(solution)/shard_map/ppermute | solution.py:316
  26.2 8.5 %all-gather = f32[16,80,128]{2,1,0:T(8,128)S(1)} all-gather(f32[4,80,128]{2,1,0:T(8,128)S(1)} %pad_maximum_fusion), channel_id=2, replica_groups=mesh['row'=8,'col'=4] {'col'}, dimensions={0}, use_global_device_ids=true | all-gather | bytes 819200 | tf_op jit(solution)/shard_map/all_gather | solution.py:368
  34.7 3.3 %collective-permute-start.9 = (bf16[512,128]{1,0:T(8,128)(2,1)S(1)}, bf16[512,128]{1,0:T(8,128)(2,1)S(1)}, u32[]{:S(2)}, u32[]{:S(2)}) collective-permute-start(bf16[512,128]{1,0:T(8,128)(2,1)S(1)} %copy-done.5), channel_id=1, source_target_pairs={{0,24},{4,28},{1,25},{5,29},{2,26},{6,30},{3,27},{7,31}} | collective-permute-start | bytes 393224 | tf_op jit(solution)/shard_map/ppermute | solution.py:316
  38.0 2.4 %collective-permute-start.10 = (bf16[512,128]{1,0:T(8,128)(2,1)S(1)}, bf16[512,128]{1,0:T(8,128)(2,1)S(1)}, u32[]{:S(2)}, u32[]{:S(2)}) collective-permute-start(bf16[512,128]{1,0:T(8,128)(2,1)S(1)} %copy-done.4), channel_id=1, source_target_pairs={{0,28},{1,29},{2,30},{3,31}} | collective-permute-start | bytes 393224 | tf_op jit(solution)/shard_map/ppermute | solution.py:316
  40.5 0.0 copy-start.1
  40.5 2.0 %collective-permute-start.4 = (bf16[512,128]{1,0:T(8,128)(2,1)S(1)}, bf16[512,128]{1,0:T(8,128)(2,1)S(1)}, u32[]{:S(2)}, u32[]{:S(2)}) collective-permute-start(bf16[512,128]{1,0:T(8,128)(2,1)S(1)} %copy-done.3), channel_id=1, source_target_pairs={{0,4},{4,8},{8,12},{12,16},{16,20},{20,24},{24,28},{1,5},{5,9},{9,... | collective-permute-start | bytes 393224 | tf_op jit(solution)/shard_map/ppermute | solution.py:316
  42.5 0.0 collective-permute-done.7.refs_7_.refs_8_
  42.5 1.3 %collective-permute-start.5 = (bf16[512,128]{1,0:T(8,128)(2,1)S(1)}, bf16[512,128]{1,0:T(8,128)(2,1)S(1)}, u32[]{:S(2)}, u32[]{:S(2)}) collective-permute-start(bf16[512,128]{1,0:T(8,128)(2,1)S(1)} %copy-done.2), channel_id=1, source_target_pairs={{0,8},{4,12},{8,16},{12,20},{16,24},{20,28},{1,9},{5,13},{9,17},{1... | collective-permute-start | bytes 393224 | tf_op jit(solution)/shard_map/ppermute | solution.py:316
  43.8 7.4 %all-gather.1 = f32[16,80,128]{2,1,0:T(8,128)S(1)} all-gather(f32[4,80,128]{2,1,0:T(8,128)S(1)} %pad_maximum_fusion.1), channel_id=3, replica_groups=mesh['row'=8,'col'=4] {'col'}, dimensions={0}, use_global_device_ids=true | all-gather | bytes 819200 | tf_op jit(solution)/shard_map/all_gather | solution.py:368
  51.3 6.0 %shard_map.47 = (f32[16,64,128]{2,1,0:T(8,128)S(1)}, f32[4,8,128]{2,1,0:T(8,128)S(1)}) custom-call(f32[4,4,80,128]{3,2,1,0:T(8,128)S(1)} %bitcast.6, f32[4,4,80,128]{3,2,1,0:T(8,128)S(1)} %bitcast.7, f32[64,128]{1,0:T(8,128)S(1)} %copy-done.1, bf16[512,128]{1,0:T(8,128)(2,1)S(1)} %copy-done, bf16[512,128]{1,0:T(8,128)(2,1)S(1)} %collective-permute-done.4.refs_4_.refs_5_, ...), custom_call_target="tpu_custom_call" | custom-call | bytes 3981312 | tf_op jit(solution)/shard_map/pallas_call | solution.py:283
  57.3 19.1 %all_to_all.20.refs_0_ = f32[16,64,128]{2,1,0:T(8,128)S(1)} all-to-all(f32[16,64,128]{2,1,0:T(8,128)S(1)} %get-tuple-element.53), channel_id=1, replica_groups={{0,2,4,6,8,10,12,14,16,18,20,22,24,26,28,30},{1,3,5,7,9,11,13,15,17,19,..., dimensions={0} | all-to-all | bytes 1048576 | tf_op jit(solution)/shard_map/all_to_all | solution.py:311
  76.4 0.6 shard_map.48.refs_2_
  77.0 1.3 %collective-permute-done.11.refs_1_ = f32[16,64,128]{2,1,0:T(8,128)S(1)} collective-permute-done((f32[16,64,128]{2,1,0:T(8,128)S(1)}, f32[16,64,128]{2,1,0:T(8,128)S(1)}, u32[]{:S(2)}, u32[]{:S(2)}) %collective-permute-start.11) | collective-permute-done | bytes 524320 | tf_op jit(solution)/shard_map/ppermute | solution.py:312
  78.3 4.1 %shard_map.49 = f32[16,64,128]{2,1,0:T(8,128)S(1)} custom-call(f32[16,64,128]{2,1,0:T(8,128)S(1)} %all_to_all.20.refs_0_, f32[16,64,128]{2,1,0:T(8,128)S(1)} %collective-permute-done.11.refs_1_, f32[64,64]{1,0:T(8,128)S(1)} %shard_map.48.refs_2_, f32[4,8,128]{2,1,0:T(8,128)S(1)} %get-tuple-element.54.refs_3_, bf16[512,128]{1,0:T(8,128)(2,1)S(1)} %copy-done, ...), custom_call_target="tpu_custom_call" | custom-call | bytes 3702784 | tf_op jit(solution)/shard_map/pallas_call | solution.py:283
  82.4 19.3 %all_to_all.21.refs_0_ = f32[16,64,128]{2,1,0:T(8,128)S(1)} all-to-all(f32[16,64,128]{2,1,0:T(8,128)S(1)} %shard_map.49), channel_id=1, replica_groups={{0,2,4,6,8,10,12,14,16,18,20,22,24,26,28,30},{1,3,5,7,9,11,13,15,17,19,..., dimensions={0} | all-to-all | bytes 1048576 | tf_op jit(solution)/shard_map/all_to_all | solution.py:311
  101.7 0.6 shard_map.50.refs_2_
  102.3 1.3 %collective-permute-done.12.refs_1_ = f32[16,64,128]{2,1,0:T(8,128)S(1)} collective-permute-done((f32[16,64,128]{2,1,0:T(8,128)S(1)}, f32[16,64,128]{2,1,0:T(8,128)S(1)}, u32[]{:S(2)}, u32[]{:S(2)}) %collective-permute-start.12) | collective-permute-done | bytes 524320 | tf_op jit(solution)/shard_map/ppermute | solution.py:312
  103.6 4.3 %shard_map.51 = (f32[64,128]{1,0:T(8,128)S(1)}, f32[16,24,128]{2,1,0:T(8,128)S(1)}) custom-call(f32[16,64,128]{2,1,0:T(8,128)S(1)} %all_to_all.21.refs_0_, f32[16,64,128]{2,1,0:T(8,128)S(1)} %collective-permute-done.12.refs_1_, f32[64,64]{1,0:T(8,128)S(1)} %shard_map.50.refs_2_, f32[4,8,128]{2,1,0:T(8,128)S(1)} %get-tuple-element.54.refs_3_, ...), custom_call_target="tpu_custom_call" | custom-call | bytes 3407872 | tf_op jit(solution)/shard_map/pallas_call | solution.py:283
  107.9 12.7 %all_to_all.22 = f32[16,24,128]{2,1,0:T(8,128)S(1)} all-to-all(f32[16,24,128]{2,1,0:T(8,128)S(1)} %get-tuple-element.55), channel_id=1, replica_groups={{0,2,4,6,8,10,12,14,16,18,20,22,24,26,28,30},{1,3,5,7,9,11,13,15,17,19,..., dimensions={0} | all-to-all | bytes 393216 | tf_op jit(solution)/shard_map/all_to_all | solution.py:395
  120.7 0.1 collective-permute-start.13
  120.7 1.2 collective-permute-done.13.refs_1_
  121.9 3.0 %shard_map.52 = f32[64,128]{1,0:T(8,128)} custom-call(f32[24,128]{1,0:T(8,128)S(1)} %reduce_sum.9.refs_0_, f32[24,128]{1,0:T(8,128)S(1)} %collective-permute-done.13.refs_1_, f32[64,128]{1,0:T(8,128)S(1)} %get-tuple-element.56.refs_2_), custom_call_target="tpu_custom_call" | custom-call | bytes 90112 | tf_op jit(solution)/shard_map/pallas_call | solution.py:283
  (30 shorter events, 0.1 us)
Async XLA Ops:
  3.3 5.2 %collective-permute-start = (f32[80,128]{1,0:T(8,128)}, f32[80,128]{1,0:T(8,128)S(1)}, u32[]{:S(2)}, u32[]{:S(2)}) collective-permute-start(f32[80,128]{1,0:T(8,128)} %get-tuple-element.31), channel_id=1, source_target_pairs={{0,4},{4,0},{8,12},{12,8},{16,20},{20,16},{24,28},{28,24},{1,5},{5... | collective-permute-start | bytes 122888 | tf_op jit(solution)/shard_map/ppermute | solution.py:295
  9.3 15.5 %collective-permute-start.1 = (f32[2,80,128]{2,1,0:T(8,128)S(1)}, f32[2,80,128]{2,1,0:T(8,128)S(1)}, u32[]{:S(2)}, u32[]{:S(2)}) collective-permute-start(f32[2,80,128]{2,1,0:T(8,128)S(1)} %pad_maximum_fusion.2), channel_id=1, source_target_pairs={{0,8},{4,12},{8,16},{12,20},{16,24},{20,28},{24,0},{28,4},{1,9},{5... | collective-permute-start | bytes 245768 | tf_op jit(solution)/shard_map/ppermute | solution.py:297
  11.4 6.8 %copy-start.7 = (bf16[512,128]{1,0:T(8,128)(2,1)S(1)}, bf16[512,128]{1,0:T(8,128)(2,1)}, u32[]{:S(2)}) copy-start(bf16[512,128]{1,0:T(8,128)(2,1)} %get-tuple-element.47) | copy-start | bytes 393220
  11.4 11.2 %copy-start.6 = (bf16[512,128]{1,0:T(8,128)(2,1)S(1)}, bf16[512,128]{1,0:T(8,128)(2,1)}, u32[]{:S(2)}) copy-start(bf16[512,128]{1,0:T(8,128)(2,1)} %get-tuple-element.48) | copy-start | bytes 393220
  11.4 39.9 %all-to-all-start = ((bf16[4,128,1024]{2,1,0:T(8,128)(2,1)}), bf16[4,128,1024]{2,1,0:T(8,128)(2,1)S(1)}, u32[]{:S(2)}, u32[]{:S(2)}) async-start(bf16[4,128,1024]{2,1,0:T(8,128)(2,1)} %get-tuple-element.52), calls=%async_computation | async-start | bytes 2097152 | tf_op jit(solution)/shard_map/all_to_all | solution.py:323
  15.0 19.6 %collective-permute-start.3 = (f32[2,80,128]{2,1,0:T(8,128)S(1)}, f32[2,80,128]{2,1,0:T(8,128)S(1)}, u32[]{:S(2)}, u32[]{:S(2)}) collective-permute-start(f32[2,80,128]{2,1,0:T(8,128)S(1)} %pad_maximum_fusion.2), channel_id=1, source_target_pairs={{0,24},{4,28},{8,0},{12,4},{16,8},{20,12},{24,16},{28,20},{1,25},{... | collective-permute-start | bytes 245768 | tf_op jit(solution)/shard_map/ppermute | solution.py:297
  17.1 20.8 %collective-permute-start.2 = (f32[2,80,128]{2,1,0:T(8,128)S(1)}, f32[2,80,128]{2,1,0:T(8,128)S(1)}, u32[]{:S(2)}, u32[]{:S(2)}) collective-permute-start(f32[2,80,128]{2,1,0:T(8,128)S(1)} %pad_maximum_fusion.2), channel_id=1, source_target_pairs={{0,16},{4,20},{8,24},{12,28},{16,0},{20,4},{24,8},{28,12},{1,17},{... | collective-permute-start | bytes 245768 | tf_op jit(solution)/shard_map/ppermute | solution.py:297
  18.1 22.4 %collective-permute-start.6 = (bf16[512,128]{1,0:T(8,128)(2,1)S(1)}, bf16[512,128]{1,0:T(8,128)(2,1)S(1)}, u32[]{:S(2)}, u32[]{:S(2)}) collective-permute-start(bf16[512,128]{1,0:T(8,128)(2,1)S(1)} %copy-done.7), channel_id=1, source_target_pairs={{0,12},{4,16},{8,20},{12,24},{16,28},{1,13},{5,17},{9,21},{13,25},... | collective-permute-start | bytes 393224 | tf_op jit(solution)/shard_map/ppermute | solution.py:316
  22.6 19.9 %collective-permute-start.7 = (bf16[512,128]{1,0:T(8,128)(2,1)S(1)}, bf16[512,128]{1,0:T(8,128)(2,1)S(1)}, u32[]{:S(2)}, u32[]{:S(2)}) collective-permute-start(bf16[512,128]{1,0:T(8,128)(2,1)S(1)} %copy-done.6), channel_id=1, source_target_pairs={{0,16},{4,20},{8,24},{12,28},{1,17},{5,21},{9,25},{13,29},{2,18},{... | collective-permute-start | bytes 393224 | tf_op jit(solution)/shard_map/ppermute | solution.py:316
  24.8 26.4 %collective-permute-start.8 = (bf16[512,128]{1,0:T(8,128)(2,1)}, bf16[512,128]{1,0:T(8,128)(2,1)S(1)}, u32[]{:S(2)}, u32[]{:S(2)}) collective-permute-start(bf16[512,128]{1,0:T(8,128)(2,1)} %get-tuple-element.49), channel_id=1, source_target_pairs={{0,20},{4,24},{8,28},{1,21},{5,25},{9,29},{2,22},{6,26},{10,30},{3... | collective-permute-start | bytes 393224 | tf_op jit(solution)/shard_map/ppermute | solution.py:316
  26.2 8.5 %copy-start.5 = (bf16[512,128]{1,0:T(8,128)(2,1)S(1)}, bf16[512,128]{1,0:T(8,128)(2,1)}, u32[]{:S(2)}) copy-start(bf16[512,128]{1,0:T(8,128)(2,1)} %get-tuple-element.50) | copy-start | bytes 393220
  26.2 11.8 %copy-start.4 = (bf16[512,128]{1,0:T(8,128)(2,1)S(1)}, bf16[512,128]{1,0:T(8,128)(2,1)}, u32[]{:S(2)}) copy-start(bf16[512,128]{1,0:T(8,128)(2,1)} %get-tuple-element.51) | copy-start | bytes 393220
  34.6 5.8 %copy-start.3 = (bf16[512,128]{1,0:T(8,128)(2,1)S(1)}, bf16[512,128]{1,0:T(8,128)(2,1)}, u32[]{:S(2)}) copy-start(bf16[512,128]{1,0:T(8,128)(2,1)} %get-tuple-element.45) | copy-start | bytes 393220
  34.6 7.8 %copy-start.2 = (bf16[512,128]{1,0:T(8,128)(2,1)S(1)}, bf16[512,128]{1,0:T(8,128)(2,1)}, u32[]{:S(2)}) copy-start(bf16[512,128]{1,0:T(8,128)(2,1)} %get-tuple-element.46) | copy-start | bytes 393220
  34.7 16.6 %collective-permute-start.9 = (bf16[512,128]{1,0:T(8,128)(2,1)S(1)}, bf16[512,128]{1,0:T(8,128)(2,1)S(1)}, u32[]{:S(2)}, u32[]{:S(2)}) collective-permute-start(bf16[512,128]{1,0:T(8,128)(2,1)S(1)} %copy-done.5), channel_id=1, source_target_pairs={{0,24},{4,28},{1,25},{5,29},{2,26},{6,30},{3,27},{7,31}} | collective-permute-start | bytes 393224 | tf_op jit(solution)/shard_map/ppermute | solution.py:316
  38.0 13.3 %collective-permute-start.10 = (bf16[512,128]{1,0:T(8,128)(2,1)S(1)}, bf16[512,128]{1,0:T(8,128)(2,1)S(1)}, u32[]{:S(2)}, u32[]{:S(2)}) collective-permute-start(bf16[512,128]{1,0:T(8,128)(2,1)S(1)} %copy-done.4), channel_id=1, source_target_pairs={{0,28},{1,29},{2,30},{3,31}} | collective-permute-start | bytes 393224 | tf_op jit(solution)/shard_map/ppermute | solution.py:316
  40.5 10.9 %copy-start = (bf16[512,128]{1,0:T(8,128)(2,1)S(1)}, bf16[512,128]{1,0:T(8,128)(2,1)}, u32[]{:S(2)}) copy-start(bf16[512,128]{1,0:T(8,128)(2,1)} %get-tuple-element.44.refs_3_.refs_4_) | copy-start | bytes 393220
  40.5 10.9 %copy-start.1 = (f32[64,128]{1,0:T(8,128)S(1)}, f32[64,128]{1,0:T(8,128)}, u32[]{:S(2)}) copy-start(f32[64,128]{1,0:T(8,128)} %get-tuple-element.43.refs_2_) | copy-start | bytes 98308
  40.5 10.8 %collective-permute-start.4 = (bf16[512,128]{1,0:T(8,128)(2,1)S(1)}, bf16[512,128]{1,0:T(8,128)(2,1)S(1)}, u32[]{:S(2)}, u32[]{:S(2)}) collective-permute-start(bf16[512,128]{1,0:T(8,128)(2,1)S(1)} %copy-done.3), channel_id=1, source_target_pairs={{0,4},{4,8},{8,12},{12,16},{16,20},{20,24},{24,28},{1,5},{5,9},{9,... | collective-permute-start | bytes 393224 | tf_op jit(solution)/shard_map/ppermute | solution.py:316
  42.5 8.8 %collective-permute-start.5 = (bf16[512,128]{1,0:T(8,128)(2,1)S(1)}, bf16[512,128]{1,0:T(8,128)(2,1)S(1)}, u32[]{:S(2)}, u32[]{:S(2)}) collective-permute-start(bf16[512,128]{1,0:T(8,128)(2,1)S(1)} %copy-done.2), channel_id=1, source_target_pairs={{0,8},{4,12},{8,16},{12,20},{16,24},{20,28},{1,9},{5,13},{9,17},{1... | collective-permute-start | bytes 393224 | tf_op jit(solution)/shard_map/ppermute | solution.py:316
  76.4 1.9 %collective-permute-start.11 = (f32[16,64,128]{2,1,0:T(8,128)S(1)}, f32[16,64,128]{2,1,0:T(8,128)S(1)}, u32[]{:S(2)}, u32[]{:S(2)}) collective-permute-start(f32[16,64,128]{2,1,0:T(8,128)S(1)} %all_to_all.20.refs_0_), channel_id=1, source_target_pairs={{0,1},{1,0},{2,3},{3,2},{4,5},{5,4},{6,7},{7,6},{8,9},{9,8},{10,11... | collective-permute-start | bytes 1572872 | tf_op jit(solution)/shard_map/ppermute | solution.py:312
  101.7 1.9 %collective-permute-start.12 = (f32[16,64,128]{2,1,0:T(8,128)S(1)}, f32[16,64,128]{2,1,0:T(8,128)S(1)}, u32[]{:S(2)}, u32[]{:S(2)}) collective-permute-start(f32[16,64,128]{2,1,0:T(8,128)S(1)} %all_to_all.21.refs_0_), channel_id=1, source_target_pairs={{0,1},{1,0},{2,3},{3,2},{4,5},{5,4},{6,7},{7,6},{8,9},{9,8},{10,11... | collective-permute-start | bytes 1572872 | tf_op jit(solution)/shard_map/ppermute | solution.py:312
  120.7 1.2 collective-permute-start.13

commit v7 on v6

--- a/solution.py
+++ b/solution.py
@@ -17,6 +17,25 @@
     return lax.dot_general(
         a, b, ((contract[0], contract[1]), ((), ())), precision=precision, preferred_element_type=F32
     )
+
+
+def split(value):
+    parts = []
+    for _ in range(3):
+        parts.append(value.astype(BF16))
+        value = value - parts[-1].astype(F32)
+    return parts
+
+
+def full_dot(a, b, contract):
+    left, right = split(a), split(b)
+    rows = a.shape[0]
+    terms = [[], [], []]
+    for n in range(3):
+        found = dot(jnp.concatenate(left[: 3 - n], axis=0), right[n], contract)
+        for m in range(3 - n):
+            terms[n + m].append(found[m * rows : (m + 1) * rows])
+    return (sum(terms[2]) + sum(terms[1])) + terms[0][0]
 
 
 def lanes(blocks):
@@ -184,7 +203,7 @@
 def panel_gram(panels):
     gram = None
     for panel in panels:
-        term = dot(panel, panel, ((1,), (1,)), HIGHEST)
+        term = full_dot(panel, panel, ((1,), (1,)))
         gram = term if gram is None else gram + term
     return gram
 
@@ -206,7 +225,7 @@
     factor = inverse_factor(panel_gram([panel_of(c) for c in range(cols)]))
     for c in range(cols):
         s = slot_of(c, cols)
-        panel = dot(factor, panel_of(c), ((1,), (0,)), HIGHEST)
+        panel = full_dot(factor, panel_of(c), ((1,), (0,)))
         for n, place in enumerate(slot_rows(rows)):
             root = roots_ref[s, pl.ds(place, 1)]
             vectors_ref[s, place] = (root * panel[:, n * width : (n + 1) * width]).astype(BF16)
@@ -232,7 +251,7 @@
     factor = inverse_factor(gram_ref[...] + panel_gram([panel_of(1, x) for x in range(half)]))
     for s in range(2):
         for x in range(half):
-            panel = dot(factor, panel_of(s, x), ((1,), (0,)), HIGHEST)
+            panel = full_dot(factor, panel_of(s, x), ((1,), (0,)))
             for i in range(rows):
                 root = roots_ref[s * half + x, i : i + 1]
                 scratch[s * half + x, i] = (root * panel[:, i * width : (i + 1) * width]).astype(BF16)

time: 125 us -> 125 us (level)
  no operation moved by 1% of the time
where the time goes in v7:
time: 125 us
  blocking collectives  66.9 us (54%)
  starting transfers between devices  28.9 us (23%)
  Pallas kernels  21.8 us (17%)
  waiting for transfers between devices  6.07 us (5%)
    all_to_all x2, blocking collectives, gather_images(): lax.all_to_all(copies, ('row', 'col'), 0, 0, tiled=True, axis_index_group...  38.4 us
    pallas_call x7, Pallas kernels, kernel_call(): pl.pallas_call(body, out_shape=outs[0] if single else tuple(outs), in_spe...  21.8 us
    ppermute x7, starting transfers between devices, move_up(): lax.ppermute(part, 'row', [(i, i + distance) for i in range(rows - distan...  17 us
    all_gather x2, blocking collectives, local(): lax.all_gather(jnp.concatenate(part), 'col', axis=0, tiled=False)  15.9 us
    all_to_all x1, blocking collectives, local(): lax.all_to_all(grams, ('row', 'col'), 0, 0, tiled=True, axis_index_groups...  12.7 us
    ppermute x3, starting transfers between devices, pass_start(): lax.ppermute(pieces, 'row', [(i, (i + distance) % rows) for i in range(ro...  5.17 us
    all_to_all x1, starting transfers between devices, exchange(): parts[rows] = lax.all_to_all(parts[rows], 'col', 0, 0, tiled=True)  3.65 us
    ppermute x1, starting transfers between devices, pass_start(): lax.ppermute(piece, 'row', [(i, i + 1 - 2 * (i % 2)) for i in range(rows)])  3.04 us
  transfers between devices with their start and end apart: 15, of which 4 were waited for; matrix products, arithmetic and copies ran while one was open for 0% of the time, Pallas kernels for 1%

profile of v7, /device:TPU:0, one launch (start us, length us, event | category | flops | bytes accessed | tf_op | source)
XLA Modules:
  0.0 124.9 jit_solution(11235382439417838857)
XLA Ops:
  0.0 3.3 %shard_map.46 = (bf16[512,128]{1,0:T(8,128)(2,1)}, bf16[512,128]{1,0:T(8,128)(2,1)}, bf16[512,128]{1,0:T(8,128)(2,1)}, bf16[512,128]{1,0:T(8,128)(2,1)}, bf16[51...) custom-call(s32[4,8]{1,0:T(4,128)} %bitcast.11, ...), custom_call_target="tpu_custom_call" | custom-call | bytes 3252864 | tf_op jit(solution)/shard_map/pallas_call | solution.py:302
  3.3 3.0 %collective-permute-start = (f32[80,128]{1,0:T(8,128)}, f32[80,128]{1,0:T(8,128)S(1)}, u32[]{:S(2)}, u32[]{:S(2)}) collective-permute-start(f32[80,128]{1,0:T(8,128)} %get-tuple-element.31), channel_id=1, source_target_pairs={{0,4},{4,0},{8,12},{12,8},{16,20},{20,16},{24,28},{28,24},{1,5},{5... | collective-permute-start | bytes 122888 | tf_op jit(solution)/shard_map/ppermute | solution.py:314
  6.3 2.2 %collective-permute-done = f32[80,128]{1,0:T(8,128)S(1)} collective-permute-done((f32[80,128]{1,0:T(8,128)}, f32[80,128]{1,0:T(8,128)S(1)}, u32[]{:S(2)}, u32[]{:S(2)}) %collective-permute-start) | collective-permute-done | bytes 40992 | tf_op jit(solution)/shard_map/ppermute | solution.py:314
  8.5 0.8 pad_maximum_fusion.2
  9.3 2.1 %collective-permute-start.1 = (f32[2,80,128]{2,1,0:T(8,128)S(1)}, f32[2,80,128]{2,1,0:T(8,128)S(1)}, u32[]{:S(2)}, u32[]{:S(2)}) collective-permute-start(f32[2,80,128]{2,1,0:T(8,128)S(1)} %pad_maximum_fusion.2), channel_id=1, source_target_pairs={{0,8},{4,12},{8,16},{12,20},{16,24},{20,28},{24,0},{28,4},{1,9},{5... | collective-permute-start | bytes 245768 | tf_op jit(solution)/shard_map/ppermute | solution.py:316
  11.4 3.6 %all-to-all-start = ((bf16[4,128,1024]{2,1,0:T(8,128)(2,1)}), bf16[4,128,1024]{2,1,0:T(8,128)(2,1)S(1)}, u32[]{:S(2)}, u32[]{:S(2)}) async-start(bf16[4,128,1024]{2,1,0:T(8,128)(2,1)} %get-tuple-element.52), calls=%async_computation | async-start | bytes 2097152 | tf_op jit(solution)/shard_map/all_to_all | solution.py:342
  15.0 2.1 %collective-permute-start.3 = (f32[2,80,128]{2,1,0:T(8,128)S(1)}, f32[2,80,128]{2,1,0:T(8,128)S(1)}, u32[]{:S(2)}, u32[]{:S(2)}) collective-permute-start(f32[2,80,128]{2,1,0:T(8,128)S(1)} %pad_maximum_fusion.2), channel_id=1, source_target_pairs={{0,24},{4,28},{8,0},{12,4},{16,8},{20,12},{24,16},{28,20},{1,25},{... | collective-permute-start | bytes 245768 | tf_op jit(solution)/shard_map/ppermute | solution.py:316
  17.1 1.0 collective-permute-start.2
  18.1 4.4 %collective-permute-start.6 = (bf16[512,128]{1,0:T(8,128)(2,1)S(1)}, bf16[512,128]{1,0:T(8,128)(2,1)S(1)}, u32[]{:S(2)}, u32[]{:S(2)}) collective-permute-start(bf16[512,128]{1,0:T(8,128)(2,1)S(1)} %copy-done.7), channel_id=1, source_target_pairs={{0,12},{4,16},{8,20},{12,24},{16,28},{1,13},{5,17},{9,21},{13,25},... | collective-permute-start | bytes 393224 | tf_op jit(solution)/shard_map/ppermute | solution.py:335
  22.6 2.3 %collective-permute-start.7 = (bf16[512,128]{1,0:T(8,128)(2,1)S(1)}, bf16[512,128]{1,0:T(8,128)(2,1)S(1)}, u32[]{:S(2)}, u32[]{:S(2)}) collective-permute-start(bf16[512,128]{1,0:T(8,128)(2,1)S(1)} %copy-done.6), channel_id=1, source_target_pairs={{0,16},{4,20},{8,24},{12,28},{1,17},{5,21},{9,25},{13,29},{2,18},{... | collective-permute-start | bytes 393224 | tf_op jit(solution)/shard_map/ppermute | solution.py:335
  24.8 1.3 %collective-permute-start.8 = (bf16[512,128]{1,0:T(8,128)(2,1)}, bf16[512,128]{1,0:T(8,128)(2,1)S(1)}, u32[]{:S(2)}, u32[]{:S(2)}) collective-permute-start(bf16[512,128]{1,0:T(8,128)(2,1)} %get-tuple-element.49), channel_id=1, source_target_pairs={{0,20},{4,24},{8,28},{1,21},{5,25},{9,29},{2,22},{6,26},{10,30},{3... | collective-permute-start | bytes 393224 | tf_op jit(solution)/shard_map/ppermute | solution.py:335
  26.2 8.5 %all-gather = f32[16,80,128]{2,1,0:T(8,128)S(1)} all-gather(f32[4,80,128]{2,1,0:T(8,128)S(1)} %pad_maximum_fusion), channel_id=2, replica_groups=mesh['row'=8,'col'=4] {'col'}, dimensions={0}, use_global_device_ids=true | all-gather | bytes 819200 | tf_op jit(solution)/shard_map/all_gather | solution.py:387
  34.7 3.3 %collective-permute-start.9 = (bf16[512,128]{1,0:T(8,128)(2,1)S(1)}, bf16[512,128]{1,0:T(8,128)(2,1)S(1)}, u32[]{:S(2)}, u32[]{:S(2)}) collective-permute-start(bf16[512,128]{1,0:T(8,128)(2,1)S(1)} %copy-done.5), channel_id=1, source_target_pairs={{0,24},{4,28},{1,25},{5,29},{2,26},{6,30},{3,27},{7,31}} | collective-permute-start | bytes 393224 | tf_op jit(solution)/shard_map/ppermute | solution.py:335
  38.0 2.4 %collective-permute-start.10 = (bf16[512,128]{1,0:T(8,128)(2,1)S(1)}, bf16[512,128]{1,0:T(8,128)(2,1)S(1)}, u32[]{:S(2)}, u32[]{:S(2)}) collective-permute-start(bf16[512,128]{1,0:T(8,128)(2,1)S(1)} %copy-done.4), channel_id=1, source_target_pairs={{0,28},{1,29},{2,30},{3,31}} | collective-permute-start | bytes 393224 | tf_op jit(solution)/shard_map/ppermute | solution.py:335
  40.5 0.0 copy-start.1
  40.5 2.0 %collective-permute-start.4 = (bf16[512,128]{1,0:T(8,128)(2,1)S(1)}, bf16[512,128]{1,0:T(8,128)(2,1)S(1)}, u32[]{:S(2)}, u32[]{:S(2)}) collective-permute-start(bf16[512,128]{1,0:T(8,128)(2,1)S(1)} %copy-done.3), channel_id=1, source_target_pairs={{0,4},{4,8},{8,12},{12,16},{16,20},{20,24},{24,28},{1,5},{5,9},{9,... | collective-permute-start | bytes 393224 | tf_op jit(solution)/shard_map/ppermute | solution.py:335
  42.5 0.0 collective-permute-done.7.refs_7_.refs_8_
  42.5 1.3 %collective-permute-start.5 = (bf16[512,128]{1,0:T(8,128)(2,1)S(1)}, bf16[512,128]{1,0:T(8,128)(2,1)S(1)}, u32[]{:S(2)}, u32[]{:S(2)}) collective-permute-start(bf16[512,128]{1,0:T(8,128)(2,1)S(1)} %copy-done.2), channel_id=1, source_target_pairs={{0,8},{4,12},{8,16},{12,20},{16,24},{20,28},{1,9},{5,13},{9,17},{1... | collective-permute-start | bytes 393224 | tf_op jit(solution)/shard_map/ppermute | solution.py:335
  43.8 7.4 %all-gather.1 = f32[16,80,128]{2,1,0:T(8,128)S(1)} all-gather(f32[4,80,128]{2,1,0:T(8,128)S(1)} %pad_maximum_fusion.1), channel_id=3, replica_groups=mesh['row'=8,'col'=4] {'col'}, dimensions={0}, use_global_device_ids=true | all-gather | bytes 819200 | tf_op jit(solution)/shard_map/all_gather | solution.py:387
  51.3 6.0 %shard_map.47 = (f32[16,64,128]{2,1,0:T(8,128)S(1)}, f32[4,8,128]{2,1,0:T(8,128)S(1)}) custom-call(f32[4,4,80,128]{3,2,1,0:T(8,128)S(1)} %bitcast.6, f32[4,4,80,128]{3,2,1,0:T(8,128)S(1)} %bitcast.7, f32[64,128]{1,0:T(8,128)S(1)} %copy-done.1, bf16[512,128]{1,0:T(8,128)(2,1)S(1)} %copy-done, bf16[512,128]{1,0:T(8,128)(2,1)S(1)} %collective-permute-done.4.refs_4_.refs_5_, ...), custom_call_target="tpu_custom_call" | custom-call | bytes 3981312 | tf_op jit(solution)/shard_map/pallas_call | solution.py:302
  57.3 19.1 %all_to_all.20.refs_0_ = f32[16,64,128]{2,1,0:T(8,128)S(1)} all-to-all(f32[16,64,128]{2,1,0:T(8,128)S(1)} %get-tuple-element.53), channel_id=1, replica_groups={{0,2,4,6,8,10,12,14,16,18,20,22,24,26,28,30},{1,3,5,7,9,11,13,15,17,19,..., dimensions={0} | all-to-all | bytes 1048576 | tf_op jit(solution)/shard_map/all_to_all | solution.py:330
  76.4 0.6 shard_map.48.refs_2_
  77.0 1.3 %collective-permute-done.11.refs_1_ = f32[16,64,128]{2,1,0:T(8,128)S(1)} collective-permute-done((f32[16,64,128]{2,1,0:T(8,128)S(1)}, f32[16,64,128]{2,1,0:T(8,128)S(1)}, u32[]{:S(2)}, u32[]{:S(2)}) %collective-permute-start.11) | collective-permute-done | bytes 524320 | tf_op jit(solution)/shard_map/ppermute | solution.py:331
  78.3 4.1 %shard_map.49 = f32[16,64,128]{2,1,0:T(8,128)S(1)} custom-call(f32[16,64,128]{2,1,0:T(8,128)S(1)} %all_to_all.20.refs_0_, f32[16,64,128]{2,1,0:T(8,128)S(1)} %collective-permute-done.11.refs_1_, f32[64,64]{1,0:T(8,128)S(1)} %shard_map.48.refs_2_, f32[4,8,128]{2,1,0:T(8,128)S(1)} %get-tuple-element.54.refs_3_, bf16[512,128]{1,0:T(8,128)(2,1)S(1)} %copy-done, ...), custom_call_target="tpu_custom_call" | custom-call | bytes 3702784 | tf_op jit(solution)/shard_map/pallas_call | solution.py:302
  82.4 19.3 %all_to_all.21.refs_0_ = f32[16,64,128]{2,1,0:T(8,128)S(1)} all-to-all(f32[16,64,128]{2,1,0:T(8,128)S(1)} %shard_map.49), channel_id=1, replica_groups={{0,2,4,6,8,10,12,14,16,18,20,22,24,26,28,30},{1,3,5,7,9,11,13,15,17,19,..., dimensions={0} | all-to-all | bytes 1048576 | tf_op jit(solution)/shard_map/all_to_all | solution.py:330
  101.7 0.6 shard_map.50.refs_2_
  102.3 1.3 %collective-permute-done.12.refs_1_ = f32[16,64,128]{2,1,0:T(8,128)S(1)} collective-permute-done((f32[16,64,128]{2,1,0:T(8,128)S(1)}, f32[16,64,128]{2,1,0:T(8,128)S(1)}, u32[]{:S(2)}, u32[]{:S(2)}) %collective-permute-start.12) | collective-permute-done | bytes 524320 | tf_op jit(solution)/shard_map/ppermute | solution.py:331
  103.6 4.3 %shard_map.51 = (f32[64,128]{1,0:T(8,128)S(1)}, f32[16,24,128]{2,1,0:T(8,128)S(1)}) custom-call(f32[16,64,128]{2,1,0:T(8,128)S(1)} %all_to_all.21.refs_0_, f32[16,64,128]{2,1,0:T(8,128)S(1)} %collective-permute-done.12.refs_1_, f32[64,64]{1,0:T(8,128)S(1)} %shard_map.50.refs_2_, f32[4,8,128]{2,1,0:T(8,128)S(1)} %get-tuple-element.54.refs_3_, ...), custom_call_target="tpu_custom_call" | custom-call | bytes 3407872 | tf_op jit(solution)/shard_map/pallas_call | solution.py:302
  108.0 12.7 %all_to_all.22 = f32[16,24,128]{2,1,0:T(8,128)S(1)} all-to-all(f32[16,24,128]{2,1,0:T(8,128)S(1)} %get-tuple-element.55), channel_id=1, replica_groups={{0,2,4,6,8,10,12,14,16,18,20,22,24,26,28,30},{1,3,5,7,9,11,13,15,17,19,..., dimensions={0} | all-to-all | bytes 393216 | tf_op jit(solution)/shard_map/all_to_all | solution.py:414
  120.7 0.1 collective-permute-start.13
  120.7 1.2 collective-permute-done.13.refs_1_
  121.9 3.0 %shard_map.52 = f32[64,128]{1,0:T(8,128)} custom-call(f32[24,128]{1,0:T(8,128)S(1)} %reduce_sum.9.refs_0_, f32[24,128]{1,0:T(8,128)S(1)} %collective-permute-done.13.refs_1_, f32[64,128]{1,0:T(8,128)S(1)} %get-tuple-element.56.refs_2_), custom_call_target="tpu_custom_call" | custom-call | bytes 90112 | tf_op jit(solution)/shard_map/pallas_call | solution.py:302
  (30 shorter events, 0.1 us)
Async XLA Ops:
  3.3 5.2 %collective-permute-start = (f32[80,128]{1,0:T(8,128)}, f32[80,128]{1,0:T(8,128)S(1)}, u32[]{:S(2)}, u32[]{:S(2)}) collective-permute-start(f32[80,128]{1,0:T(8,128)} %get-tuple-element.31), channel_id=1, source_target_pairs={{0,4},{4,0},{8,12},{12,8},{16,20},{20,16},{24,28},{28,24},{1,5},{5... | collective-permute-start | bytes 122888 | tf_op jit(solution)/shard_map/ppermute | solution.py:314
  9.3 15.5 %collective-permute-start.1 = (f32[2,80,128]{2,1,0:T(8,128)S(1)}, f32[2,80,128]{2,1,0:T(8,128)S(1)}, u32[]{:S(2)}, u32[]{:S(2)}) collective-permute-start(f32[2,80,128]{2,1,0:T(8,128)S(1)} %pad_maximum_fusion.2), channel_id=1, source_target_pairs={{0,8},{4,12},{8,16},{12,20},{16,24},{20,28},{24,0},{28,4},{1,9},{5... | collective-permute-start | bytes 245768 | tf_op jit(solution)/shard_map/ppermute | solution.py:316
  11.4 6.8 %copy-start.7 = (bf16[512,128]{1,0:T(8,128)(2,1)S(1)}, bf16[512,128]{1,0:T(8,128)(2,1)}, u32[]{:S(2)}) copy-start(bf16[512,128]{1,0:T(8,128)(2,1)} %get-tuple-element.47) | copy-start | bytes 393220
  11.4 11.2 %copy-start.6 = (bf16[512,128]{1,0:T(8,128)(2,1)S(1)}, bf16[512,128]{1,0:T(8,128)(2,1)}, u32[]{:S(2)}) copy-start(bf16[512,128]{1,0:T(8,128)(2,1)} %get-tuple-element.48) | copy-start | bytes 393220
  11.4 39.9 %all-to-all-start = ((bf16[4,128,1024]{2,1,0:T(8,128)(2,1)}), bf16[4,128,1024]{2,1,0:T(8,128)(2,1)S(1)}, u32[]{:S(2)}, u32[]{:S(2)}) async-start(bf16[4,128,1024]{2,1,0:T(8,128)(2,1)} %get-tuple-element.52), calls=%async_computation | async-start | bytes 2097152 | tf_op jit(solution)/shard_map/all_to_all | solution.py:342
  15.0 19.6 %collective-permute-start.3 = (f32[2,80,128]{2,1,0:T(8,128)S(1)}, f32[2,80,128]{2,1,0:T(8,128)S(1)}, u32[]{:S(2)}, u32[]{:S(2)}) collective-permute-start(f32[2,80,128]{2,1,0:T(8,128)S(1)} %pad_maximum_fusion.2), channel_id=1, source_target_pairs={{0,24},{4,28},{8,0},{12,4},{16,8},{20,12},{24,16},{28,20},{1,25},{... | collective-permute-start | bytes 245768 | tf_op jit(solution)/shard_map/ppermute | solution.py:316
  17.1 20.8 %collective-permute-start.2 = (f32[2,80,128]{2,1,0:T(8,128)S(1)}, f32[2,80,128]{2,1,0:T(8,128)S(1)}, u32[]{:S(2)}, u32[]{:S(2)}) collective-permute-start(f32[2,80,128]{2,1,0:T(8,128)S(1)} %pad_maximum_fusion.2), channel_id=1, source_target_pairs={{0,16},{4,20},{8,24},{12,28},{16,0},{20,4},{24,8},{28,12},{1,17},{... | collective-permute-start | bytes 245768 | tf_op jit(solution)/shard_map/ppermute | solution.py:316
  18.1 22.4 %collective-permute-start.6 = (bf16[512,128]{1,0:T(8,128)(2,1)S(1)}, bf16[512,128]{1,0:T(8,128)(2,1)S(1)}, u32[]{:S(2)}, u32[]{:S(2)}) collective-permute-start(bf16[512,128]{1,0:T(8,128)(2,1)S(1)} %copy-done.7), channel_id=1, source_target_pairs={{0,12},{4,16},{8,20},{12,24},{16,28},{1,13},{5,17},{9,21},{13,25},... | collective-permute-start | bytes 393224 | tf_op jit(solution)/shard_map/ppermute | solution.py:335
  22.6 19.9 %collective-permute-start.7 = (bf16[512,128]{1,0:T(8,128)(2,1)S(1)}, bf16[512,128]{1,0:T(8,128)(2,1)S(1)}, u32[]{:S(2)}, u32[]{:S(2)}) collective-permute-start(bf16[512,128]{1,0:T(8,128)(2,1)S(1)} %copy-done.6), channel_id=1, source_target_pairs={{0,16},{4,20},{8,24},{12,28},{1,17},{5,21},{9,25},{13,29},{2,18},{... | collective-permute-start | bytes 393224 | tf_op jit(solution)/shard_map/ppermute | solution.py:335
  24.8 26.4 %collective-permute-start.8 = (bf16[512,128]{1,0:T(8,128)(2,1)}, bf16[512,128]{1,0:T(8,128)(2,1)S(1)}, u32[]{:S(2)}, u32[]{:S(2)}) collective-permute-start(bf16[512,128]{1,0:T(8,128)(2,1)} %get-tuple-element.49), channel_id=1, source_target_pairs={{0,20},{4,24},{8,28},{1,21},{5,25},{9,29},{2,22},{6,26},{10,30},{3... | collective-permute-start | bytes 393224 | tf_op jit(solution)/shard_map/ppermute | solution.py:335
  26.2 8.5 %copy-start.5 = (bf16[512,128]{1,0:T(8,128)(2,1)S(1)}, bf16[512,128]{1,0:T(8,128)(2,1)}, u32[]{:S(2)}) copy-start(bf16[512,128]{1,0:T(8,128)(2,1)} %get-tuple-element.50) | copy-start | bytes 393220
  26.2 11.8 %copy-start.4 = (bf16[512,128]{1,0:T(8,128)(2,1)S(1)}, bf16[512,128]{1,0:T(8,128)(2,1)}, u32[]{:S(2)}) copy-start(bf16[512,128]{1,0:T(8,128)(2,1)} %get-tuple-element.51) | copy-start | bytes 393220
  34.6 5.8 %copy-start.3 = (bf16[512,128]{1,0:T(8,128)(2,1)S(1)}, bf16[512,128]{1,0:T(8,128)(2,1)}, u32[]{:S(2)}) copy-start(bf16[512,128]{1,0:T(8,128)(2,1)} %get-tuple-element.45) | copy-start | bytes 393220
  34.6 7.8 %copy-start.2 = (bf16[512,128]{1,0:T(8,128)(2,1)S(1)}, bf16[512,128]{1,0:T(8,128)(2,1)}, u32[]{:S(2)}) copy-start(bf16[512,128]{1,0:T(8,128)(2,1)} %get-tuple-element.46) | copy-start | bytes 393220
  34.7 16.6 %collective-permute-start.9 = (bf16[512,128]{1,0:T(8,128)(2,1)S(1)}, bf16[512,128]{1,0:T(8,128)(2,1)S(1)}, u32[]{:S(2)}, u32[]{:S(2)}) collective-permute-start(bf16[512,128]{1,0:T(8,128)(2,1)S(1)} %copy-done.5), channel_id=1, source_target_pairs={{0,24},{4,28},{1,25},{5,29},{2,26},{6,30},{3,27},{7,31}} | collective-permute-start | bytes 393224 | tf_op jit(solution)/shard_map/ppermute | solution.py:335
  38.0 13.3 %collective-permute-start.10 = (bf16[512,128]{1,0:T(8,128)(2,1)S(1)}, bf16[512,128]{1,0:T(8,128)(2,1)S(1)}, u32[]{:S(2)}, u32[]{:S(2)}) collective-permute-start(bf16[512,128]{1,0:T(8,128)(2,1)S(1)} %copy-done.4), channel_id=1, source_target_pairs={{0,28},{1,29},{2,30},{3,31}} | collective-permute-start | bytes 393224 | tf_op jit(solution)/shard_map/ppermute | solution.py:335
  40.5 10.9 %copy-start = (bf16[512,128]{1,0:T(8,128)(2,1)S(1)}, bf16[512,128]{1,0:T(8,128)(2,1)}, u32[]{:S(2)}) copy-start(bf16[512,128]{1,0:T(8,128)(2,1)} %get-tuple-element.44.refs_3_.refs_4_) | copy-start | bytes 393220
  40.5 10.9 %copy-start.1 = (f32[64,128]{1,0:T(8,128)S(1)}, f32[64,128]{1,0:T(8,128)}, u32[]{:S(2)}) copy-start(f32[64,128]{1,0:T(8,128)} %get-tuple-element.43.refs_2_) | copy-start | bytes 98308
  40.5 10.8 %collective-permute-start.4 = (bf16[512,128]{1,0:T(8,128)(2,1)S(1)}, bf16[512,128]{1,0:T(8,128)(2,1)S(1)}, u32[]{:S(2)}, u32[]{:S(2)}) collective-permute-start(bf16[512,128]{1,0:T(8,128)(2,1)S(1)} %copy-done.3), channel_id=1, source_target_pairs={{0,4},{4,8},{8,12},{12,16},{16,20},{20,24},{24,28},{1,5},{5,9},{9,... | collective-permute-start | bytes 393224 | tf_op jit(solution)/shard_map/ppermute | solution.py:335
  42.5 8.8 %collective-permute-start.5 = (bf16[512,128]{1,0:T(8,128)(2,1)S(1)}, bf16[512,128]{1,0:T(8,128)(2,1)S(1)}, u32[]{:S(2)}, u32[]{:S(2)}) collective-permute-start(bf16[512,128]{1,0:T(8,128)(2,1)S(1)} %copy-done.2), channel_id=1, source_target_pairs={{0,8},{4,12},{8,16},{12,20},{16,24},{20,28},{1,9},{5,13},{9,17},{1... | collective-permute-start | bytes 393224 | tf_op jit(solution)/shard_map/ppermute | solution.py:335
  76.4 1.9 %collective-permute-start.11 = (f32[16,64,128]{2,1,0:T(8,128)S(1)}, f32[16,64,128]{2,1,0:T(8,128)S(1)}, u32[]{:S(2)}, u32[]{:S(2)}) collective-permute-start(f32[16,64,128]{2,1,0:T(8,128)S(1)} %all_to_all.20.refs_0_), channel_id=1, source_target_pairs={{0,1},{1,0},{2,3},{3,2},{4,5},{5,4},{6,7},{7,6},{8,9},{9,8},{10,11... | collective-permute-start | bytes 1572872 | tf_op jit(solution)/shard_map/ppermute | solution.py:331
  101.7 1.9 %collective-permute-start.12 = (f32[16,64,128]{2,1,0:T(8,128)S(1)}, f32[16,64,128]{2,1,0:T(8,128)S(1)}, u32[]{:S(2)}, u32[]{:S(2)}) collective-permute-start(f32[16,64,128]{2,1,0:T(8,128)S(1)} %all_to_all.21.refs_0_), channel_id=1, source_target_pairs={{0,1},{1,0},{2,3},{3,2},{4,5},{5,4},{6,7},{7,6},{8,9},{9,8},{10,11... | collective-permute-start | bytes 1572872 | tf_op jit(solution)/shard_map/ppermute | solution.py:331
  120.7 1.2 collective-permute-start.13
